TPU v7x, 128 devices: a whole 4x4x4 slice. The times are simulated.
128 devices in a mesh: grp: 4 (over y), page: 32 (over x, z, core).
Axes of the slice: x: 4, y: 4, z: 4, core: 2. Of those that a mesh axis runs over, the one named last changes fastest.
Arguments:
- tokens: bfloat16 [32768, 3584], P(('grp', 'page')), may hold values from -40 to 40
- page_lengths: int32 [128, 8], P(('grp', 'page')), may hold values from 1 to 128, 256 in all within a row
- page_group: int32 [1024, 1], P(('grp', 'page')), may hold values from 0 to 3; in each aligned block of 8 rows (0 to 7, 8 to 15, ...) at most 4 rows name the same one
- page_report: int32 [1024], P(('grp', 'page')), may hold values from 0 to 15
- attn_gain: float32 [3584], replicated, may hold values from 0.1 to 1.9
- w_query: bfloat16 [3584, 1792], P('page'), may hold values from -1 to 1
- w_keyval: bfloat16 [3584, 512], P('page'), may hold values from -1 to 1
- w_out: bfloat16 [1792, 3584], P('page'), may hold values from -0.125 to 0.125
- doc_gain: float32 [3584], replicated, may hold values from 0.4 to 3.5
- ffn_gain: float32 [3584], replicated, may hold values from 0.1 to 1.9
- gate_up_weight: bfloat16 [2, 3584, 16384], P(None, None, 'page'), may hold values from -0.09375 to 0.09375
- w_down: bfloat16 [16384, 3584], P('page'), may hold values from -0.046875 to 0.046875
Outputs:
- token_states: bfloat16 [32768, 3584], P(('grp', 'page'))
- page_embeddings: bfloat16 [1024, 3584], P(('grp', 'page'))
Inputs may be any that keep to these rules, and one draw needn't show every extreme that they name: `page_lengths`: the 8 lengths of one row sum to 256; some length is exactly 128. `page_group`: of the 8 pages of one device at most 4 name the same group, a bound that some block reaches.
All inputs are finite; a program needn't handle non-finite values.
Results may differ from a plain program's by a relative error of at most 0.018.
Values may be sent and summed in bfloat16 or wider, within the bound.
No kernel may reach another device: no remote copies, remote signals or barrier semaphores. Data moves between devices by JAX's collectives and lax.ppermute only.
A program may use at most 128 MiB of HBM per device.

v0:
```python
import math

import jax
import jax.numpy as jnp
from jax import lax
from jax.sharding import PartitionSpec as P

HD = 128
CAP = 4


def rms_scale(values, gain):
    wide = values.astype(jnp.float32)
    return wide * lax.rsqrt(jnp.mean(wide * wide, axis=-1, keepdims=True) + 1e-06) * gain


def page_index(lengths, count):
    ends = jnp.cumsum(lengths, dtype=jnp.int32)
    position = jnp.arange(count, dtype=jnp.int32)
    return jnp.sum((position[:, None] >= ends[None, :]).astype(jnp.int32), axis=1)


def page_attention(query, keyval, segment, kv_heads):
    count = query.shape[0]
    heads = query.shape[1] // HD
    grouped = query.reshape(count, kv_heads, heads // kv_heads, HD)
    keys = keyval[:, : kv_heads * HD].reshape(count, kv_heads, HD)
    values = keyval[:, kv_heads * HD :].reshape(count, kv_heads, HD)
    scores = jnp.einsum(
        "tgjd,sgd->gjts", grouped, keys, preferred_element_type=jnp.float32
    ) / math.sqrt(HD)
    scores = jnp.where(segment[:, None] == segment[None, :], scores, -1e30)
    weights = jax.nn.softmax(scores, axis=-1).astype(jnp.bfloat16)
    mixed = jnp.einsum("gjts,sgd->tgjd", weights, values, preferred_element_type=jnp.float32)
    return mixed.reshape(count, heads * HD).astype(jnp.bfloat16)


def report_mix(query_rows, query_keys, query_labels, key_rows, key_labels):
    count = query_keys.shape[0]
    heads = query_keys.shape[1] // HD
    split_query = query_keys.reshape(count, heads, HD)
    split_keys = key_rows.reshape(key_rows.shape[0], heads, HD)
    scores = (
        jnp.einsum("qhd,khd->hqk", split_query, split_keys, preferred_element_type=jnp.float32) / HD
    )
    scores = jnp.where(query_labels[:, None] == key_labels[None, :], scores, -1e30)
    weights = jax.nn.softmax(scores, axis=-1).astype(jnp.bfloat16)
    context = jnp.einsum(
        "hqk,khd->qhd", weights, split_keys, preferred_element_type=jnp.float32
    ).reshape(count, heads * HD)
    return (query_rows.astype(jnp.float32) + context).astype(jnp.bfloat16)


def feed_hidden(states, gain, gate_up_weight):
    mixed_in = rms_scale(states, gain).astype(jnp.bfloat16)
    gate = jnp.dot(mixed_in, gate_up_weight[0], preferred_element_type=jnp.float32)
    up = jnp.dot(mixed_in, gate_up_weight[1], preferred_element_type=jnp.float32)
    return (jax.nn.silu(gate) * up).astype(jnp.bfloat16)


def on_device(
    tokens,
    page_lengths,
    page_group,
    page_report,
    attn_gain,
    w_query,
    w_keyval,
    w_out,
    doc_gain,
    ffn_gain,
    gate_up_weight,
    w_down,
):
    count = tokens.shape[0]
    kv_heads = w_keyval.shape[1] // (2 * HD)
    normed = rms_scale(tokens, attn_gain).astype(jnp.bfloat16)
    segment = page_index(page_lengths[0], count)

    def fold_normed(piece):
        return jnp.dot(normed, piece, preferred_element_type=jnp.float32)

    query = fold_normed(lax.all_gather(w_query, "page", axis=0, tiled=True)).astype(jnp.bfloat16)
    keyval = fold_normed(lax.all_gather(w_keyval, "page", axis=0, tiled=True)).astype(jnp.bfloat16)
    attended = page_attention(query, keyval, segment, kv_heads)
    projected = jnp.dot(
        attended,
        lax.all_gather(w_out, "page", axis=0, tiled=True),
        preferred_element_type=jnp.float32,
    )
    token_states = (tokens.astype(jnp.float32) + projected).astype(jnp.bfloat16)
    lengths = page_lengths[0]
    pages = lengths.shape[0]
    member = (segment[None, :] == jnp.arange(pages, dtype=jnp.int32)[:, None]).astype(jnp.bfloat16)
    pooled_vectors = (
        jnp.dot(member, token_states, preferred_element_type=jnp.float32)
        / lengths[:, None].astype(jnp.float32)
    ).astype(jnp.bfloat16)
    groups = lax.axis_size("grp")
    target = page_group[:, 0]
    order = jnp.arange(pages, dtype=jnp.int32)
    earlier = (order[None, :] < order[:, None]) & (target[None, :] == target[:, None])
    rank = jnp.sum(earlier.astype(jnp.int32), axis=1)
    chosen = (target[None, None, :] == jnp.arange(groups, dtype=jnp.int32)[:, None, None]) & (
        rank[None, None, :] == jnp.arange(CAP, dtype=jnp.int32)[None, :, None]
    )
    chosen_int = chosen.astype(jnp.int32)
    selected_flattened = chosen.astype(jnp.bfloat16)
    outgoing = jnp.einsum(
        "vnt,tz->vnz", selected_flattened, pooled_vectors, preferred_element_type=jnp.float32
    ).astype(jnp.bfloat16)
    labels_out = jnp.sum(chosen_int * (page_report[None, None, :] + 1), axis=2) - 1
    incoming, labels_in = (
        lax.all_to_all(outgoing, "grp", split_axis=0, concat_axis=0, tiled=True),
        lax.all_to_all(labels_out, "grp", split_axis=0, concat_axis=0, tiled=True),
    )
    width = incoming.shape[2]
    slots = groups * CAP
    rows = incoming.reshape(slots, width)
    labels = labels_in.reshape(slots)
    group_vectors, group_labels = (
        lax.all_gather(rows, "page", axis=0, tiled=True),
        lax.all_gather(labels, "page", axis=0, tiled=True),
    )
    group_keys = rms_scale(group_vectors, doc_gain).astype(jnp.bfloat16)
    own_keys = rms_scale(rows, doc_gain).astype(jnp.bfloat16)
    own_states = report_mix(rows, own_keys, labels, group_keys, group_labels)
    group_states = lax.all_gather(own_states, "page", axis=0, tiled=True)
    hidden = feed_hidden(group_states, ffn_gain, gate_up_weight)
    summed = lax.psum_scatter(
        jnp.dot(hidden, w_down, preferred_element_type=jnp.float32).astype(jnp.bfloat16),
        "page",
        scatter_dimension=0,
        tiled=True,
    ).astype(jnp.float32)
    finished = (
        (own_states.astype(jnp.float32) + summed).astype(jnp.bfloat16).reshape(groups, CAP, width)
    )
    returned_values = lax.all_to_all(finished, "grp", split_axis=0, concat_axis=0, tiled=True)
    page_embeddings = jnp.einsum(
        "anv,anf->vf", selected_flattened, returned_values, preferred_element_type=jnp.float32
    ).astype(jnp.bfloat16)
    return (token_states, page_embeddings)


def solution(mesh):
    in_specs = (
        P(("grp", "page"), None),
        P(("grp", "page"), None),
        P(("grp", "page"), None),
        P(("grp", "page")),
        P(),
        P("page", None),
        P("page", None),
        P("page", None),
        P(),
        P(),
        P(None, None, "page"),
        P("page", None),
    )
    out_specs = (P(("grp", "page"), None), P(("grp", "page"), None))
    return jax.shard_map(
        on_device, mesh=mesh, in_specs=in_specs, out_specs=out_specs, check_vma=False
    )
```

profile of v0, /device:TPU:0, one launch (start us, length us, event | category | flops | bytes accessed | tf_op | source)
XLA Modules:
  0.0 433.7 jit_solution(6673224623142714692)
XLA Ops:
  7.2 0.7 all-gather.6.cloned.1.call-update
  7.9 0.7 all-gather.8.cloned.1.call-update
  9.4 0.8 reduce-window.8
  10.3 0.9 convert_reduce_fusion.1
  11.9 1.9 fusion.12
  14.7 44.0 %all-gather.6.cloned.1.call-done = bf16[3584,512]{1,0:T(8,128)(2,1)} async-done(((bf16[112,512]{1,0:T(8,128)(2,1)}), bf16[3584,512]{1,0:T(8,128)(2,1)}) %all-gather.6.cloned.1.call-update) | async-done | bytes 3670032 | tf_op jit(solution)/shard_map/all_gather | solution.py:84
  58.6 3.8 convolution_convert_fusion.3
  62.6 61.2 %all-gather.8.cloned.1.call-done = bf16[3584,1792]{1,0:T(8,128)(2,1)} async-done(((bf16[112,1792]{1,0:T(8,128)(2,1)}), bf16[3584,1792]{1,0:T(8,128)(2,1)}) %all-gather.8.cloned.1.call-update) | async-done | bytes 12845072 | tf_op jit(solution)/shard_map/all_gather | solution.py:83
  123.8 6.7 %convolution_convert_fusion.2 = bf16[256,1792]{1,0:T(8,128)(2,1)S(1)} fusion(bf16[3584,1792]{1,0:T(8,128)(2,1)} %all-gather.8.cloned.1.call-done, bf16[256,3584]{1,0:T(8,128)(2,1)S(1)} %copy-done.2, f32[3584]{0:T(1024)S(1)} %copy-done.7, f32[256]{0:T(256)S(1)} %add_rsqrt_fusion.3), kind=kOutput, calls=%fused_computation.36 | convolution fusion | flops 3292463104 | bytes 15612928 | tf_op jit(solution)/shard_map/dot_general | solution.py:81
  131.1 3.0 fusion.76
  134.1 2.7 fusion.26
  136.8 52.3 %all-gather.10.cloned.1.call-done = bf16[1792,3584]{1,0:T(8,128)(2,1)} async-done(((bf16[56,3584]{1,0:T(8,128)(2,1)}), bf16[1792,3584]{1,0:T(8,128)(2,1)}) %all-gather.10.cloned.1.call-update) | async-done | bytes 12845072 | tf_op jit(solution)/shard_map/all_gather | solution.py:88
  189.2 8.7 %fusion.8 = bf16[256,3584]{1,0:T(8,128)(2,1)S(1)} fusion(bf16[256,1792]{0,1:T(8,128)(2,1)S(1)} %bitcast.73, bf16[1792,3584]{1,0:T(8,128)(2,1)} %all-gather.10.cloned.1.call-done, bf16[256,3584]{1,0:T(8,128)(2,1)} %param.12), kind=kOutput, calls=%fused_computation.16 | convolution fusion | flops 3291086848 | bytes 17432576 | tf_op jit(solution)/shard_map/dot_general | solution.py:86
  198.4 10.0 %all_to_all.16 = bf16[4,4,3584]{2,1,0:T(4,128)(2,1)S(1)} all-to-all(bf16[4,4,3584]{2,1,0:T(4,128)(2,1)S(1)} %convolution_convert_fusion.1), channel_id=1, replica_groups=mesh['grp'=4,'page'=32] {'grp'}, dimensions={0} | all-to-all | bytes 229376 | tf_op jit(solution)/shard_map/all_to_all | solution.py:114
  209.8 3.2 all-to-all-start.1
  214.2 3.9 all-to-all-done.1
  219.6 14.6 %all-reduce = s32[512]{0:T(512)S(1)} all-reduce(s32[512]{0:T(512)S(1)} %dynamic-update-slice), channel_id=1, replica_groups=mesh['grp'=4,'page'=32] {'page'}, use_global_device_ids=true, to_apply=%add | all-reduce | flops 512 | bytes 4096
  234.8 17.9 %all-gather.12.cloned.1.call-done = bf16[512,3584]{1,0:T(8,128)(2,1)} async-done(((bf16[16,3584]{1,0:T(8,128)(2,1)}), bf16[512,3584]{1,0:T(8,128)(2,1)}) %all-gather.12.cloned.1.call-update) | async-done | bytes 3670032 | tf_op jit(solution)/shard_map/all_gather | solution.py:122
  252.7 3.0 fusion.2
  255.9 3.0 fusion.4
  258.9 6.0 %copy.47 = bf16[512,3584]{0,1:T(8,128)(2,1)} copy(bf16[512,3584]{1,0:T(8,128)(2,1)} %fusion.4) | data formatting | bytes 7340032 | tf_op jit(solution)/shard_map/convert_element_type | solution.py:125
  264.8 2.8 fusion.81
  267.7 3.2 convolution_bitcast_fusion.1
  270.9 0.7 fusion.52
  271.6 45.3 %all-gather.14.cloned.1.call-done = bf16[512,3584]{1,0:T(8,128)(2,1)} async-done(((bf16[16,3584]{1,0:T(8,128)(2,1)}), bf16[512,3584]{1,0:T(8,128)(2,1)}) %all-gather.14.cloned.1.call-update) | async-done | bytes 3670032 | tf_op jit(solution)/shard_map/all_gather | solution.py:128
  316.9 3.0 fusion.5
  320.1 4.1 fusion.17
  324.2 10.1 %convolution_convert_fusion = bf16[512,3584]{1,0:T(8,128)(2,1)} fusion(bf16[512,3584]{1,0:T(8,128)(2,1)} %param.23, bf16[2,3584,512]{2,1,0:T(8,128)(2,1)} %param.22, bf16[512,3584]{1,0:T(8,128)(2,1)} %all-gather.14.cloned.1.call-done, f32[3584]{0:T(1024)S(1)} %copy-done.8, f32[512]{0:T(512)S(1)} %add_rsqrt_fusion, f32[512,512]{1,0:T(8,128)S(1)} %fusion.17), kind=kOutput, calls=%fused_computation.12 | convolution fusion | flops 3768844288 | bytes 15745024 | tf_op jit(solution)/shard_map/dot_general | solution.py:131
  334.4 80.6 %reduce-scatter.2.cloned.1.call-done = bf16[16,3584]{1,0:T(8,128)(2,1)} async-done(((bf16[512,3584]{1,0:T(8,128)(2,1)}), bf16[16,3584]{1,0:T(8,128)(2,1)}) %reduce-scatter.2.cloned.1.call-update) | async-done | bytes 114704 | tf_op jit(solution)/shard_map/reduce_scatter | solution.py:130
  415.0 0.9 add_convert_fusion
  416.0 10.0 %all_to_all.17 = bf16[4,4,3584]{2,1,0:T(4,128)(2,1)S(1)} all-to-all(bf16[4,4,3584]{2,1,0:T(4,128)(2,1)S(1)} %reshape.198), channel_id=1, replica_groups=mesh['grp'=4,'page'=32] {'grp'}, dimensions={0} | all-to-all | bytes 229376 | tf_op jit(solution)/shard_map/all_to_all | solution.py:139
  426.0 0.9 fusion.9
  (61 shorter events, 8.0 us)
Async XLA Ops:
  7.2 51.5 %all-gather.6.cloned.1.call-start = ((), (), s32[]{:S(2)}) async-start(), calls=%async_computation.4 | async-start | bytes 3784704 | tf_op jit(solution)/shard_map/all_gather | solution.py:84
  7.9 115.9 %all-gather.8.cloned.1.call-start = ((), (), s32[]{:S(2)}) async-start(), calls=%async_computation.5 | async-start | bytes 13246464 | tf_op jit(solution)/shard_map/all_gather | solution.py:83
  8.6 180.5 %all-gather.10.cloned.1.call-start = ((), (), s32[]{:S(2)}) async-start(), calls=%async_computation.6 | async-start | bytes 13246464 | tf_op jit(solution)/shard_map/all_gather | solution.py:88
  9.4 243.3 %all-gather.12.cloned.1.call-start = ((), (), s32[]{:S(2)}) async-start(), calls=%async_computation.7 | async-start | bytes 3784704 | tf_op jit(solution)/shard_map/all_gather | solution.py:122
  14.7 109.2 %copy-start.2 = (bf16[256,3584]{1,0:T(8,128)(2,1)S(1)}, bf16[256,3584]{1,0:T(8,128)(2,1)}, u32[]{:S(2)}) copy-start(bf16[256,3584]{1,0:T(8,128)(2,1)} %param.12) | copy-start | bytes 5505028
  14.7 109.2 %copy-start.7 = (f32[3584]{0:T(1024)S(1)}, f32[3584]{0:T(1024)}, u32[]{:S(2)}) copy-start(f32[3584]{0:T(1024)} %param.16) | copy-start | bytes 43012
  189.1 19.9 %copy-start.9 = (s32[8]{0:T(128)S(1)}, s32[8]{0:T(128)}, u32[]{:S(2)}) copy-start(s32[8]{0:T(128)} %param.15) | copy-start | bytes 100
  189.1 23.9 %copy-start.10 = (u32[128]{0:T(128)S(1)}, u32[128]{0:T(128)}, u32[]{:S(2)}) copy-start(u32[128]{0:T(128)} %constant.48) | copy-start | bytes 1540
  189.2 45.5 %copy-start.6 = (f32[3584]{0:T(1024)S(1)}, f32[3584]{0:T(1024)}, u32[]{:S(2)}) copy-start(f32[3584]{0:T(1024)} %param.20) | copy-start | bytes 43012
  197.9 61.0 %copy-start.1 = (bf16[256,3584]{1,0:T(8,128)(2,1)}, bf16[256,3584]{1,0:T(8,128)(2,1)S(1)}, u32[]{:S(2)}) copy-start(bf16[256,3584]{1,0:T(8,128)(2,1)S(1)} %fusion.8) | copy-start | bytes 5505028
  209.8 8.4 %all-to-all-start.1 = ((s32[4,1,4]{2,1,0:T(1,128)}), s32[4,1,4]{2,1,0:T(1,128)S(1)}, u32[]{:S(2)}, u32[]{:S(2)}) async-start(s32[4,1,4]{2,1,0:T(1,128)} %bitcast.15), calls=%async_computation.1 | async-start | bytes 4096 | tf_op jit(solution)/shard_map/all_to_all | solution.py:115
  213.0 103.9 %all-gather.14.cloned.1.call-start = ((), (), s32[]{:S(2)}) async-start(), calls=%async_computation.8 | async-start | bytes 3784704 | tf_op jit(solution)/shard_map/all_gather | solution.py:128
  252.7 3.1 copy-start
  267.7 3.2 copy-start.4
  270.9 49.0 %copy-start.8 = (f32[3584]{0:T(1024)S(1)}, f32[3584]{0:T(1024)}, u32[]{:S(2)}) copy-start(f32[3584]{0:T(1024)} %param.21) | copy-start | bytes 43012
  271.6 143.4 %reduce-scatter.2.cloned.1.call-start = ((), (), s32[]{:S(2)}) async-start(), calls=%async_computation.9 | async-start | bytes 3784704 | tf_op jit(solution)/shard_map/reduce_scatter | solution.py:130
  316.9 3.1 copy-start.3
  334.3 80.7 %copy-start.5 = (bf16[16,3584]{1,0:T(8,128)(2,1)S(1)}, bf16[16,3584]{1,0:T(8,128)(2,1)}, u32[]{:S(2)}) copy-start(bf16[16,3584]{1,0:T(8,128)(2,1)} %fusion.52) | copy-start | bytes 344068
Sparse Core Ops, SparseCore 0:
  10.3 48.3 all-gather.5
  60.9 62.8 all-gather.7
  126.1 63.0 all-gather.9
  209.2 43.5 all-gather.11
  271.7 45.1 all-gather.13
  334.5 80.4 reduce-scatter.1
where the time goes:
time: 434 us
  waiting for transfers between devices  307 us (71%)
  matrix products  46.6 us (11%)
  blocking collectives  34.5 us (8%)
  other arithmetic  17.6 us (4%)
  between operations  14.9 us (3%)
  local copies, waits for them, and re-layouts  9.25 us (2%)
    reduce_scatter x1, waiting for transfers between devices, on_device(): lax.psum_scatter(jnp.dot(hidden, w_down, preferred_element_type=jnp.float...  80.6 us
    all_gather x1, waiting for transfers between devices, on_device(): lax.all_gather(w_query, 'page', axis=0, tiled=True)  61.2 us
    all_gather x1, waiting for transfers between devices, on_device(): lax.all_gather(w_out, 'page', axis=0, tiled=True)  52.3 us
    all_gather x1, waiting for transfers between devices, on_device(): group_states = lax.all_gather(own_states, 'page', axis=0, tiled=True)  45.3 us
    all_gather x1, waiting for transfers between devices, on_device(): lax.all_gather(w_keyval, 'page', axis=0, tiled=True)  44 us
    all_gather x1, waiting for transfers between devices, on_device(): lax.all_gather(rows, 'page', axis=0, tiled=True)  17.9 us
    unnamed x1, blocking collectives  14.6 us
    dot_general x2, matrix products, fold_normed(): return jnp.dot(normed, piece, preferred_element_type=jnp.float32)  10.5 us
  transfers between devices with their start and end apart: 7, of which 7 were waited for; matrix products, arithmetic and copies ran while one was open for 6% of the time, Pallas kernels for 0%

commit v1 on v0

v1 whole, which is shorter than its diff:
```python
import functools
import math

import jax
import jax.numpy as jnp
from jax import lax
from jax.experimental import pallas as pl
from jax.experimental.pallas import tpu as pltpu
from jax.sharding import PartitionSpec as P

HD = 128
REPORTS = 16
SIDE = 4
WY = 256
BF = jnp.bfloat16
F32 = jnp.float32
MIB = 1 << 20


def vmem():
    return pl.BlockSpec(memory_space=pltpu.VMEM)


def smem():
    return pl.BlockSpec(memory_space=pltpu.SMEM)


def anym():
    return pl.BlockSpec(memory_space=pl.ANY)


def params(mib):
    return pltpu.CompilerParams(vmem_limit_bytes=mib * MIB)


def chip_perm(step):
    pairs = []
    for x in range(SIDE):
        for z in range(SIDE):
            for c in range(2):
                a, b, d = step(x, z, c)
                pairs.append(((x * SIDE + z) * 2 + c, ((a % SIDE) * SIDE + b % SIDE) * 2 + d))
    return pairs


def swap(v):
    return lax.ppermute(v, "page", chip_perm(lambda x, z, c: (x, z, 1 - c)))


def move_a(v, k):
    return lax.ppermute(
        v, "page", chip_perm(lambda x, z, c: (x + k, z, c) if c == 0 else (x, z + k, c))
    )


def move_b(v, k):
    return lax.ppermute(
        v, "page", chip_perm(lambda x, z, c: (x, z + k, c) if c == 0 else (x + k, z, c))
    )


def move_y(v, k):
    return lax.ppermute(v, "grp", [(i, (i + k) % SIDE) for i in range(SIDE)])


def after(v, *others):
    return lax.optimization_barrier((v,) + others)[0]


def rms_scale(values, gain):
    wide = values.astype(F32)
    return wide * lax.rsqrt(jnp.mean(wide * wide, axis=-1, keepdims=True) + 1e-06) * gain


def page_index(lengths, count):
    ends = jnp.cumsum(lengths, dtype=jnp.int32)
    position = jnp.arange(count, dtype=jnp.int32)
    return jnp.sum((position[:, None] >= ends[None, :]).astype(jnp.int32), axis=1)


def run_copies(copies, sems):
    started = []
    for i, (src, dst) in enumerate(copies):
        copy = pltpu.make_async_copy(src, dst, sems.at[i])
        copy.start()
        started.append(copy)
    return started


def gather_line(first, move):
    one = move(first, 1)
    three = move(first, -1)
    half = first.shape[0] // 2
    two_low = move(one[:half], 1)
    two_high = move(three[half:], -1)
    return one, three, two_low, two_high


def qkv_kernel(order, xo, xt, seg_col, seg_row, t, s1, s3, s2a, s2b, out, w, qkv, sems):
    depth = t.shape[1]
    copies = []
    for k, piece, lo, n in ((0, t, 0, 4), (1, s1, 0, 4), (3, s3, 0, 4), (2, s2a, 0, 2), (2, s2b, 2, 2)):
        for j in range(n):
            q = order[k * SIDE + lo + j]
            rows = pl.ds(pl.multiple_of(q * depth, 16), depth)
            copies.append((piece.at[j], w.at[rows, :]))
    for copy in run_copies(copies, sems):
        copy.wait()
    tokens = xo.shape[0]
    tile = 384

    @pl.loop(0, w.shape[1] // tile)
    def _(n):
        cols = pl.ds(pl.multiple_of(n * tile, 128), tile)
        weight = w[:, cols]
        qkv[pl.ds(0, tokens), cols] = jnp.dot(xo[...], weight, preferred_element_type=F32).astype(BF)
        qkv[pl.ds(tokens, tokens), cols] = jnp.dot(xt[...], weight, preferred_element_type=F32).astype(BF)

    heads = out.shape[1] // HD

    @pl.loop(0, 2)
    def _(b):
        rows = pl.ds(pl.multiple_of(b * tokens, tokens), tokens)
        same = seg_col[rows, :] == seg_row[b]
        keys = qkv[rows, heads * HD : (heads + 1) * HD]
        values = qkv[rows, (heads + 1) * HD : (heads + 2) * HD]
        for h in range(heads):
            query = qkv[rows, h * HD : (h + 1) * HD]
            scores = lax.dot_general(
                query, keys, (((1,), (1,)), ((), ())), preferred_element_type=F32
            ) * (1.0 / math.sqrt(HD))
            scores = jnp.where(same, scores, -1e30)
            top = jnp.max(scores, axis=1, keepdims=True)
            e = jnp.exp(scores - top)
            weights = (e / jnp.sum(e, axis=1, keepdims=True)).astype(BF)
            out[rows, h * HD : (h + 1) * HD] = jnp.dot(
                weights, values, preferred_element_type=F32
            ).astype(BF)


def page_qkv(order, x_own, x_other, seg_col, seg_row, pieces):
    tokens, width = x_own.shape
    cols = pieces[0].shape[2]
    return pl.pallas_call(
        qkv_kernel,
        out_shape=jax.ShapeDtypeStruct((2 * tokens, cols - 2 * HD), BF),
        in_specs=[smem()] + [vmem()] * 4 + [anym()] * 5,
        out_specs=vmem(),
        scratch_shapes=[
            pltpu.VMEM((width, cols), BF),
            pltpu.VMEM((2 * tokens, cols), BF),
            pltpu.SemaphoreType.DMA((16,)),
        ],
        compiler_params=params(40),
        cost_estimate=pl.CostEstimate(
            flops=2 * 2 * tokens * width * cols, bytes_accessed=2 * width * cols, transcendentals=0
        ),
    )(order, x_own, x_other, seg_col, seg_row, *pieces)


def out_kernel(
    order, pos, tok_own, tok_other, att, att_in, member, member_t, inv, inv_t,
    w4, u1, u3, u2a, u2b, rt, r1, r3, r2a, r2b,
    st_own, st_other, pool_own, pool_other, w, full, sems,
):
    depth = w4.shape[2]
    wy = w4.shape[3]
    core = pos[0]
    grp = pos[1]
    copies = []
    for i, piece, lo, n in ((0, w4, 0, 4), (1, u1, 0, 4), (3, u3, 0, 4), (2, u2a, 0, 2), (2, u2b, 2, 2)):
        block = lax.rem(grp + (SIDE - i), SIDE)
        cols = pl.ds(pl.multiple_of(block * wy, 128), wy)
        for k in range(n):
            for j in range(SIDE):
                rows = pl.ds(pl.multiple_of(order[(lo + k) * SIDE + j] * depth, 16), depth)
                copies.append((piece.at[k, j], w.at[rows, cols]))
    wr = rt.shape[2]
    for k, piece, lo, n in ((0, rt, 0, 4), (1, r1, 0, 4), (3, r3, 0, 4), (2, r2a, 0, 2), (2, r2b, 2, 2)):
        for j in range(n):
            rows = pl.ds(pl.multiple_of(order[k * SIDE + lo + j] * depth, 16), depth)
            copies.append((piece.at[j], w.at[rows, pl.ds(SIDE * wy, wr)]))
    started = run_copies(copies, sems)
    tokens = tok_own.shape[0]
    half = att.shape[1]
    mine = pl.ds(pl.multiple_of(core * half, 128), half)
    theirs = pl.ds(pl.multiple_of((1 - core) * half, 128), half)
    full[0:tokens, mine] = att[0:tokens, :]
    full[tokens : 2 * tokens, mine] = att[tokens : 2 * tokens, :]
    full[0:tokens, theirs] = att_in[tokens : 2 * tokens, :]
    full[tokens : 2 * tokens, theirs] = att_in[0:tokens, :]
    for copy in started:
        copy.wait()
    tile = 256
    width = w.shape[1]

    @pl.loop(0, width // tile)
    def _(n):
        cols = pl.ds(pl.multiple_of(n * tile, 128), tile)
        there = pl.ds(pl.multiple_of(core * width + n * tile, 128), tile)
        weight = w[:, cols]
        for rows, tok, st, mem, ratio, pool in (
            (0, tok_own, st_own, member, inv, pool_own),
            (tokens, tok_other, st_other, member_t, inv_t, pool_other),
        ):
            projected = jnp.dot(full[rows : rows + tokens, :], weight, preferred_element_type=F32)
            states = (tok[:, there].astype(F32) + projected).astype(BF)
            st[:, cols] = states
            pool[:, cols] = (
                jnp.dot(mem[...], states, preferred_element_type=F32) / ratio[...]
            ).astype(BF)


def page_out(order, pos, tok_own, tok_other, att, att_in, members, lens, y_pieces, r_pieces):
    tokens = tok_own.shape[0]
    depth = y_pieces[0].shape[2]
    width = SIDE * y_pieces[0].shape[3] + r_pieces[0].shape[2]
    rows = SIDE * SIDE * depth
    pages = members[0].shape[0]
    st = jax.ShapeDtypeStruct((tokens, width), BF)
    pool = jax.ShapeDtypeStruct((pages, width), BF)
    return pl.pallas_call(
        out_kernel,
        out_shape=(st, st, pool, pool),
        in_specs=[smem()] * 2 + [vmem()] * 8 + [anym()] * 10,
        out_specs=(vmem(),) * 4,
        scratch_shapes=[
            pltpu.VMEM((rows, width), BF),
            pltpu.VMEM((2 * tokens, rows), BF),
            pltpu.SemaphoreType.DMA((80,)),
        ],
        compiler_params=params(40),
        cost_estimate=pl.CostEstimate(
            flops=2 * 2 * tokens * width * rows, bytes_accessed=2 * width * rows, transcendentals=0
        ),
    )(order, pos, tok_own, tok_other, att, att_in, *members, *lens, *y_pieces, *r_pieces)


def doc_kernel(pos, rows, label_col, label_row, out):
    count = out.shape[0]
    mine = pl.ds(pl.multiple_of(pos[1] * count, count), count)
    keys = rows[:, HD : 2 * HD]
    query = rows[mine, HD : 2 * HD]
    scores = lax.dot_general(
        query, keys, (((1,), (1,)), ((), ())), preferred_element_type=F32
    ) * (1.0 / HD)
    scores = jnp.where(label_col[...] == label_row[...], scores, -1e30)
    top = jnp.max(scores, axis=1, keepdims=True)
    e = jnp.exp(scores - top)
    weights = (e / jnp.sum(e, axis=1, keepdims=True)).astype(BF)
    context = jnp.dot(weights, keys, preferred_element_type=F32)
    out[...] = (rows[mine, 0:HD].astype(F32) + context).astype(BF)


def doc_attention(pos, rows, label_col, label_row):
    count = label_col.shape[0]
    return pl.pallas_call(
        doc_kernel,
        out_shape=jax.ShapeDtypeStruct((count, HD), BF),
        in_specs=[smem()] + [vmem()] * 3,
        out_specs=vmem(),
        compiler_params=params(24),
    )(pos, rows, label_col, label_row)


def ffn_kernel(
    order, order_t, pos, t, b1, b2, b3, tt, c1, c2, c3, gain, gate_up, down, pick,
    own, other, states, x, mixed, hidden, wgu, wd, acc, sems,
):
    core = pos[0]
    width = gain.shape[1]
    units = hidden.shape[1]
    half = units // 2
    weights = []
    n_sem = 32
    for n in range(2):
        for g in range(2):
            weights.append(
                pltpu.make_async_copy(
                    gate_up.at[g, :, n * half : (n + 1) * half],
                    wgu.at[g, :, n * half : (n + 1) * half],
                    sems.at[n_sem + 2 * n + g],
                )
            )
    down_copy = pltpu.make_async_copy(down, wd, sems.at[n_sem + 4])
    copies = []
    for table, side, pieces in ((order, core, (t, b1, b2, b3)), (order_t, 1 - core, (tt, c1, c2, c3))):
        for k, piece in enumerate(pieces):
            for j in range(SIDE):
                head = table[k * SIDE + j] * 2 + side
                copies.append((piece.at[j], x.at[:, pl.ds(pl.multiple_of(head * HD, HD), HD)]))
    started = run_copies(copies, sems)
    for copy in weights:
        copy.start()
    down_copy.start()
    for copy in started:
        copy.wait()
    chunk = 32

    @pl.loop(0, x.shape[0] // chunk)
    def _(i):
        rows = pl.ds(pl.multiple_of(i * chunk, chunk), chunk)
        wide = x[rows, 0:width].astype(F32)
        scale = lax.rsqrt(jnp.mean(wide * wide, axis=1, keepdims=True) + 1e-06)
        mixed[rows, :] = (wide * scale * gain[...]).astype(BF)

    for n in range(2):
        weights[2 * n].wait()
        weights[2 * n + 1].wait()
        cols = slice(n * half, (n + 1) * half)
        gate = jnp.dot(mixed[...], wgu[0, :, cols], preferred_element_type=F32)
        up = jnp.dot(mixed[...], wgu[1, :, cols], preferred_element_type=F32)
        hidden[:, cols] = (gate * jax.nn.sigmoid(gate) * up).astype(BF)
    down_copy.wait()
    tile = 512
    pages = acc.shape[1]

    @pl.loop(0, width // tile)
    def _(n):
        cols = pl.ds(pl.multiple_of(n * tile, 128), tile)
        part = jnp.dot(hidden[...], wd[:, cols], preferred_element_type=F32)
        acc[...] = part.reshape(acc.shape)
        for k in range(SIDE):
            for j in range(SIDE):
                own[j, k, :, cols] = acc[order[16 + k * SIDE + j] * 2 + core].astype(BF)
                other[j, k, :, cols] = acc[order_t[16 + k * SIDE + j] * 2 + 1 - core].astype(BF)
        states[:, cols] = jnp.dot(pick[...], x[:, cols], preferred_element_type=F32)


def feed_forward(order, order_t, pos, pieces, pieces_t, gain, gate_up, down, pick):
    width = gain.shape[1]
    units = down.shape[0]
    pages, count = pick.shape
    part = jax.ShapeDtypeStruct((SIDE, SIDE, pages, width), BF)
    return pl.pallas_call(
        ffn_kernel,
        out_shape=(part, part, jax.ShapeDtypeStruct((pages, width), F32)),
        in_specs=[smem()] * 3 + [anym()] * 8 + [vmem()] + [anym()] * 2 + [vmem()],
        out_specs=(vmem(),) * 3,
        scratch_shapes=[
            pltpu.VMEM((count, 2 * SIDE * SIDE * HD), BF),
            pltpu.VMEM((count, width), BF),
            pltpu.VMEM((count, units), BF),
            pltpu.VMEM((2, width, units), BF),
            pltpu.VMEM((units, width), BF),
            pltpu.VMEM((count // pages, pages, 512), F32),
            pltpu.SemaphoreType.DMA((40,)),
        ],
        compiler_params=params(40),
        cost_estimate=pl.CostEstimate(
            flops=6 * count * width * units, bytes_accessed=6 * width * units, transcendentals=0
        ),
    )(order, order_t, pos, *pieces, *pieces_t, gain, gate_up, down, pick)


def on_device(
    tokens,
    page_lengths,
    page_group,
    page_report,
    attn_gain,
    w_query,
    w_keyval,
    w_out,
    doc_gain,
    ffn_gain,
    gate_up_weight,
    w_down,
):
    count, width = tokens.shape
    pages = page_lengths.shape[1]
    grp = lax.axis_index("grp")
    page = lax.axis_index("page")
    core = page % 2
    z = (page // 2) % SIDE
    x = page // (2 * SIDE)
    pos = jnp.stack([core, grp]).astype(jnp.int32)
    step = jnp.arange(SIDE, dtype=jnp.int32)
    zero_order = (((x - step) % SIDE)[None, :] * SIDE + ((z - step) % SIDE)[:, None]).reshape(-1)
    one_order = (((x - step) % SIDE)[:, None] * SIDE + ((z - step) % SIDE)[None, :]).reshape(-1)
    order = jnp.where(core == 0, zero_order, one_order)
    order_t = jnp.where(core == 0, one_order, zero_order)
    zero_dest = (((x + step) % SIDE)[None, :] * SIDE + ((z + step) % SIDE)[:, None]).reshape(-1)
    one_dest = (((x + step) % SIDE)[:, None] * SIDE + ((z + step) % SIDE)[None, :]).reshape(-1)
    dest = jnp.where(core == 0, zero_dest, one_dest)
    dest_t = jnp.where(core == 0, one_dest, zero_dest)

    out_half = w_out.shape[1] // 2
    q_half = w_query.shape[1] // 2

    def out_cols(c):
        return lax.dynamic_slice_in_dim(w_out, c * out_half, out_half, 1)

    def qkv_cols(c):
        return jnp.concatenate(
            [
                lax.dynamic_slice_in_dim(w_query, c * q_half, q_half, 1),
                lax.dynamic_slice_in_dim(w_keyval, c * HD, HD, 1),
                lax.dynamic_slice_in_dim(w_keyval, (2 + c) * HD, HD, 1),
            ],
            axis=1,
        )

    def pair_up(mine, got):
        low = jnp.where(core == 0, mine, got)
        high = jnp.where(core == 0, got, mine)
        return jnp.concatenate([low, high], axis=0)

    wo = pair_up(out_cols(core), swap(out_cols(1 - core)))
    wq = pair_up(qkv_cols(core), swap(qkv_cols(1 - core)))
    tok_other = swap(tokens)
    len_other = swap(page_lengths)

    wo_y = lax.dynamic_slice_in_dim(wo, grp * WY, WY, 1)
    wo_r = wo[:, SIDE * WY :]

    def line_a(v):
        return jnp.stack([v, move_a(v, 1), move_a(v, 2), move_a(v, -1)])

    def line_b(t):
        one = move_b(t, 1)
        three = move_b(t, -1)
        return (t, one, three, move_b(one[:2], 1), move_b(three[2:], -1))

    ty = line_a(wo_y)
    tq = line_a(wq)
    tr = line_a(wo_r)
    w4 = jnp.stack([ty, move_b(ty, 1), move_b(ty, 2), move_b(ty, -1)])
    y1 = move_y(w4, 1)
    y3 = move_y(w4, -1)
    y_pieces = (w4, y1, y3, move_y(y1[:2], 1), move_y(y3[2:], -1))
    q_pieces = line_b(tq)
    r_pieces = line_b(tr)

    labels = page_group[:, 0] * REPORTS + page_report
    all_labels = lax.all_gather(labels, ("grp", "page"), axis=0, tiled=True)

    gain = attn_gain[None, :]
    x_own = rms_scale(tokens, gain).astype(BF)
    x_other = rms_scale(tok_other, gain).astype(BF)
    seg_own = page_index(page_lengths[0], count)
    seg_other = page_index(len_other[0], count)
    seg_col = jnp.concatenate([seg_own, seg_other])[:, None]
    seg_row = jnp.stack([seg_own, seg_other])[:, None, :]
    att = page_qkv(order, x_own, x_other, seg_col, seg_row, q_pieces)
    att_in = swap(att)
    names = jnp.arange(pages, dtype=jnp.int32)[:, None]
    members = tuple((seg[None, :] == names).astype(BF) for seg in (seg_own, seg_other))
    lens = tuple(v[0][:, None].astype(F32) for v in (page_lengths, len_other))
    st_own, st_other, pool_own, pool_other = page_out(
        order, pos, tokens, tok_other, att, att_in, members, lens, y_pieces, r_pieces
    )

    def side_by_side(mine, got):
        left = jnp.where(core == 0, mine, got)
        right = jnp.where(core == 0, got, mine)
        return jnp.concatenate([left, right], axis=1)

    vectors = side_by_side(pool_own, swap(pool_other))
    token_states = side_by_side(st_own, swap(st_other))

    keys = rms_scale(vectors, doc_gain).astype(BF)
    heads = width // HD
    slots = 2 * SIDE * SIDE
    blocks = jnp.stack([vectors.reshape(pages, heads, HD), keys.reshape(pages, heads, HD)], axis=2)
    blocks = blocks.reshape(pages, heads, 2 * HD).transpose(1, 0, 2)
    blocks = jnp.pad(blocks, ((0, slots - heads), (0, 0), (0, 0)))
    blocks = jnp.broadcast_to(blocks[None], (SIDE,) + blocks.shape).reshape(-1, pages, 2 * HD)
    gathered = lax.all_to_all(blocks, ("grp", "page"), split_axis=0, concat_axis=0, tiled=True)
    plane = slots * pages
    label_col = lax.dynamic_slice_in_dim(all_labels, grp * plane, plane)[:, None]
    mixed = doc_attention(pos, gathered.reshape(-1, 2 * HD), label_col, all_labels[None, :])

    line = line_a(mixed)
    pieces = (line, move_b(line, 1), move_b(line, 2), move_b(line, -1))
    pieces_t = tuple(swap(v) for v in pieces)
    pick = (
        jnp.arange(plane, dtype=jnp.int32)[None, :] == page * pages + jnp.arange(pages)[:, None]
    ).astype(BF)
    own, other, states = feed_forward_call(
        order, order_t, dest, dest_t, pos, pieces, pieces_t, ffn_gain[None, :], gate_up_weight, w_down, pick
    )
    got = swap(other)

    def total(*terms):
        return sum(v.astype(F32) for v in terms)

    part = [total(own[j], got[j]).astype(BF) for j in range(SIDE)]
    part = total(part[0], *(move_a(part[j], j) for j in range(1, SIDE)))
    part = [part[k].astype(BF) if k else part[k] for k in range(SIDE)]
    summed = total(part[0], *(move_b(part[k], k) for k in range(1, SIDE)))
    page_embeddings = (states + summed).astype(BF)
    return (token_states, page_embeddings)


def feed_forward_call(order, order_t, dest, dest_t, pos, *rest):
    tables = jnp.concatenate([order, dest])
    tables_t = jnp.concatenate([order_t, dest_t])
    return feed_forward(tables, tables_t, pos, *rest)


def solution(mesh):
    in_specs = (
        P(("grp", "page"), None),
        P(("grp", "page"), None),
        P(("grp", "page"), None),
        P(("grp", "page")),
        P(),
        P("page", None),
        P("page", None),
        P("page", None),
        P(),
        P(),
        P(None, None, "page"),
        P("page", None),
    )
    out_specs = (P(("grp", "page"), None), P(("grp", "page"), None))
    return jax.shard_map(
        on_device, mesh=mesh, in_specs=in_specs, out_specs=out_specs, check_vma=False
    )
```

time: 434 us -> 282 us (0.65)
  waiting for transfers between devices: 307 us -> 82.1 us
  starting transfers between devices: 3.46 us -> 57.8 us
  matrix products: 46.6 us -> 0 us
  Pallas kernels: 0 us -> 37.5 us
  blocking collectives: 34.5 us -> 67.3 us
  between operations: 14.9 us -> 1.1 us
  local copies, waits for them, and re-layouts: 9.25 us -> 20.1 us
    all_gather x5 -> x0, waiting for transfers between devices: 221 us -> none  [the longest x1 61.2 us: on_device(): lax.all_gather(w_query, 'page', axis=0, tiled=True)]
    ppermute x0 -> x48, waiting for transfers between devices: none -> 82.1 us  [the longest x15 45 us: move_a(): lax.ppermute(v, 'page', chip_perm(lambda x, z, c: (x + k, z, c) if c == 0...]
    reduce_scatter x1 -> x0, waiting for transfers between devices: 80.6 us -> none  [on_device(): lax.psum_scatter(jnp.dot(hidden, w_down, preferred_element_type=jnp.float...]
    unnamed x1, blocking collectives: 14.6 us -> 67.3 us
    ppermute x0 -> x48, starting transfers between devices: none -> 48.8 us  [the longest x17 26.6 us: move_b(): lax.ppermute(v, 'page', chip_perm(lambda x, z, c: (x, z + k, c) if c == 0...]
    dot_general x9 -> x0, matrix products: 40.7 us -> none  [the longest x2 10.5 us: fold_normed(): return jnp.dot(normed, piece, preferred_element_type=jnp.float32)]
    pallas_call x0 -> x4, Pallas kernels: none -> 37.5 us  [the longest x1 14.3 us: page_out(): pl.pallas_call(out_kernel, out_shape=(st, st, pool, pool), in_specs=[smem...]
    all_to_all x2 -> x0, blocking collectives: 19.9 us -> none  [the longest x1 9.99 us: on_device(): lax.all_to_all(finished, 'grp', split_axis=0, concat_axis=0, tiled=True)]
  transfers between devices with their start and end apart: 7 -> 49, of which waited for: 7 -> 31; matrix products, arithmetic and copies ran while one was open for 6% -> 8% of each run, Pallas kernels for 0% -> 5%
where the time goes in v1:
time: 282 us; the launch traced here: 281 us
  waiting for transfers between devices  82.1 us (29%)
  blocking collectives  67.3 us (24%)
  starting transfers between devices  57.8 us (20%)
  Pallas kernels  37.5 us (13%)
  local copies, waits for them, and re-layouts  20.1 us (7%)
  other arithmetic  15.1 us (5%)
    unnamed x1, blocking collectives  67.3 us
    ppermute x15, waiting for transfers between devices, move_a(): lax.ppermute(v, 'page', chip_perm(lambda x, z, c: (x + k, z, c) if c == 0...  45 us
    ppermute x17, waiting for transfers between devices, move_b(): lax.ppermute(v, 'page', chip_perm(lambda x, z, c: (x, z + k, c) if c == 0...  31.6 us
    ppermute x17, starting transfers between devices, move_b(): lax.ppermute(v, 'page', chip_perm(lambda x, z, c: (x, z + k, c) if c == 0...  26.6 us
    pallas_call x1, Pallas kernels, page_out(): pl.pallas_call(out_kernel, out_shape=(st, st, pool, pool), in_specs=[smem...  14.3 us
    ppermute x15, starting transfers between devices, move_a(): lax.ppermute(v, 'page', chip_perm(lambda x, z, c: (x + k, z, c) if c == 0...  13.7 us
    pallas_call x1, Pallas kernels, page_qkv(): pl.pallas_call(qkv_kernel, out_shape=jax.ShapeDtypeStruct((2 * tokens, co...  13.6 us
    all_to_all x1, starting transfers between devices, on_device(): lax.all_to_all(blocks, ('grp', 'page'), split_axis=0, concat_axis=0, tile...  8.99 us
  transfers between devices with their start and end apart: 49, of which 31 were waited for; matrix products, arithmetic and copies ran while one was open for 8% of the time, Pallas kernels for 5%

profile of v1, /device:TPU:0, one launch (start us, length us, event | category | flops | bytes accessed | tf_op | source)
XLA Modules:
  0.0 280.8 jit_solution(11468821225550951993)
XLA Ops:
  4.5 2.9 %collective-permute-start.5 = (bf16[224,1152]{1,0:T(8,128)(2,1)S(1)}, bf16[224,1152]{1,0:T(8,128)(2,1)S(1)}, u32[]{:S(2)}, u32[]{:S(2)}) collective-permute-start(bf16[224,1152]{1,0:T(8,128)(2,1)S(1)} %get-tuple-element.26), channel_id=1, source_target_pairs={{0,24},{1,7},{2,26},{3,1},{4,28},{5,3},{6,30},{7,5},{8,0},{9,15},{... | collective-permute-start | bytes 1548296 | tf_op jit(solution)/shard_map/ppermute | solution.py:51
  10.6 9.0 %collective-permute-done.5 = bf16[224,1152]{1,0:T(8,128)(2,1)S(1)} collective-permute-done((bf16[224,1152]{1,0:T(8,128)(2,1)S(1)}, bf16[224,1152]{1,0:T(8,128)(2,1)S(1)}, u32[]{:S(2)}, u32[]{:S(2)}) %collective-permute-start.5) | collective-permute-done | bytes 516128 | tf_op jit(solution)/shard_map/ppermute | solution.py:51
  20.1 3.5 %collective-permute-done.3 = bf16[224,1152]{1,0:T(8,128)(2,1)} collective-permute-done((bf16[224,1152]{1,0:T(8,128)(2,1)S(1)}, bf16[224,1152]{1,0:T(8,128)(2,1)}, u32[]{:S(2)}, u32[]{:S(2)}) %collective-permute-start.3) | collective-permute-done | bytes 516128 | tf_op jit(solution)/shard_map/ppermute | solution.py:51
  23.7 2.9 %pad_maximum_fusion.t = bf16[4,224,1152]{2,1,0:T(8,128)(2,1)} fusion(bf16[1,224,1152]{2,1,0:T(8,128)(2,1)S(1)} %bitcast.88, bf16[1,224,1152]{2,1,0:T(8,128)(2,1)} %bitcast.11, bf16[1,224,1152]{2,1,0:T(8,128)(2,1)} %bitcast.10, bf16[1,224,1152]{2,1,0:T(8,128)(2,1)S(1)} %get-tuple-element.25), kind=kLoop, calls=%fused_computation.10 | loop fusion | flops 3096576 | bytes 4128768 | tf_op jit(solution)/shard_map/stack | solution.py:418
  28.5 2.1 collective-permute-start.7
  32.2 3.4 %collective-permute-done.14 = bf16[112,256]{1,0:T(8,128)(2,1)S(1)} collective-permute-done((bf16[112,256]{1,0:T(8,128)(2,1)S(1)}, bf16[112,256]{1,0:T(8,128)(2,1)S(1)}, u32[]{:S(2)}, u32[]{:S(2)}) %collective-permute-start.14) | collective-permute-done | bytes 57376 | tf_op jit(solution)/shard_map/ppermute | solution.py:51
  35.6 2.1 collective-permute-done.13
  42.5 2.6 collective-permute-done.24
  47.4 3.1 %collective-permute-done.23 = bf16[112,768]{1,0:T(8,128)(2,1)S(1)} collective-permute-done((bf16[112,768]{1,0:T(8,128)(2,1)S(1)}, bf16[112,768]{1,0:T(8,128)(2,1)S(1)}, u32[]{:S(2)}, u32[]{:S(2)}) %collective-permute-start.23) | collective-permute-done | bytes 172064 | tf_op jit(solution)/shard_map/ppermute | solution.py:51
  51.5 6.1 %collective-permute-done.22 = bf16[112,768]{1,0:T(8,128)(2,1)S(1)} collective-permute-done((bf16[112,768]{1,0:T(8,128)(2,1)S(1)}, bf16[112,768]{1,0:T(8,128)(2,1)S(1)}, u32[]{:S(2)}, u32[]{:S(2)}) %collective-permute-start.22) | collective-permute-done | bytes 172064 | tf_op jit(solution)/shard_map/ppermute | solution.py:51
  59.0 2.5 collective-permute-done.17
  66.6 4.4 %collective-permute-done.15 = bf16[4,112,256]{2,1,0:T(8,128)(2,1)S(1)} collective-permute-done((bf16[4,112,256]{2,1,0:T(8,128)(2,1)S(1)}, bf16[4,112,256]{2,1,0:T(8,128)(2,1)S(1)}, u32[]{:S(2)}, u32[]{:S(2)}) %collective-permute-start.15) | collective-permute-done | bytes 229408 | tf_op jit(solution)/shard_map/ppermute | solution.py:57
  80.1 3.3 %collective-permute-start.9 = (bf16[2,224,1152]{2,1,0:T(8,128)(2,1)S(1)}, bf16[2,224,1152]{2,1,0:T(8,128)(2,1)S(1)}, u32[]{:S(2)}, u32[]{:S(2)}) collective-permute-start(bf16[2,224,1152]{2,1,0:T(8,128)(2,1)S(1)} %slice.80), channel_id=1, source_target_pairs={{0,6},{1,25},{2,0},{3,27},{4,2},{5,29},{6,4},{7,31},{8,14},{9,1},{... | collective-permute-start | bytes 3096584 | tf_op jit(solution)/shard_map/ppermute | solution.py:57
  83.4 2.7 fusion.5
  86.0 8.5 %collective-permute-done.8.s2a = bf16[2,224,1152]{2,1,0:T(8,128)(2,1)S(1)} collective-permute-done((bf16[2,224,1152]{2,1,0:T(8,128)(2,1)S(1)}, bf16[2,224,1152]{2,1,0:T(8,128)(2,1)S(1)}, u32[]{:S(2)}, u32[]{:S(2)}) %collective-permute-start.8) | collective-permute-done | bytes 1032224 | tf_op jit(solution)/shard_map/ppermute | solution.py:57
  95.5 13.6 %shard_map.131.att = bf16[512,896]{1,0:T(8,128)(2,1)} custom-call(s32[16]{0:T(128)S(1)} %select_n.194.order, bf16[256,3584]{1,0:T(8,128)(2,1)S(1)} %get-tuple-element.43.xo, bf16[256,3584]{1,0:T(8,128)(2,1)S(1)} %get-tuple-element.42.xt, s32[512,1]{1,0:T(8,128)S(1)} %copy-done.4, s32[2,1,256]{2,1,0:T(1,128)S(1)} %broadcast_in_dim.13.seg_row, ...), custom_call_target="tpu_custom_call" | custom-call | flops 4227858432 | bytes 8257536 | tf_op jit(solution)/shard_map/pallas_call | solution.py:144
  111.3 2.9 %collective-permute-start.21 = (bf16[2,4,112,256]{3,2,1,0:T(8,128)(2,1)}, bf16[2,4,112,256]{3,2,1,0:T(8,128)(2,1)}, u32[]{:S(2)}, u32[]{:S(2)}) collective-permute-start(bf16[2,4,112,256]{3,2,1,0:T(8,128)(2,1)} %slice.82), channel_id=1, source_target_pairs={{0,96},{32,0},{64,32},{96,64},{1,97},{33,1},{65,33},{97,65},{2,98}... | collective-permute-start | bytes 1376264 | tf_op jit(solution)/shard_map/ppermute | solution.py:63
  117.1 2.6 collective-permute-start.28
  120.0 4.3 %collective-permute-done.27.r2a = bf16[2,112,768]{2,1,0:T(8,128)(2,1)} collective-permute-done((bf16[2,112,768]{2,1,0:T(8,128)(2,1)}, bf16[2,112,768]{2,1,0:T(8,128)(2,1)}, u32[]{:S(2)}, u32[]{:S(2)}) %collective-permute-start.27) | collective-permute-done | bytes 344096 | tf_op jit(solution)/shard_map/ppermute | solution.py:57
  129.4 14.3 %shard_map.132 = (bf16[256,1792]{1,0:T(8,128)(2,1)S(1)}, bf16[256,1792]{1,0:T(8,128)(2,1)S(1)}, bf16[8,1792]{1,0:T(8,128)(2,1)S(1)}, bf16[8,1792]{1,0:T(8,128)(2,1)S(1)}) custom-call(s32[16]{0:T(128)S(1)} %select_n.194.order, s32[2]{0:T(128)S(1)} %pad_add_fusion.2.pos, bf16[256,3584]{1,0:T(8,128)(2,1)S(1)} %copy-done, ...), custom_call_target="tpu_custom_call" | custom-call | flops 3288334336 | bytes 6422528 | tf_op jit(solution)/shard_map/pallas_call | solution.py:222
  148.0 9.0 %all-to-all-start = ((bf16[128,8,256]{2,1,0:T(8,128)(2,1)}), bf16[128,8,256]{2,1,0:T(8,128)(2,1)S(1)}, u32[]{:S(2)}, u32[]{:S(2)}) async-start(bf16[128,8,256]{2,1,0:T(8,128)(2,1)} %bitcast.34), calls=%async_computation | async-start | bytes 1048576 | tf_op jit(solution)/shard_map/all_to_all | solution.py:469
  157.1 67.3 %all-reduce.1 = s32[1024]{0:T(1024)S(1)} all-reduce(s32[1024]{0:T(1024)S(1)} %fusion.28), channel_id=1, replica_groups=mesh['grp'=4,'page'=32] {'grp','page'}, use_global_device_ids=true, to_apply=%add.1 | all-reduce | flops 1024 | bytes 8192
  230.3 2.1 collective-permute-done.32
  234.6 2.5 collective-permute-start.35
  238.6 2.6 collective-permute-done.34.b1
  241.2 3.1 %collective-permute-done.35.b2 = bf16[4,256,128]{2,1,0:T(8,128)(2,1)S(1)} collective-permute-done((bf16[4,256,128]{2,1,0:T(8,128)(2,1)S(1)}, bf16[4,256,128]{2,1,0:T(8,128)(2,1)S(1)}, u32[]{:S(2)}, u32[]{:S(2)}) %collective-permute-start.35) | collective-permute-done | bytes 262176 | tf_op jit(solution)/shard_map/ppermute | solution.py:57
  248.5 8.2 %shard_map.134 = (bf16[4,4,8,3584]{3,2,1,0:T(8,128)(2,1)S(1)}, bf16[4,4,8,3584]{3,2,1,0:T(8,128)(2,1)S(1)}, f32[8,3584]{1,0:T(8,128)S(1)}) custom-call(s32[32]{0:T(128)S(1)} %pad_add_fusion.3.order, s32[32]{0:T(128)S(1)} %pad_add_fusion.4.order_t, s32[2]{0:T(128)S(1)} %pad_add_fusion.2.pos, bf16[4,256,128]{2,1,0:T(8,128)(2,1)S(1)} %pad_maximum_fusion.5.t, ...), custom_call_target="tpu_custom_call" | custom-call | flops 2818572288 | bytes 11010048 | tf_op jit(solution)/shard_map/pallas_call | solution.py:335
  262.1 3.4 %collective-permute-done.44 = bf16[4,8,3584]{2,1,0:T(8,128)(2,1)S(1)} collective-permute-done((bf16[4,8,3584]{2,1,0:T(8,128)(2,1)S(1)}, bf16[4,8,3584]{2,1,0:T(8,128)(2,1)S(1)}, u32[]{:S(2)}, u32[]{:S(2)}) %collective-permute-start.44) | collective-permute-done | bytes 229408 | tf_op jit(solution)/shard_map/ppermute | solution.py:51
  265.5 3.1 %collective-permute-done.43 = bf16[4,8,3584]{2,1,0:T(8,128)(2,1)S(1)} collective-permute-done((bf16[4,8,3584]{2,1,0:T(8,128)(2,1)S(1)}, bf16[4,8,3584]{2,1,0:T(8,128)(2,1)S(1)}, u32[]{:S(2)}, u32[]{:S(2)}) %collective-permute-start.43) | collective-permute-done | bytes 229408 | tf_op jit(solution)/shard_map/ppermute | solution.py:51
  268.6 2.4 collective-permute-done.42
  271.2 2.7 collective-permute-start.47
  276.2 3.4 %collective-permute-done.46 = bf16[8,3584]{1,0:T(8,128)(2,1)S(1)} collective-permute-done((bf16[8,3584]{1,0:T(8,128)(2,1)S(1)}, bf16[8,3584]{1,0:T(8,128)(2,1)S(1)}, u32[]{:S(2)}, u32[]{:S(2)}) %collective-permute-start.46) | collective-permute-done | bytes 57376 | tf_op jit(solution)/shard_map/ppermute | solution.py:57
  (189 shorter events, 73.1 us)
Async XLA Ops:
  2.8 70.9 %collective-permute-start = (bf16[256,3584]{1,0:T(8,128)(2,1)}, bf16[256,3584]{1,0:T(8,128)(2,1)}, u32[]{:S(2)}, u32[]{:S(2)}) collective-permute-start(bf16[256,3584]{1,0:T(8,128)(2,1)} %tok_own.1), channel_id=1, source_target_pairs={{0,1},{1,0},{2,3},{3,2},{4,5},{5,4},{6,7},{7,6},{8,9},{9,8},{10,11... | collective-permute-start | bytes 5505032 | tf_op jit(solution)/shard_map/ppermute | solution.py:47
  3.3 28.1 %collective-permute-start.1 = (s32[1,8]{1,0:T(1,128)}, s32[1,8]{1,0:T(1,128)S(1)}, u32[]{:S(2)}, u32[]{:S(2)}) collective-permute-start(s32[1,8]{1,0:T(1,128)} %param.13), channel_id=1, source_target_pairs={{0,1},{1,0},{2,3},{3,2},{4,5},{5,4},{6,7},{7,6},{8,9},{9,8},{10,11... | collective-permute-start | bytes 104 | tf_op jit(solution)/shard_map/ppermute | solution.py:47
  4.5 15.1 %collective-permute-start.5 = (bf16[224,1152]{1,0:T(8,128)(2,1)S(1)}, bf16[224,1152]{1,0:T(8,128)(2,1)S(1)}, u32[]{:S(2)}, u32[]{:S(2)}) collective-permute-start(bf16[224,1152]{1,0:T(8,128)(2,1)S(1)} %get-tuple-element.26), channel_id=1, source_target_pairs={{0,24},{1,7},{2,26},{3,1},{4,28},{5,3},{6,30},{7,5},{8,0},{9,15},{... | collective-permute-start | bytes 1548296 | tf_op jit(solution)/shard_map/ppermute | solution.py:51
  7.4 12.7 %collective-permute-start.4 = (bf16[224,1152]{1,0:T(8,128)(2,1)S(1)}, bf16[224,1152]{1,0:T(8,128)(2,1)}, u32[]{:S(2)}, u32[]{:S(2)}) collective-permute-start(bf16[224,1152]{1,0:T(8,128)(2,1)S(1)} %get-tuple-element.26), channel_id=1, source_target_pairs={{0,16},{1,5},{2,18},{3,7},{4,20},{5,1},{6,22},{7,3},{8,24},{9,13},... | collective-permute-start | bytes 1548296 | tf_op jit(solution)/shard_map/ppermute | solution.py:51
  8.2 15.4 %collective-permute-start.3 = (bf16[224,1152]{1,0:T(8,128)(2,1)S(1)}, bf16[224,1152]{1,0:T(8,128)(2,1)}, u32[]{:S(2)}, u32[]{:S(2)}) collective-permute-start(bf16[224,1152]{1,0:T(8,128)(2,1)S(1)} %get-tuple-element.26), channel_id=1, source_target_pairs={{0,8},{1,3},{2,10},{3,5},{4,12},{5,7},{6,14},{7,1},{8,16},{9,11},{... | collective-permute-start | bytes 1548296 | tf_op jit(solution)/shard_map/ppermute | solution.py:51
  19.6 11.0 %collective-permute-start.11 = (bf16[56,1792]{1,0:T(8,128)(2,1)S(1)}, bf16[56,1792]{1,0:T(8,128)(2,1)S(1)}, u32[]{:S(2)}, u32[]{:S(2)}) collective-permute-start(bf16[56,1792]{1,0:T(8,128)(2,1)S(1)} %constant_dynamic-slice_fusion), channel_id=1, source_target_pairs={{0,1},{1,0},{2,3},{3,2},{4,5},{5,4},{6,7},{7,6},{8,9},{9,8},{10,11... | collective-permute-start | bytes 602120 | tf_op jit(solution)/shard_map/ppermute | solution.py:47
  26.6 50.8 %collective-permute-start.6 = (bf16[4,224,1152]{2,1,0:T(8,128)(2,1)}, bf16[4,224,1152]{2,1,0:T(8,128)(2,1)}, u32[]{:S(2)}, u32[]{:S(2)}) collective-permute-start(bf16[4,224,1152]{2,1,0:T(8,128)(2,1)} %pad_maximum_fusion.t), channel_id=1, source_target_pairs={{0,2},{1,9},{2,4},{3,11},{4,6},{5,13},{6,0},{7,15},{8,10},{9,17},{... | collective-permute-start | bytes 6193160 | tf_op jit(solution)/shard_map/ppermute | solution.py:57
  28.5 50.3 %collective-permute-start.7 = (bf16[4,224,1152]{2,1,0:T(8,128)(2,1)}, bf16[4,224,1152]{2,1,0:T(8,128)(2,1)}, u32[]{:S(2)}, u32[]{:S(2)}) collective-permute-start(bf16[4,224,1152]{2,1,0:T(8,128)(2,1)} %pad_maximum_fusion.t), channel_id=1, source_target_pairs={{0,6},{1,25},{2,0},{3,27},{4,2},{5,29},{6,4},{7,31},{8,14},{9,1},{... | collective-permute-start | bytes 6193160 | tf_op jit(solution)/shard_map/ppermute | solution.py:57
  37.7 7.3 %collective-permute-start.24 = (bf16[112,768]{1,0:T(8,128)(2,1)S(1)}, bf16[112,768]{1,0:T(8,128)(2,1)S(1)}, u32[]{:S(2)}, u32[]{:S(2)}) collective-permute-start(bf16[112,768]{1,0:T(8,128)(2,1)S(1)} %pad_maximum_fusion.9), channel_id=1, source_target_pairs={{0,24},{1,7},{2,26},{3,1},{4,28},{5,3},{6,30},{7,5},{8,0},{9,15},{... | collective-permute-start | bytes 516104 | tf_op jit(solution)/shard_map/ppermute | solution.py:51
  41.7 8.8 %collective-permute-start.23 = (bf16[112,768]{1,0:T(8,128)(2,1)S(1)}, bf16[112,768]{1,0:T(8,128)(2,1)S(1)}, u32[]{:S(2)}, u32[]{:S(2)}) collective-permute-start(bf16[112,768]{1,0:T(8,128)(2,1)S(1)} %pad_maximum_fusion.9), channel_id=1, source_target_pairs={{0,16},{1,5},{2,18},{3,7},{4,20},{5,1},{6,22},{7,3},{8,24},{9,13},... | collective-permute-start | bytes 516104 | tf_op jit(solution)/shard_map/ppermute | solution.py:51
  45.1 16.4 %collective-permute-start.17 = (bf16[4,112,256]{2,1,0:T(8,128)(2,1)S(1)}, bf16[4,112,256]{2,1,0:T(8,128)(2,1)S(1)}, u32[]{:S(2)}, u32[]{:S(2)}) collective-permute-start(bf16[4,112,256]{2,1,0:T(8,128)(2,1)S(1)} %get-tuple-element.35), channel_id=1, source_target_pairs={{0,6},{1,25},{2,0},{3,27},{4,2},{5,29},{6,4},{7,31},{8,14},{9,1},{... | collective-permute-start | bytes 688136 | tf_op jit(solution)/shard_map/ppermute | solution.py:57
  50.5 7.1 %collective-permute-start.22 = (bf16[112,768]{1,0:T(8,128)(2,1)S(1)}, bf16[112,768]{1,0:T(8,128)(2,1)S(1)}, u32[]{:S(2)}, u32[]{:S(2)}) collective-permute-start(bf16[112,768]{1,0:T(8,128)(2,1)S(1)} %pad_maximum_fusion.9), channel_id=1, source_target_pairs={{0,8},{1,3},{2,10},{3,5},{4,12},{5,7},{6,14},{7,1},{8,16},{9,11},{... | collective-permute-start | bytes 516104 | tf_op jit(solution)/shard_map/ppermute | solution.py:51
  57.6 7.5 %collective-permute-start.16 = (bf16[4,112,256]{2,1,0:T(8,128)(2,1)S(1)}, bf16[4,112,256]{2,1,0:T(8,128)(2,1)S(1)}, u32[]{:S(2)}, u32[]{:S(2)}) collective-permute-start(bf16[4,112,256]{2,1,0:T(8,128)(2,1)S(1)} %get-tuple-element.35), channel_id=1, source_target_pairs={{0,4},{1,17},{2,6},{3,19},{4,0},{5,21},{6,2},{7,23},{8,12},{9,25},... | collective-permute-start | bytes 688136 | tf_op jit(solution)/shard_map/ppermute | solution.py:57
  61.5 9.4 %collective-permute-start.15 = (bf16[4,112,256]{2,1,0:T(8,128)(2,1)S(1)}, bf16[4,112,256]{2,1,0:T(8,128)(2,1)S(1)}, u32[]{:S(2)}, u32[]{:S(2)}) collective-permute-start(bf16[4,112,256]{2,1,0:T(8,128)(2,1)S(1)} %get-tuple-element.35), channel_id=1, source_target_pairs={{0,2},{1,9},{2,4},{3,11},{4,6},{5,13},{6,0},{7,15},{8,10},{9,17},{... | collective-permute-start | bytes 688136 | tf_op jit(solution)/shard_map/ppermute | solution.py:57
  65.1 49.1 %collective-permute-start.25 = (bf16[4,112,768]{2,1,0:T(8,128)(2,1)S(1)}, bf16[4,112,768]{2,1,0:T(8,128)(2,1)S(1)}, u32[]{:S(2)}, u32[]{:S(2)}) collective-permute-start(bf16[4,112,768]{2,1,0:T(8,128)(2,1)S(1)} %pad_maximum_fusion.3.rt), channel_id=1, source_target_pairs={{0,2},{1,9},{2,4},{3,11},{4,6},{5,13},{6,0},{7,15},{8,10},{9,17},{... | collective-permute-start | bytes 2064392 | tf_op jit(solution)/shard_map/ppermute | solution.py:57
  72.1 37.1 %collective-permute-start.18 = (bf16[4,4,112,256]{3,2,1,0:T(8,128)(2,1)S(1)}, bf16[4,4,112,256]{3,2,1,0:T(8,128)(2,1)S(1)}, u32[]{:S(2)}, u32[]{:S(2)}) collective-permute-start(bf16[4,4,112,256]{3,2,1,0:T(8,128)(2,1)S(1)} %pad_maximum_fusion.2.w4), channel_id=1, source_target_pairs={{0,32},{32,64},{64,96},{96,0},{1,33},{33,65},{65,97},{97,1},{2,34}... | collective-permute-start | bytes 2752520 | tf_op jit(solution)/shard_map/ppermute | solution.py:63
  73.7 36.7 %collective-permute-start.19 = (bf16[4,4,112,256]{3,2,1,0:T(8,128)(2,1)S(1)}, bf16[4,4,112,256]{3,2,1,0:T(8,128)(2,1)S(1)}, u32[]{:S(2)}, u32[]{:S(2)}) collective-permute-start(bf16[4,4,112,256]{3,2,1,0:T(8,128)(2,1)S(1)} %pad_maximum_fusion.2.w4), channel_id=1, source_target_pairs={{0,96},{32,0},{64,32},{96,64},{1,97},{33,1},{65,33},{97,65},{2,98}... | collective-permute-start | bytes 2752520 | tf_op jit(solution)/shard_map/ppermute | solution.py:63
  78.7 15.9 %collective-permute-start.8 = (bf16[2,224,1152]{2,1,0:T(8,128)(2,1)S(1)}, bf16[2,224,1152]{2,1,0:T(8,128)(2,1)S(1)}, u32[]{:S(2)}, u32[]{:S(2)}) collective-permute-start(bf16[2,224,1152]{2,1,0:T(8,128)(2,1)S(1)} %slice.79), channel_id=1, source_target_pairs={{0,2},{1,9},{2,4},{3,11},{4,6},{5,13},{6,0},{7,15},{8,10},{9,17},{... | collective-permute-start | bytes 3096584 | tf_op jit(solution)/shard_map/ppermute | solution.py:57
  80.1 15.4 %collective-permute-start.9 = (bf16[2,224,1152]{2,1,0:T(8,128)(2,1)S(1)}, bf16[2,224,1152]{2,1,0:T(8,128)(2,1)S(1)}, u32[]{:S(2)}, u32[]{:S(2)}) collective-permute-start(bf16[2,224,1152]{2,1,0:T(8,128)(2,1)S(1)} %slice.80), channel_id=1, source_target_pairs={{0,6},{1,25},{2,0},{3,27},{4,2},{5,29},{6,4},{7,31},{8,14},{9,1},{... | collective-permute-start | bytes 3096584 | tf_op jit(solution)/shard_map/ppermute | solution.py:57
  94.6 21.5 %collective-permute-start.26 = (bf16[4,112,768]{2,1,0:T(8,128)(2,1)S(1)}, bf16[4,112,768]{2,1,0:T(8,128)(2,1)S(1)}, u32[]{:S(2)}, u32[]{:S(2)}) collective-permute-start(bf16[4,112,768]{2,1,0:T(8,128)(2,1)S(1)} %pad_maximum_fusion.3.rt), channel_id=1, source_target_pairs={{0,6},{1,25},{2,0},{3,27},{4,2},{5,29},{6,4},{7,31},{8,14},{9,1},{... | collective-permute-start | bytes 2064392 | tf_op jit(solution)/shard_map/ppermute | solution.py:57
  109.1 15.7 %collective-permute-start.10 = (bf16[512,896]{1,0:T(8,128)(2,1)}, bf16[512,896]{1,0:T(8,128)(2,1)}, u32[]{:S(2)}, u32[]{:S(2)}) collective-permute-start(bf16[512,896]{1,0:T(8,128)(2,1)} %shard_map.131.att), channel_id=1, source_target_pairs={{0,1},{1,0},{2,3},{3,2},{4,5},{5,4},{6,7},{7,6},{8,9},{9,8},{10,11... | collective-permute-start | bytes 2752520 | tf_op jit(solution)/shard_map/ppermute | solution.py:47
  110.1 14.7 %collective-permute-start.20 = (bf16[2,4,112,256]{3,2,1,0:T(8,128)(2,1)}, bf16[2,4,112,256]{3,2,1,0:T(8,128)(2,1)}, u32[]{:S(2)}, u32[]{:S(2)}) collective-permute-start(bf16[2,4,112,256]{3,2,1,0:T(8,128)(2,1)} %slice.81), channel_id=1, source_target_pairs={{0,32},{32,64},{64,96},{96,0},{1,33},{33,65},{65,97},{97,1},{2,34}... | collective-permute-start | bytes 1376264 | tf_op jit(solution)/shard_map/ppermute | solution.py:63
  111.3 13.5 %collective-permute-start.21 = (bf16[2,4,112,256]{3,2,1,0:T(8,128)(2,1)}, bf16[2,4,112,256]{3,2,1,0:T(8,128)(2,1)}, u32[]{:S(2)}, u32[]{:S(2)}) collective-permute-start(bf16[2,4,112,256]{3,2,1,0:T(8,128)(2,1)} %slice.82), channel_id=1, source_target_pairs={{0,96},{32,0},{64,32},{96,64},{1,97},{33,1},{65,33},{97,65},{2,98}... | collective-permute-start | bytes 1376264 | tf_op jit(solution)/shard_map/ppermute | solution.py:63
  115.0 9.2 %collective-permute-start.27 = (bf16[2,112,768]{2,1,0:T(8,128)(2,1)}, bf16[2,112,768]{2,1,0:T(8,128)(2,1)}, u32[]{:S(2)}, u32[]{:S(2)}) collective-permute-start(bf16[2,112,768]{2,1,0:T(8,128)(2,1)} %slice.83), channel_id=1, source_target_pairs={{0,2},{1,9},{2,4},{3,11},{4,6},{5,13},{6,0},{7,15},{8,10},{9,17},{... | collective-permute-start | bytes 1032200 | tf_op jit(solution)/shard_map/ppermute | solution.py:57
  117.1 7.7 %collective-permute-start.28 = (bf16[2,112,768]{2,1,0:T(8,128)(2,1)}, bf16[2,112,768]{2,1,0:T(8,128)(2,1)}, u32[]{:S(2)}, u32[]{:S(2)}) collective-permute-start(bf16[2,112,768]{2,1,0:T(8,128)(2,1)} %slice.84), channel_id=1, source_target_pairs={{0,6},{1,25},{2,0},{3,27},{4,2},{5,29},{6,4},{7,31},{8,14},{9,1},{... | collective-permute-start | bytes 1032200 | tf_op jit(solution)/shard_map/ppermute | solution.py:57
  148.0 76.6 %all-to-all-start = ((bf16[128,8,256]{2,1,0:T(8,128)(2,1)}), bf16[128,8,256]{2,1,0:T(8,128)(2,1)S(1)}, u32[]{:S(2)}, u32[]{:S(2)}) async-start(bf16[128,8,256]{2,1,0:T(8,128)(2,1)} %bitcast.34), calls=%async_computation | async-start | bytes 1048576 | tf_op jit(solution)/shard_map/all_to_all | solution.py:469
  233.5 7.7 %collective-permute-start.34 = (bf16[4,256,128]{2,1,0:T(8,128)(2,1)S(1)}, bf16[4,256,128]{2,1,0:T(8,128)(2,1)S(1)}, u32[]{:S(2)}, u32[]{:S(2)}) collective-permute-start(bf16[4,256,128]{2,1,0:T(8,128)(2,1)S(1)} %pad_maximum_fusion.5.t), channel_id=1, source_target_pairs={{0,2},{1,9},{2,4},{3,11},{4,6},{5,13},{6,0},{7,15},{8,10},{9,17},{... | collective-permute-start | bytes 786440 | tf_op jit(solution)/shard_map/ppermute | solution.py:57
  234.6 9.7 %collective-permute-start.35 = (bf16[4,256,128]{2,1,0:T(8,128)(2,1)S(1)}, bf16[4,256,128]{2,1,0:T(8,128)(2,1)S(1)}, u32[]{:S(2)}, u32[]{:S(2)}) collective-permute-start(bf16[4,256,128]{2,1,0:T(8,128)(2,1)S(1)} %pad_maximum_fusion.5.t), channel_id=1, source_target_pairs={{0,4},{1,17},{2,6},{3,19},{4,0},{5,21},{6,2},{7,23},{8,12},{9,25},... | collective-permute-start | bytes 786440 | tf_op jit(solution)/shard_map/ppermute | solution.py:57
  237.2 7.7 %collective-permute-start.36 = (bf16[4,256,128]{2,1,0:T(8,128)(2,1)S(1)}, bf16[4,256,128]{2,1,0:T(8,128)(2,1)S(1)}, u32[]{:S(2)}, u32[]{:S(2)}) collective-permute-start(bf16[4,256,128]{2,1,0:T(8,128)(2,1)S(1)} %pad_maximum_fusion.5.t), channel_id=1, source_target_pairs={{0,6},{1,25},{2,0},{3,27},{4,2},{5,29},{6,4},{7,31},{8,14},{9,1},{... | collective-permute-start | bytes 786440 | tf_op jit(solution)/shard_map/ppermute | solution.py:57
  238.6 6.5 %collective-permute-start.37 = (bf16[4,256,128]{2,1,0:T(8,128)(2,1)S(1)}, bf16[4,256,128]{2,1,0:T(8,128)(2,1)S(1)}, u32[]{:S(2)}, u32[]{:S(2)}) collective-permute-start(bf16[4,256,128]{2,1,0:T(8,128)(2,1)S(1)} %pad_maximum_fusion.5.t), channel_id=1, source_target_pairs={{0,1},{1,0},{2,3},{3,2},{4,5},{5,4},{6,7},{7,6},{8,9},{9,8},{10,11... | collective-permute-start | bytes 786440 | tf_op jit(solution)/shard_map/ppermute | solution.py:47
  261.0 7.6 %collective-permute-start.43 = (bf16[4,8,3584]{2,1,0:T(8,128)(2,1)S(1)}, bf16[4,8,3584]{2,1,0:T(8,128)(2,1)S(1)}, u32[]{:S(2)}, u32[]{:S(2)}) collective-permute-start(bf16[4,8,3584]{2,1,0:T(8,128)(2,1)S(1)} %get-tuple-element.20), channel_id=1, source_target_pairs={{0,16},{1,5},{2,18},{3,7},{4,20},{5,1},{6,22},{7,3},{8,24},{9,13},... | collective-permute-start | bytes 688136 | tf_op jit(solution)/shard_map/ppermute | solution.py:51
  261.9 9.1 %collective-permute-start.42 = (bf16[4,8,3584]{2,1,0:T(8,128)(2,1)S(1)}, bf16[4,8,3584]{2,1,0:T(8,128)(2,1)S(1)}, u32[]{:S(2)}, u32[]{:S(2)}) collective-permute-start(bf16[4,8,3584]{2,1,0:T(8,128)(2,1)S(1)} %get-tuple-element.18), channel_id=1, source_target_pairs={{0,8},{1,3},{2,10},{3,5},{4,12},{5,7},{6,14},{7,1},{8,16},{9,11},{... | collective-permute-start | bytes 688136 | tf_op jit(solution)/shard_map/ppermute | solution.py:51
  (41 other events, 319.7 us)

commit v2 on v1

--- a/solution.py
+++ b/solution.py
@@ -11,7 +11,7 @@
 HD = 128
 REPORTS = 16
 SIDE = 4
-WY = 256
+WY = 384
 BF = jnp.bfloat16
 F32 = jnp.float32
 MIB = 1 << 20
@@ -59,14 +59,6 @@
     )
 
 
-def move_y(v, k):
-    return lax.ppermute(v, "grp", [(i, (i + k) % SIDE) for i in range(SIDE)])
-
-
-def after(v, *others):
-    return lax.optimization_barrier((v,) + others)[0]
-
-
 def rms_scale(values, gain):
     wide = values.astype(F32)
     return wide * lax.rsqrt(jnp.mean(wide * wide, axis=-1, keepdims=True) + 1e-06) * gain
@@ -87,36 +79,83 @@
     return started
 
 
-def gather_line(first, move):
-    one = move(first, 1)
-    three = move(first, -1)
-    half = first.shape[0] // 2
-    two_low = move(one[:half], 1)
-    two_high = move(three[half:], -1)
-    return one, three, two_low, two_high
-
-
-def qkv_kernel(order, xo, xt, seg_col, seg_row, t, s1, s3, s2a, s2b, out, w, qkv, sems):
-    depth = t.shape[1]
+QKV_COLS = 1152
+BLOCK = 256
+
+
+def norm_kernel(tok, gain, out, wide_ref):
+    chunk = 32
+    depth = tok.shape[1] // out.shape[0]
+
+    @pl.loop(0, tok.shape[0] // chunk)
+    def _(i):
+        rows = pl.ds(pl.multiple_of(i * chunk, chunk), chunk)
+        wide = tok[rows, :].astype(F32)
+        scale = lax.rsqrt(jnp.mean(wide * wide, axis=1, keepdims=True) + 1e-06)
+        wide_ref[...] = wide * scale * gain[...]
+        for n in range(out.shape[0]):
+            piece = wide_ref[:, n * depth : (n + 1) * depth]
+            pad = jnp.zeros((chunk, BLOCK - depth), F32)
+            out[n, rows, :] = jnp.concatenate([piece, pad], axis=1).astype(BF)
+
+
+def norm_blocks(tok, gain):
+    count, width = tok.shape
+    chips = SIDE * SIDE
+    return pl.pallas_call(
+        norm_kernel,
+        out_shape=jax.ShapeDtypeStruct((chips, count, BLOCK), BF),
+        in_specs=[vmem()] * 2,
+        out_specs=vmem(),
+        scratch_shapes=[pltpu.VMEM((32, width), F32)],
+        compiler_params=params(24),
+        cost_estimate=pl.CostEstimate(flops=0, bytes_accessed=4 * count * width, transcendentals=0),
+    )(tok, gain)
+
+
+def qkv_load(order, steps, pieces, xo, xt, w, x, sems):
+    cols = w.shape[1]
+    depth = pieces[0].shape[1]
+    tokens = xo.shape[1]
     copies = []
-    for k, piece, lo, n in ((0, t, 0, 4), (1, s1, 0, 4), (3, s3, 0, 4), (2, s2a, 0, 2), (2, s2b, 2, 2)):
-        for j in range(n):
-            q = order[k * SIDE + lo + j]
-            rows = pl.ds(pl.multiple_of(q * depth, 16), depth)
-            copies.append((piece.at[j], w.at[rows, :]))
-    for copy in run_copies(copies, sems):
+    for n in range(2 * len(pieces)):
+        piece = pieces[n // 2].at[n % 2, :, pl.ds(0, cols)]
+        copies.append((piece, w.at[pl.ds(n * BLOCK, depth), :]))
+    started = run_copies(copies, sems)
+    for n in range(2 * len(pieces)):
+        q = order[steps[n // SIDE] * SIDE + n % SIDE]
+        x[0:tokens, n * BLOCK : (n + 1) * BLOCK] = xo[q]
+        x[tokens : 2 * tokens, n * BLOCK : (n + 1) * BLOCK] = xt[q]
+        w[n * BLOCK + depth : (n + 1) * BLOCK, :] = jnp.zeros((BLOCK - depth, cols), BF)
+    for copy in started:
         copy.wait()
-    tokens = xo.shape[0]
-    tile = 384
-
-    @pl.loop(0, w.shape[1] // tile)
+
+
+QKV_TILE = 384
+
+
+def qkv_first_kernel(order, xo, xt, *refs):
+    *pieces, part, w, x, sems = refs
+    qkv_load(order, (0, 1, 3), pieces, xo, xt, w, x, sems)
+
+    @pl.loop(0, part.shape[1] // QKV_TILE)
     def _(n):
-        cols = pl.ds(pl.multiple_of(n * tile, 128), tile)
-        weight = w[:, cols]
-        qkv[pl.ds(0, tokens), cols] = jnp.dot(xo[...], weight, preferred_element_type=F32).astype(BF)
-        qkv[pl.ds(tokens, tokens), cols] = jnp.dot(xt[...], weight, preferred_element_type=F32).astype(BF)
+        there = pl.ds(pl.multiple_of(n * QKV_TILE, 128), QKV_TILE)
+        part[:, there] = jnp.dot(x[...], w[:, there], preferred_element_type=F32)
+
+
+def qkv_last_kernel(order, xo, xt, seg_col, seg_row, part, *refs):
+    *pieces, out, w, x, qkv, sems = refs
+    qkv_load(order, (2,), pieces, xo, xt, w, x, sems)
+
+    @pl.loop(0, part.shape[1] // QKV_TILE)
+    def _(n):
+        there = pl.ds(pl.multiple_of(n * QKV_TILE, 128), QKV_TILE)
+        last = jnp.dot(x[...], w[:, there], preferred_element_type=F32)
+        qkv[:, there] = (part[:, there] + last).astype(BF)
 
     heads = out.shape[1] // HD
+    tokens = xo.shape[1]
 
     @pl.loop(0, 2)
     def _(b):
@@ -128,93 +167,115 @@
             query = qkv[rows, h * HD : (h + 1) * HD]
             scores = lax.dot_general(
                 query, keys, (((1,), (1,)), ((), ())), preferred_element_type=F32
-            ) * (1.0 / math.sqrt(HD))
+            ) * (math.log2(math.e) / math.sqrt(HD))
             scores = jnp.where(same, scores, -1e30)
             top = jnp.max(scores, axis=1, keepdims=True)
-            e = jnp.exp(scores - top)
-            weights = (e / jnp.sum(e, axis=1, keepdims=True)).astype(BF)
+            e = jnp.exp2(scores - top)
+            weights = (e * (1.0 / jnp.sum(e, axis=1, keepdims=True))).astype(BF)
             out[rows, h * HD : (h + 1) * HD] = jnp.dot(
                 weights, values, preferred_element_type=F32
             ).astype(BF)
 
 
-def page_qkv(order, x_own, x_other, seg_col, seg_row, pieces):
-    tokens, width = x_own.shape
-    cols = pieces[0].shape[2]
+def qkv_first(order, x_own, x_other, pieces, cols):
+    tokens = x_own.shape[1]
     return pl.pallas_call(
-        qkv_kernel,
-        out_shape=jax.ShapeDtypeStruct((2 * tokens, cols - 2 * HD), BF),
-        in_specs=[smem()] + [vmem()] * 4 + [anym()] * 5,
+        qkv_first_kernel,
+        out_shape=jax.ShapeDtypeStruct((2 * tokens, cols), F32),
+        in_specs=[smem()] + [vmem()] * 2 + [anym()] * 6,
         out_specs=vmem(),
         scratch_shapes=[
-            pltpu.VMEM((width, cols), BF),
-            pltpu.VMEM((2 * tokens, cols), BF),
-            pltpu.SemaphoreType.DMA((16,)),
+            pltpu.VMEM((12 * BLOCK, cols), BF),
+            pltpu.VMEM((2 * tokens, 12 * BLOCK), BF),
+            pltpu.SemaphoreType.DMA((12,)),
         ],
         compiler_params=params(40),
         cost_estimate=pl.CostEstimate(
-            flops=2 * 2 * tokens * width * cols, bytes_accessed=2 * width * cols, transcendentals=0
+            flops=4 * tokens * 12 * BLOCK * cols, bytes_accessed=24 * BLOCK * cols, transcendentals=0
         ),
-    )(order, x_own, x_other, seg_col, seg_row, *pieces)
+    )(order, x_own, x_other, *pieces)
+
+
+def qkv_last(order, x_own, x_other, seg_col, seg_row, part, pieces):
+    tokens = x_own.shape[1]
+    cols = part.shape[1]
+    return pl.pallas_call(
+        qkv_last_kernel,
+        out_shape=jax.ShapeDtypeStruct((2 * tokens, cols - 2 * HD), BF),
+        in_specs=[smem()] + [vmem()] * 5 + [anym()] * 2,
+        out_specs=vmem(),
+        scratch_shapes=[
+            pltpu.VMEM((4 * BLOCK, cols), BF),
+            pltpu.VMEM((2 * tokens, 4 * BLOCK), BF),
+            pltpu.VMEM((2 * tokens, cols), BF),
+            pltpu.SemaphoreType.DMA((4,)),
+        ],
+        compiler_params=params(40),
+        cost_estimate=pl.CostEstimate(
+            flops=4 * tokens * 8 * BLOCK * cols, bytes_accessed=24 * BLOCK * cols, transcendentals=0
+        ),
+    )(order, x_own, x_other, seg_col, seg_row, part, *pieces)
 
 
 def out_kernel(
-    order, pos, tok_own, tok_other, att, att_in, member, member_t, inv, inv_t,
-    w4, u1, u3, u2a, u2b, rt, r1, r3, r2a, r2b,
-    st_own, st_other, pool_own, pool_other, w, full, sems,
+    order, pos, tok_own, tok_other, att, att_in, member, member_t, inv, inv_t, w_all, *refs
 ):
-    depth = w4.shape[2]
-    wy = w4.shape[3]
+    pieces, refs = refs[: 2 * SIDE], refs[2 * SIDE :]
+    st_own, st_other, pool_own, pool_other, w, rest, full, sems = refs
     core = pos[0]
-    grp = pos[1]
+    depth, wy = w_all.shape[2:]
+    tile = rest.shape[1] // 2
+    chips = SIDE * SIDE
     copies = []
-    for i, piece, lo, n in ((0, w4, 0, 4), (1, u1, 0, 4), (3, u3, 0, 4), (2, u2a, 0, 2), (2, u2b, 2, 2)):
-        block = lax.rem(grp + (SIDE - i), SIDE)
-        cols = pl.ds(pl.multiple_of(block * wy, 128), wy)
-        for k in range(n):
-            for j in range(SIDE):
-                rows = pl.ds(pl.multiple_of(order[(lo + k) * SIDE + j] * depth, 16), depth)
-                copies.append((piece.at[k, j], w.at[rows, cols]))
-    wr = rt.shape[2]
-    for k, piece, lo, n in ((0, rt, 0, 4), (1, r1, 0, 4), (3, r3, 0, 4), (2, r2a, 0, 2), (2, r2b, 2, 2)):
-        for j in range(n):
-            rows = pl.ds(pl.multiple_of(order[k * SIDE + lo + j] * depth, 16), depth)
-            copies.append((piece.at[j], w.at[rows, pl.ds(SIDE * wy, wr)]))
+    rows = [pl.ds(pl.multiple_of(order[n] * depth, 16), depth) for n in range(chips)]
+    for i in range(SIDE):
+        for n in range(chips):
+            copies.append((w_all.at[i, n], w.at[i, rows[n], :]))
+    for n in range(chips):
+        for t in range(2):
+            copies.append(
+                (
+                    pieces[n // 2].at[n % 2, pl.ds(t * depth, depth), pl.ds(QKV_COLS, tile)],
+                    rest.at[rows[n], pl.ds(t * tile, tile)],
+                )
+            )
     started = run_copies(copies, sems)
     tokens = tok_own.shape[0]
     half = att.shape[1]
     mine = pl.ds(pl.multiple_of(core * half, 128), half)
     theirs = pl.ds(pl.multiple_of((1 - core) * half, 128), half)
-    full[0:tokens, mine] = att[0:tokens, :]
-    full[tokens : 2 * tokens, mine] = att[tokens : 2 * tokens, :]
+    full[:, mine] = att[...]
     full[0:tokens, theirs] = att_in[tokens : 2 * tokens, :]
     full[tokens : 2 * tokens, theirs] = att_in[0:tokens, :]
-    for copy in started:
-        copy.wait()
-    tile = 256
-    width = w.shape[1]
-
-    @pl.loop(0, width // tile)
-    def _(n):
-        cols = pl.ds(pl.multiple_of(n * tile, 128), tile)
-        there = pl.ds(pl.multiple_of(core * width + n * tile, 128), tile)
-        weight = w[:, cols]
-        for rows, tok, st, mem, ratio, pool in (
+    width = st_own.shape[1]
+
+    def columns(lo, n, weight):
+        cols = slice(lo, lo + n)
+        there = pl.ds(pl.multiple_of(core * width + lo, 128), n)
+        projected = jnp.dot(full[...], weight, preferred_element_type=F32)
+        for first, tok, st, mem, ratio, pool in (
             (0, tok_own, st_own, member, inv, pool_own),
             (tokens, tok_other, st_other, member_t, inv_t, pool_other),
         ):
-            projected = jnp.dot(full[rows : rows + tokens, :], weight, preferred_element_type=F32)
-            states = (tok[:, there].astype(F32) + projected).astype(BF)
+            states = (tok[:, there].astype(F32) + projected[first : first + tokens]).astype(BF)
             st[:, cols] = states
             pool[:, cols] = (
                 jnp.dot(mem[...], states, preferred_element_type=F32) / ratio[...]
             ).astype(BF)
 
-
-def page_out(order, pos, tok_own, tok_other, att, att_in, members, lens, y_pieces, r_pieces):
-    tokens = tok_own.shape[0]
-    depth = y_pieces[0].shape[2]
-    width = SIDE * y_pieces[0].shape[3] + r_pieces[0].shape[2]
+    for i in range(SIDE):
+        for copy in started[i * chips : (i + 1) * chips]:
+            copy.wait()
+        columns(i * wy, wy, w[i])
+    for copy in started[SIDE * chips :]:
+        copy.wait()
+    columns(SIDE * wy, 2 * tile, rest[...])
+
+
+def page_out(order, pos, tok_own, tok_other, att, att_in, members, lens, w_all, pieces):
+    tokens, width = tok_own.shape
+    width = width // 2
+    depth, wy = w_all.shape[2:]
     rows = SIDE * SIDE * depth
     pages = members[0].shape[0]
     st = jax.ShapeDtypeStruct((tokens, width), BF)
@@ -222,45 +283,82 @@
     return pl.pallas_call(
         out_kernel,
         out_shape=(st, st, pool, pool),
-        in_specs=[smem()] * 2 + [vmem()] * 8 + [anym()] * 10,
+        in_specs=[smem()] * 2 + [vmem()] * 8 + [anym()] * 9,
         out_specs=(vmem(),) * 4,
         scratch_shapes=[
-            pltpu.VMEM((rows, width), BF),
+            pltpu.VMEM((SIDE, rows, wy), BF),
+            pltpu.VMEM((rows, width - SIDE * wy), BF),
             pltpu.VMEM((2 * tokens, rows), BF),
-            pltpu.SemaphoreType.DMA((80,)),
+            pltpu.SemaphoreType.DMA((6 * SIDE * SIDE,)),
         ],
         compiler_params=params(40),
         cost_estimate=pl.CostEstimate(
             flops=2 * 2 * tokens * width * rows, bytes_accessed=2 * width * rows, transcendentals=0
         ),
-    )(order, pos, tok_own, tok_other, att, att_in, *members, *lens, *y_pieces, *r_pieces)
-
-
-def doc_kernel(pos, rows, label_col, label_row, out):
+    )(order, pos, tok_own, tok_other, att, att_in, *members, *lens, w_all, *pieces)
+
+
+def block_kernel(vec, label, out):
+    pages, width = vec.shape
+    wide = vec[...].astype(F32)
+    scale = lax.rsqrt(jnp.mean(wide * wide, axis=1, keepdims=True) + 1e-06)
+    high = scale.astype(BF)
+    low = (scale - high.astype(F32)).astype(BF)
+    lane = lax.broadcasted_iota(jnp.int32, (pages, HD), 1)
+    side = jnp.where(lane == 0, high.astype(F32), jnp.where(lane == 1, low.astype(F32), 0.0))
+    side = jnp.where(lane == 2, label[...].astype(F32), side).astype(BF)
+    for h in range(width // HD):
+        out[h, :, 0:HD] = vec[:, h * HD : (h + 1) * HD]
+        out[h, :, HD : 2 * HD] = side
+    for h in range(width // HD, out.shape[0]):
+        out[h] = jnp.zeros((pages, 2 * HD), BF)
+
+
+def page_blocks(vectors, labels, slots):
+    return pl.pallas_call(
+        block_kernel,
+        out_shape=jax.ShapeDtypeStruct((slots, vectors.shape[0], 2 * HD), BF),
+        in_specs=[vmem()] * 2,
+        out_specs=vmem(),
+        compiler_params=params(16),
+    )(vectors, labels)
+
+
+def doc_kernel(pos, rows, gain, out, keys_ref):
     count = out.shape[0]
-    mine = pl.ds(pl.multiple_of(pos[1] * count, count), count)
-    keys = rows[:, HD : 2 * HD]
-    query = rows[mine, HD : 2 * HD]
+    every = rows.shape[0]
+    start = pl.multiple_of(pos[1] * count, count)
+    mine = pl.ds(start, count)
+    side = rows[:, HD : 2 * HD].astype(F32)
+    scale = side[:, 0:1] + side[:, 1:2]
+    keys = (rows[:, 0:HD].astype(F32) * scale * gain[...]).astype(BF)
+    keys_ref[...] = keys
+    query = keys_ref[mine, :]
+    pick = (lax.broadcasted_iota(jnp.int32, (8, HD), 1) == 2).astype(BF)
+    label_row = lax.dot_general(
+        pick, rows[:, HD : 2 * HD], (((1,), (1,)), ((), ())), preferred_element_type=F32
+    )[0:1, :]
+    label_col = rows[mine, HD : 2 * HD].astype(F32)[:, 2:3]
     scores = lax.dot_general(
         query, keys, (((1,), (1,)), ((), ())), preferred_element_type=F32
-    ) * (1.0 / HD)
-    scores = jnp.where(label_col[...] == label_row[...], scores, -1e30)
+    ) * (math.log2(math.e) / HD)
+    scores = jnp.where(label_col == label_row, scores, -1e30)
     top = jnp.max(scores, axis=1, keepdims=True)
-    e = jnp.exp(scores - top)
-    weights = (e / jnp.sum(e, axis=1, keepdims=True)).astype(BF)
+    e = jnp.exp2(scores - top)
+    weights = (e * (1.0 / jnp.sum(e, axis=1, keepdims=True))).astype(BF)
     context = jnp.dot(weights, keys, preferred_element_type=F32)
     out[...] = (rows[mine, 0:HD].astype(F32) + context).astype(BF)
 
 
-def doc_attention(pos, rows, label_col, label_row):
-    count = label_col.shape[0]
+def doc_attention(pos, rows, gain, count):
     return pl.pallas_call(
         doc_kernel,
         out_shape=jax.ShapeDtypeStruct((count, HD), BF),
-        in_specs=[smem()] + [vmem()] * 3,
+        in_specs=[smem()] + [vmem()] * 2,
         out_specs=vmem(),
+        scratch_shapes=[pltpu.VMEM((rows.shape[0], HD), BF)],
         compiler_params=params(24),
-    )(pos, rows, label_col, label_row)
+    )(pos, rows, gain)
 
 
 def ffn_kernel(
@@ -408,47 +506,62 @@
 
     wo = pair_up(out_cols(core), swap(out_cols(1 - core)))
     wq = pair_up(qkv_cols(core), swap(qkv_cols(1 - core)))
+    wo_y = lax.dynamic_slice_in_dim(wo, grp * WY, WY, 1)
+    tile = (out_half - SIDE * WY) // 2
+    wo_r = wo[:, SIDE * WY :]
+    wq = jnp.concatenate([wq, jnp.concatenate([wo_r[:, :tile], wo_r[:, tile:]], axis=0)], axis=1)
+
     tok_other = swap(tokens)
     len_other = swap(page_lengths)
-
-    wo_y = lax.dynamic_slice_in_dim(wo, grp * WY, WY, 1)
-    wo_r = wo[:, SIDE * WY :]
-
-    def line_a(v):
-        return jnp.stack([v, move_a(v, 1), move_a(v, 2), move_a(v, -1)])
-
-    def line_b(t):
-        one = move_b(t, 1)
-        three = move_b(t, -1)
-        return (t, one, three, move_b(one[:2], 1), move_b(three[2:], -1))
-
-    ty = line_a(wo_y)
-    tq = line_a(wq)
-    tr = line_a(wo_r)
-    w4 = jnp.stack([ty, move_b(ty, 1), move_b(ty, 2), move_b(ty, -1)])
-    y1 = move_y(w4, 1)
-    y3 = move_y(w4, -1)
-    y_pieces = (w4, y1, y3, move_y(y1[:2], 1), move_y(y3[2:], -1))
-    q_pieces = line_b(tq)
-    r_pieces = line_b(tr)
-
-    labels = page_group[:, 0] * REPORTS + page_report
-    all_labels = lax.all_gather(labels, ("grp", "page"), axis=0, tiled=True)
-
     gain = attn_gain[None, :]
-    x_own = rms_scale(tokens, gain).astype(BF)
-    x_other = rms_scale(tok_other, gain).astype(BF)
+    x_own = norm_blocks(tokens, gain)
+    x_other = norm_blocks(tok_other, gain)
     seg_own = page_index(page_lengths[0], count)
     seg_other = page_index(len_other[0], count)
     seg_col = jnp.concatenate([seg_own, seg_other])[:, None]
     seg_row = jnp.stack([seg_own, seg_other])[:, None, :]
-    att = page_qkv(order, x_own, x_other, seg_col, seg_row, q_pieces)
-    att_in = swap(att)
     names = jnp.arange(pages, dtype=jnp.int32)[:, None]
     members = tuple((seg[None, :] == names).astype(BF) for seg in (seg_own, seg_other))
     lens = tuple(v[0][:, None].astype(F32) for v in (page_lengths, len_other))
+    slots = 2 * SIDE * SIDE
+    plane = slots * pages
+    labels = page_group * REPORTS + page_report[:, None]
+    head_gain = jnp.pad(doc_gain, (0, slots * HD - width))
+    head_gain = lax.dynamic_slice_in_dim(head_gain, page * HD, HD)[None, :]
+    pick = (
+        jnp.arange(plane, dtype=jnp.int32)[None, :] == page * pages + jnp.arange(pages)[:, None]
+    ).astype(BF)
+    tables = jnp.concatenate([order, dest])
+    tables_t = jnp.concatenate([order_t, dest_t])
+    early = (
+        x_own, x_other, seg_col, seg_row, members, lens, labels, head_gain, pick,
+        tables, tables_t, pos, ffn_gain[None, :],
+    )
+
+    line_y = jnp.stack([wo_y, move_a(wo_y, 1), move_a(wo_y, 2), move_a(wo_y, -1)])
+    line_y, wq = lax.optimization_barrier((line_y, wq))
+    square = (line_y, move_b(line_y, 1), move_b(line_y, 2), move_b(line_y, -1))
+    q1, q3 = move_a(wq, 1), move_a(wq, -1)
+    square, q1, q3 = lax.optimization_barrier((square, q1, q3))
+    wo_all = lax.all_gather(jnp.concatenate(square), "grp", axis=0, tiled=True)
+    wo_all = wo_all.reshape((SIDE, SIDE * SIDE) + wo_y.shape)
+    low = jnp.stack([wq, q1])
+    high = jnp.stack([move_a(wq, 2), q3])
+    up = [move_b(low, 1), move_b(high, 1)]
+    down = [move_b(low, -1), move_b(high, -1)]
+    up[0], early = lax.optimization_barrier((up[0], early))
+    far = [move_b(up[0], 1), move_b(down[1], -1)]
+    pieces = [low, high] + up + far + down
+    (
+        x_own, x_other, seg_col, seg_row, members, lens, labels, head_gain, pick,
+        tables, tables_t, pos, ffn_row,
+    ) = early
+
+    part = qkv_first(tables, x_own, x_other, pieces[:4] + pieces[6:], QKV_COLS)
+    att = qkv_last(tables, x_own, x_other, seg_col, seg_row, part, far)
+    att_in = swap(att)
     st_own, st_other, pool_own, pool_other = page_out(
-        order, pos, tokens, tok_other, att, att_in, members, lens, y_pieces, r_pieces
+        tables, pos, tokens, tok_other, att, att_in, members, lens, wo_all, pieces
     )
 
     def side_by_side(mine, got):
@@ -459,26 +572,16 @@
     vectors = side_by_side(pool_own, swap(pool_other))
     token_states = side_by_side(st_own, swap(st_other))
 
-    keys = rms_scale(vectors, doc_gain).astype(BF)
-    heads = width // HD
-    slots = 2 * SIDE * SIDE
-    blocks = jnp.stack([vectors.reshape(pages, heads, HD), keys.reshape(pages, heads, HD)], axis=2)
-    blocks = blocks.reshape(pages, heads, 2 * HD).transpose(1, 0, 2)
-    blocks = jnp.pad(blocks, ((0, slots - heads), (0, 0), (0, 0)))
+    blocks = page_blocks(vectors, labels, slots)
     blocks = jnp.broadcast_to(blocks[None], (SIDE,) + blocks.shape).reshape(-1, pages, 2 * HD)
     gathered = lax.all_to_all(blocks, ("grp", "page"), split_axis=0, concat_axis=0, tiled=True)
-    plane = slots * pages
-    label_col = lax.dynamic_slice_in_dim(all_labels, grp * plane, plane)[:, None]
-    mixed = doc_attention(pos, gathered.reshape(-1, 2 * HD), label_col, all_labels[None, :])
-
-    line = line_a(mixed)
+    mixed = doc_attention(pos, gathered.reshape(-1, 2 * HD), head_gain, plane)
+
+    line = jnp.stack([mixed, move_a(mixed, 1), move_a(mixed, 2), move_a(mixed, -1)])
     pieces = (line, move_b(line, 1), move_b(line, 2), move_b(line, -1))
     pieces_t = tuple(swap(v) for v in pieces)
-    pick = (
-        jnp.arange(plane, dtype=jnp.int32)[None, :] == page * pages + jnp.arange(pages)[:, None]
-    ).astype(BF)
-    own, other, states = feed_forward_call(
-        order, order_t, dest, dest_t, pos, pieces, pieces_t, ffn_gain[None, :], gate_up_weight, w_down, pick
+    own, other, states = feed_forward(
+        tables, tables_t, pos, pieces, pieces_t, ffn_row, gate_up_weight, w_down, pick
     )
     got = swap(other)
 
@@ -491,12 +594,6 @@
     summed = total(part[0], *(move_b(part[k], k) for k in range(1, SIDE)))
     page_embeddings = (states + summed).astype(BF)
     return (token_states, page_embeddings)
-
-
-def feed_forward_call(order, order_t, dest, dest_t, pos, *rest):
-    tables = jnp.concatenate([order, dest])
-    tables_t = jnp.concatenate([order_t, dest_t])
-    return feed_forward(tables, tables_t, pos, *rest)
 
 
 def solution(mesh):

time: 282 us -> 209 us (0.74)
  blocking collectives: 67.3 us -> 25.3 us
  waiting for transfers between devices: 82.1 us -> 55.4 us
  between operations: 1.1 us -> 14.4 us
  local copies, waits for them, and re-layouts: 20.1 us -> 10.6 us
  starting transfers between devices: 57.8 us -> 49.4 us
  Pallas kernels: 37.5 us -> 44.5 us
  other arithmetic: 15.1 us -> 9.26 us
    unnamed x1 -> x0, blocking collectives: 67.3 us -> none
    all_to_all x0 -> x1, blocking collectives: none -> 25.3 us  [on_device(): lax.all_to_all(blocks, ('grp', 'page'), split_axis=0, concat_axis=0, tile...]
    ppermute x15 -> x12, waiting for transfers between devices: 45 us -> 23 us  [move_a(): lax.ppermute(v, 'page', chip_perm(lambda x, z, c: (x + k, z, c) if c == 0...]
    pallas_call x1 -> x5, Pallas kernels: 13.6 us -> 23.5 us  [the longest x1 8.55 us: qkv_first(): pl.pallas_call(qkv_first_kernel, out_shape=jax.ShapeDtypeStruct((2 * toke...]
    all_to_all x1 -> x0, starting transfers between devices: 8.99 us -> none  [on_device(): lax.all_to_all(blocks, ('grp', 'page'), split_axis=0, concat_axis=0, tile...]
    ppermute x4 -> x0, starting transfers between devices: 6.54 us -> none  [move_y(): return lax.ppermute(v, 'grp', [(i, (i + k) % SIDE) for i in range(SIDE)])]
    slice x6 -> x0, local copies, waits for them, and re-layouts: 5.95 us -> none  [the longest x4 4.22 us: line_b(): return (t, one, three, move_b(one[:2], 1), move_b(three[2:], -1))]
    ppermute x17 -> x15, waiting for transfers between devices: 31.6 us -> 26.4 us  [move_b(): lax.ppermute(v, 'page', chip_perm(lambda x, z, c: (x, z + k, c) if c == 0...]
  transfers between devices with their start and end apart: 49 -> 40, of which waited for: 31 -> 26; matrix products, arithmetic and copies ran while one was open for 8% -> 5% of each run, Pallas kernels for 5% -> 11%
where the time goes in v2:
time: 209 us
  waiting for transfers between devices  55.4 us (27%)
  starting transfers between devices  49.4 us (24%)
  Pallas kernels  44.5 us (21%)
  blocking collectives  25.3 us (12%)
  between operations  14.4 us (7%)
  local copies, waits for them, and re-layouts  10.6 us (5%)
  other arithmetic  9.26 us (4%)
    ppermute x15, starting transfers between devices, move_b(): lax.ppermute(v, 'page', chip_perm(lambda x, z, c: (x, z + k, c) if c == 0...  27.1 us
    ppermute x15, waiting for transfers between devices, move_b(): lax.ppermute(v, 'page', chip_perm(lambda x, z, c: (x, z + k, c) if c == 0...  26.4 us
    all_to_all x1, blocking collectives, on_device(): lax.all_to_all(blocks, ('grp', 'page'), split_axis=0, concat_axis=0, tile...  25.3 us
    ppermute x12, waiting for transfers between devices, move_a(): lax.ppermute(v, 'page', chip_perm(lambda x, z, c: (x + k, z, c) if c == 0...  23 us
    ppermute x12, starting transfers between devices, move_a(): lax.ppermute(v, 'page', chip_perm(lambda x, z, c: (x + k, z, c) if c == 0...  18.8 us
    pallas_call x1, Pallas kernels, page_out(): pl.pallas_call(out_kernel, out_shape=(st, st, pool, pool), in_specs=[smem...  11.2 us
    pallas_call x1, Pallas kernels, qkv_first(): pl.pallas_call(qkv_first_kernel, out_shape=jax.ShapeDtypeStruct((2 * toke...  8.55 us
    pallas_call x1, Pallas kernels, feed_forward(): pl.pallas_call(ffn_kernel, out_shape=(part, part, jax.ShapeDtypeStruct((p...  8.22 us
  transfers between devices with their start and end apart: 40, of which 26 were waited for; matrix products, arithmetic and copies ran while one was open for 5% of the time, Pallas kernels for 11%

profile of v2, /device:TPU:0, one launch (start us, length us, event | category | flops | bytes accessed | tf_op | source)
XLA Modules:
  0.0 208.9 jit_solution(8557353468239844902)
XLA Ops:
  11.8 2.7 %collective-permute-start.2 = (bf16[112,384]{1,0:T(8,128)(2,1)S(1)}, bf16[112,384]{1,0:T(8,128)(2,1)S(1)}, u32[]{:S(2)}, u32[]{:S(2)}) collective-permute-start(bf16[112,384]{1,0:T(8,128)(2,1)S(1)} %fusion.19), channel_id=1, source_target_pairs={{0,16},{1,5},{2,18},{3,7},{4,20},{5,1},{6,22},{7,3},{8,24},{9,13},... | collective-permute-start | bytes 258056 | tf_op jit(solution)/shard_map/ppermute | solution.py:51
  16.2 1.8 collective-permute-done.2
  19.9 2.5 %collective-permute-start.9 = (bf16[224,1280]{1,0:T(8,128)(2,1)S(1)}, bf16[224,1280]{1,0:T(8,128)(2,1)S(1)}, u32[]{:S(2)}, u32[]{:S(2)}) collective-permute-start(bf16[224,1280]{1,0:T(8,128)(2,1)S(1)} %fusion.7), channel_id=1, source_target_pairs={{0,24},{1,7},{2,26},{3,1},{4,28},{5,3},{6,30},{7,5},{8,0},{9,15},{... | collective-permute-start | bytes 1720328 | tf_op jit(solution)/shard_map/ppermute | solution.py:51
  22.4 1.9 collective-permute-start.5
  24.3 3.6 %collective-permute-start.6 = (bf16[4,112,384]{2,1,0:T(8,128)(2,1)S(1)}, bf16[4,112,384]{2,1,0:T(8,128)(2,1)S(1)}, u32[]{:S(2)}, u32[]{:S(2)}) collective-permute-start(bf16[4,112,384]{2,1,0:T(8,128)(2,1)S(1)} %pad_maximum_fusion.4), channel_id=1, source_target_pairs={{0,4},{1,17},{2,6},{3,19},{4,0},{5,21},{6,2},{7,23},{8,12},{9,25},... | collective-permute-start | bytes 1032200 | tf_op jit(solution)/shard_map/ppermute | solution.py:57
  28.9 3.8 %collective-permute-done.5 = bf16[4,112,384]{2,1,0:T(8,128)(2,1)S(1)} collective-permute-done((bf16[4,112,384]{2,1,0:T(8,128)(2,1)S(1)}, bf16[4,112,384]{2,1,0:T(8,128)(2,1)S(1)}, u32[]{:S(2)}, u32[]{:S(2)}) %collective-permute-start.5) | collective-permute-done | bytes 344096 | tf_op jit(solution)/shard_map/ppermute | solution.py:57
  32.7 4.1 %collective-permute-done.6 = bf16[4,112,384]{2,1,0:T(8,128)(2,1)S(1)} collective-permute-done((bf16[4,112,384]{2,1,0:T(8,128)(2,1)S(1)}, bf16[4,112,384]{2,1,0:T(8,128)(2,1)S(1)}, u32[]{:S(2)}, u32[]{:S(2)}) %collective-permute-start.6) | collective-permute-done | bytes 344096 | tf_op jit(solution)/shard_map/ppermute | solution.py:57
  40.5 2.1 collective-permute-start.13
  42.9 1.8 collective-permute-start.10
  44.7 10.1 %collective-permute-done.13 = bf16[224,1280]{1,0:T(8,128)(2,1)} collective-permute-done((bf16[224,1280]{1,0:T(8,128)(2,1)S(1)}, bf16[224,1280]{1,0:T(8,128)(2,1)}, u32[]{:S(2)}, u32[]{:S(2)}) %collective-permute-start.13) | collective-permute-done | bytes 573472 | tf_op jit(solution)/shard_map/ppermute | solution.py:51
  54.8 2.2 %pad_maximum_fusion.3.refs_1_ = bf16[2,224,1280]{2,1,0:T(8,128)(2,1)} fusion(bf16[1,224,1280]{2,1,0:T(8,128)(2,1)S(1)} %bitcast.62, bf16[1,224,1280]{2,1,0:T(8,128)(2,1)} %bitcast.17), kind=kLoop, calls=%fused_computation.8 | loop fusion | flops 573440 | bytes 2293760 | tf_op jit(solution)/shard_map/stack | solution.py:549
  57.0 4.5 %collective-permute-start.16 = (bf16[2,224,1280]{2,1,0:T(8,128)(2,1)}, bf16[2,224,1280]{2,1,0:T(8,128)(2,1)}, u32[]{:S(2)}, u32[]{:S(2)}) collective-permute-start(bf16[2,224,1280]{2,1,0:T(8,128)(2,1)} %pad_maximum_fusion.3.refs_1_), channel_id=1, source_target_pairs={{0,6},{1,25},{2,0},{3,27},{4,2},{5,29},{6,4},{7,31},{8,14},{9,1},{... | collective-permute-start | bytes 3440648 | tf_op jit(solution)/shard_map/ppermute | solution.py:57
  62.5 3.8 %shard_map.131.xo = bf16[16,256,256]{2,1,0:T(8,128)(2,1)S(1)} custom-call(bf16[256,3584]{1,0:T(8,128)(2,1)} %tok_own.1, f32[1,3584]{1,0:T(1,128)S(1)} %broadcast_in_dim.14.gain), custom_call_target="tpu_custom_call" | custom-call | bytes 3670016 | tf_op jit(solution)/shard_map/pallas_call | solution.py:105
  68.1 3.2 %collective-permute-start.15 = (bf16[2,224,1280]{2,1,0:T(8,128)(2,1)S(1)}, bf16[2,224,1280]{2,1,0:T(8,128)(2,1)}, u32[]{:S(2)}, u32[]{:S(2)}) collective-permute-start(bf16[2,224,1280]{2,1,0:T(8,128)(2,1)S(1)} %pad_maximum_fusion.2.refs_0_), channel_id=1, source_target_pairs={{0,6},{1,25},{2,0},{3,27},{4,2},{5,29},{6,4},{7,31},{8,14},{9,1},{... | collective-permute-start | bytes 3440648 | tf_op jit(solution)/shard_map/ppermute | solution.py:57
  72.0 3.8 %shard_map.132.xt = bf16[16,256,256]{2,1,0:T(8,128)(2,1)S(1)} custom-call(bf16[256,3584]{1,0:T(8,128)(2,1)} %collective-permute-done.11.tok.tok_other, f32[1,3584]{1,0:T(1,128)S(1)} %broadcast_in_dim.14.gain), custom_call_target="tpu_custom_call" | custom-call | bytes 3670016 | tf_op jit(solution)/shard_map/pallas_call | solution.py:105
  77.2 3.2 %collective-permute-start.18 = (bf16[2,224,1280]{2,1,0:T(8,128)(2,1)}, bf16[2,224,1280]{2,1,0:T(8,128)(2,1)}, u32[]{:S(2)}, u32[]{:S(2)}) collective-permute-start(bf16[2,224,1280]{2,1,0:T(8,128)(2,1)} %collective-permute-done.16.refs_5_.refs_7_), channel_id=1, source_target_pairs={{0,6},{1,25},{2,0},{3,27},{4,2},{5,29},{6,4},{7,31},{8,14},{9,1},{... | collective-permute-start | bytes 3440648 | tf_op jit(solution)/shard_map/ppermute | solution.py:57
  81.2 4.2 %collective-permute-done.14.refs_3_ = bf16[2,224,1280]{2,1,0:T(8,128)(2,1)} collective-permute-done((bf16[2,224,1280]{2,1,0:T(8,128)(2,1)}, bf16[2,224,1280]{2,1,0:T(8,128)(2,1)}, u32[]{:S(2)}, u32[]{:S(2)}) %collective-permute-start.14) | collective-permute-done | bytes 1146912 | tf_op jit(solution)/shard_map/ppermute | solution.py:57
  85.5 1.9 collective-permute-done.15.refs_4_.refs_6_
  89.0 8.6 %shard_map.133.part = f32[512,1152]{1,0:T(8,128)S(1)} custom-call(s32[32]{0:T(128)S(1)} %pad_add_fusion.2.order, bf16[16,256,256]{2,1,0:T(8,128)(2,1)S(1)} %shard_map.131.xo, bf16[16,256,256]{2,1,0:T(8,128)(2,1)S(1)} %copy-done.1, bf16[2,224,1280]{2,1,0:T(8,128)(2,1)S(1)} %pad_maximum_fusion.2.refs_0_, bf16[2,224,1280]{2,1,0:T(8,128)(2,1)} %pad_maximum_fusion.3.refs_1_, ...), custom_call_target="tpu_custom_call" | custom-call | flops 3623878656 | bytes 7077888 | tf_op jit(solution)/shard_map/pallas_call | solution.py:182
  97.8 2.0 collective-permute-done.18.refs_1_.refs_5_
  99.8 7.2 %shard_map.134.att = bf16[512,896]{1,0:T(8,128)(2,1)S(1)} custom-call(s32[32]{0:T(128)S(1)} %pad_add_fusion.2.order, bf16[16,256,256]{2,1,0:T(8,128)(2,1)S(1)} %shard_map.131.xo, bf16[16,256,256]{2,1,0:T(8,128)(2,1)S(1)} %copy-done.1, s32[512,1]{1,0:T(8,128)S(1)} %copy.36.seg_col, s32[2,1,256]{2,1,0:T(1,128)S(1)} %broadcast_in_dim.16.seg_row, ...), custom_call_target="tpu_custom_call" | custom-call | flops 2415919104 | bytes 7077888 | tf_op jit(solution)/shard_map/pallas_call | solution.py:202
  111.6 11.2 %shard_map.135 = (bf16[256,1792]{1,0:T(8,128)(2,1)S(1)}, bf16[256,1792]{1,0:T(8,128)(2,1)S(1)}, bf16[8,1792]{1,0:T(8,128)(2,1)S(1)}, bf16[8,1792]{1,0:T(8,128)(2,1)S(1)}) custom-call(s32[32]{0:T(128)S(1)} %pad_add_fusion.2.order, s32[2]{0:T(128)S(1)} %copy-done.5, bf16[256,3584]{1,0:T(8,128)(2,1)} %tok_own.1, ...), custom_call_target="tpu_custom_call" | custom-call | flops 3288334336 | bytes 6422528 | tf_op jit(solution)/shard_map/pallas_call | solution.py:283
  124.4 25.3 %all_to_all.5 = bf16[128,8,256]{2,1,0:T(8,128)(2,1)S(1)} all-to-all(bf16[128,8,256]{2,1,0:T(8,128)(2,1)S(1)} %bitcast.61), channel_id=1, replica_groups=mesh['grp'=4,'page'=32] {'grp','page'}, dimensions={0} | all-to-all | bytes 1048576 | tf_op jit(solution)/shard_map/all_to_all | solution.py:577
  152.0 1.8 collective-permute-start.23
  154.7 2.1 %collective-permute-done.22 = bf16[256,128]{1,0:T(8,128)(2,1)S(1)} collective-permute-done((bf16[256,128]{1,0:T(8,128)(2,1)S(1)}, bf16[256,128]{1,0:T(8,128)(2,1)S(1)}, u32[]{:S(2)}, u32[]{:S(2)}) %collective-permute-start.22) | collective-permute-done | bytes 65568 | tf_op jit(solution)/shard_map/ppermute | solution.py:51
  162.1 6.8 %collective-permute-done.25.b1 = bf16[4,256,128]{2,1,0:T(8,128)(2,1)S(1)} collective-permute-done((bf16[4,256,128]{2,1,0:T(8,128)(2,1)S(1)}, bf16[4,256,128]{2,1,0:T(8,128)(2,1)S(1)}, u32[]{:S(2)}, u32[]{:S(2)}) %collective-permute-start.25) | collective-permute-done | bytes 262176 | tf_op jit(solution)/shard_map/ppermute | solution.py:57
  171.3 8.2 %shard_map.138 = (bf16[4,4,8,3584]{3,2,1,0:T(8,128)(2,1)S(1)}, bf16[4,4,8,3584]{3,2,1,0:T(8,128)(2,1)S(1)}, f32[8,3584]{1,0:T(8,128)S(1)}) custom-call(s32[32]{0:T(128)S(1)} %pad_add_fusion.2.order, s32[32]{0:T(128)S(1)} %copy-done.7, s32[2]{0:T(128)S(1)} %copy-done.5, bf16[4,256,128]{2,1,0:T(8,128)(2,1)S(1)} %pad_maximum_fusion.5.t, ...), custom_call_target="tpu_custom_call" | custom-call | flops 2818572288 | bytes 11010048 | tf_op jit(solution)/shard_map/pallas_call | solution.py:433
  180.1 2.0 collective-permute-done.32
  183.7 2.7 %collective-permute-start.34 = (bf16[4,8,3584]{2,1,0:T(8,128)(2,1)S(1)}, bf16[4,8,3584]{2,1,0:T(8,128)(2,1)S(1)}, u32[]{:S(2)}, u32[]{:S(2)}) collective-permute-start(bf16[4,8,3584]{2,1,0:T(8,128)(2,1)S(1)} %get-tuple-element.68), channel_id=1, source_target_pairs={{0,16},{1,5},{2,18},{3,7},{4,20},{5,1},{6,22},{7,3},{8,24},{9,13},... | collective-permute-start | bytes 688136 | tf_op jit(solution)/shard_map/ppermute | solution.py:51
  186.7 2.9 %collective-permute-done.33 = bf16[4,8,3584]{2,1,0:T(8,128)(2,1)S(1)} collective-permute-done((bf16[4,8,3584]{2,1,0:T(8,128)(2,1)S(1)}, bf16[4,8,3584]{2,1,0:T(8,128)(2,1)S(1)}, u32[]{:S(2)}, u32[]{:S(2)}) %collective-permute-start.33) | collective-permute-done | bytes 229408 | tf_op jit(solution)/shard_map/ppermute | solution.py:51
  189.6 3.2 %collective-permute-done.34 = bf16[4,8,3584]{2,1,0:T(8,128)(2,1)S(1)} collective-permute-done((bf16[4,8,3584]{2,1,0:T(8,128)(2,1)S(1)}, bf16[4,8,3584]{2,1,0:T(8,128)(2,1)S(1)}, u32[]{:S(2)}, u32[]{:S(2)}) %collective-permute-start.34) | collective-permute-done | bytes 229408 | tf_op jit(solution)/shard_map/ppermute | solution.py:51
  193.5 3.8 %collective-permute-start.37 = (bf16[8,3584]{1,0:T(8,128)(2,1)S(1)}, bf16[8,3584]{1,0:T(8,128)(2,1)S(1)}, u32[]{:S(2)}, u32[]{:S(2)}) collective-permute-start(bf16[8,3584]{1,0:T(8,128)(2,1)S(1)} %get-tuple-element.79), channel_id=1, source_target_pairs={{0,4},{1,17},{2,6},{3,19},{4,0},{5,21},{6,2},{7,23},{8,12},{9,25},... | collective-permute-start | bytes 172040 | tf_op jit(solution)/shard_map/ppermute | solution.py:57
  (146 shorter events, 45.3 us)
Async XLA Ops:
  7.2 102.6 %all-gather.2.cloned.1.call-start = ((), (), s32[]{:S(2)}) async-start(), calls=%async_computation.1 | async-start | bytes 6881280 | tf_op jit(solution)/shard_map/all_gather | solution.py:546
  9.5 6.5 %collective-permute-start.4 = (bf16[112,1152]{1,0:T(8,128)(2,1)S(1)}, bf16[112,1152]{1,0:T(8,128)(2,1)S(1)}, u32[]{:S(2)}, u32[]{:S(2)}) collective-permute-start(bf16[112,1152]{1,0:T(8,128)(2,1)S(1)} %pad_maximum_fusion.7), channel_id=1, source_target_pairs={{0,1},{1,0},{2,3},{3,2},{4,5},{5,4},{6,7},{7,6},{8,9},{9,8},{10,11... | collective-permute-start | bytes 774152 | tf_op jit(solution)/shard_map/ppermute | solution.py:47
  10.2 6.0 %collective-permute-start.1 = (bf16[112,384]{1,0:T(8,128)(2,1)S(1)}, bf16[112,384]{1,0:T(8,128)(2,1)S(1)}, u32[]{:S(2)}, u32[]{:S(2)}) collective-permute-start(bf16[112,384]{1,0:T(8,128)(2,1)S(1)} %fusion.19), channel_id=1, source_target_pairs={{0,8},{1,3},{2,10},{3,5},{4,12},{5,7},{6,14},{7,1},{8,16},{9,11},{... | collective-permute-start | bytes 258056 | tf_op jit(solution)/shard_map/ppermute | solution.py:51
  11.8 6.1 %collective-permute-start.2 = (bf16[112,384]{1,0:T(8,128)(2,1)S(1)}, bf16[112,384]{1,0:T(8,128)(2,1)S(1)}, u32[]{:S(2)}, u32[]{:S(2)}) collective-permute-start(bf16[112,384]{1,0:T(8,128)(2,1)S(1)} %fusion.19), channel_id=1, source_target_pairs={{0,16},{1,5},{2,18},{3,7},{4,20},{5,1},{6,22},{7,3},{8,24},{9,13},... | collective-permute-start | bytes 258056 | tf_op jit(solution)/shard_map/ppermute | solution.py:51
  14.5 4.5 %collective-permute-start.3 = (bf16[112,384]{1,0:T(8,128)(2,1)S(1)}, bf16[112,384]{1,0:T(8,128)(2,1)S(1)}, u32[]{:S(2)}, u32[]{:S(2)}) collective-permute-start(bf16[112,384]{1,0:T(8,128)(2,1)S(1)} %fusion.19), channel_id=1, source_target_pairs={{0,24},{1,7},{2,26},{3,1},{4,28},{5,3},{6,30},{7,5},{8,0},{9,15},{... | collective-permute-start | bytes 258056 | tf_op jit(solution)/shard_map/ppermute | solution.py:51
  19.1 17.8 %collective-permute-start.8 = (bf16[224,1280]{1,0:T(8,128)(2,1)S(1)}, bf16[224,1280]{1,0:T(8,128)(2,1)S(1)}, u32[]{:S(2)}, u32[]{:S(2)}) collective-permute-start(bf16[224,1280]{1,0:T(8,128)(2,1)S(1)} %fusion.7), channel_id=1, source_target_pairs={{0,8},{1,3},{2,10},{3,5},{4,12},{5,7},{6,14},{7,1},{8,16},{9,11},{... | collective-permute-start | bytes 1720328 | tf_op jit(solution)/shard_map/ppermute | solution.py:51
  19.9 17.1 %collective-permute-start.9 = (bf16[224,1280]{1,0:T(8,128)(2,1)S(1)}, bf16[224,1280]{1,0:T(8,128)(2,1)S(1)}, u32[]{:S(2)}, u32[]{:S(2)}) collective-permute-start(bf16[224,1280]{1,0:T(8,128)(2,1)S(1)} %fusion.7), channel_id=1, source_target_pairs={{0,24},{1,7},{2,26},{3,1},{4,28},{5,3},{6,30},{7,5},{8,0},{9,15},{... | collective-permute-start | bytes 1720328 | tf_op jit(solution)/shard_map/ppermute | solution.py:51
  22.4 10.3 %collective-permute-start.5 = (bf16[4,112,384]{2,1,0:T(8,128)(2,1)S(1)}, bf16[4,112,384]{2,1,0:T(8,128)(2,1)S(1)}, u32[]{:S(2)}, u32[]{:S(2)}) collective-permute-start(bf16[4,112,384]{2,1,0:T(8,128)(2,1)S(1)} %pad_maximum_fusion.4), channel_id=1, source_target_pairs={{0,2},{1,9},{2,4},{3,11},{4,6},{5,13},{6,0},{7,15},{8,10},{9,17},{... | collective-permute-start | bytes 1032200 | tf_op jit(solution)/shard_map/ppermute | solution.py:57
  24.3 12.5 %collective-permute-start.6 = (bf16[4,112,384]{2,1,0:T(8,128)(2,1)S(1)}, bf16[4,112,384]{2,1,0:T(8,128)(2,1)S(1)}, u32[]{:S(2)}, u32[]{:S(2)}) collective-permute-start(bf16[4,112,384]{2,1,0:T(8,128)(2,1)S(1)} %pad_maximum_fusion.4), channel_id=1, source_target_pairs={{0,4},{1,17},{2,6},{3,19},{4,0},{5,21},{6,2},{7,23},{8,12},{9,25},... | collective-permute-start | bytes 1032200 | tf_op jit(solution)/shard_map/ppermute | solution.py:57
  27.9 8.9 %collective-permute-start.7 = (bf16[4,112,384]{2,1,0:T(8,128)(2,1)S(1)}, bf16[4,112,384]{2,1,0:T(8,128)(2,1)S(1)}, u32[]{:S(2)}, u32[]{:S(2)}) collective-permute-start(bf16[4,112,384]{2,1,0:T(8,128)(2,1)S(1)} %pad_maximum_fusion.4), channel_id=1, source_target_pairs={{0,6},{1,25},{2,0},{3,27},{4,2},{5,29},{6,4},{7,31},{8,14},{9,1},{... | collective-permute-start | bytes 1032200 | tf_op jit(solution)/shard_map/ppermute | solution.py:57
  38.9 28.9 %collective-permute-start.12 = (s32[1,8]{1,0:T(1,128)S(1)}, s32[1,8]{1,0:T(1,128)S(1)}, u32[]{:S(2)}, u32[]{:S(2)}) collective-permute-start(s32[1,8]{1,0:T(1,128)S(1)} %copy-done.14), channel_id=1, source_target_pairs={{0,1},{1,0},{2,3},{3,2},{4,5},{5,4},{6,7},{7,6},{8,9},{9,8},{10,11... | collective-permute-start | bytes 104 | tf_op jit(solution)/shard_map/ppermute | solution.py:47
  40.1 31.9 %collective-permute-start.11 = (bf16[256,3584]{1,0:T(8,128)(2,1)}, bf16[256,3584]{1,0:T(8,128)(2,1)}, u32[]{:S(2)}, u32[]{:S(2)}) collective-permute-start(bf16[256,3584]{1,0:T(8,128)(2,1)} %tok_own.1), channel_id=1, source_target_pairs={{0,1},{1,0},{2,3},{3,2},{4,5},{5,4},{6,7},{7,6},{8,9},{9,8},{10,11... | collective-permute-start | bytes 5505032 | tf_op jit(solution)/shard_map/ppermute | solution.py:47
  40.5 14.4 %collective-permute-start.13 = (bf16[224,1280]{1,0:T(8,128)(2,1)S(1)}, bf16[224,1280]{1,0:T(8,128)(2,1)}, u32[]{:S(2)}, u32[]{:S(2)}) collective-permute-start(bf16[224,1280]{1,0:T(8,128)(2,1)S(1)} %fusion.7), channel_id=1, source_target_pairs={{0,16},{1,5},{2,18},{3,7},{4,20},{5,1},{6,22},{7,3},{8,24},{9,13},... | collective-permute-start | bytes 1720328 | tf_op jit(solution)/shard_map/ppermute | solution.py:51
  42.9 34.3 %collective-permute-start.10 = (bf16[2,224,1280]{2,1,0:T(8,128)(2,1)S(1)}, bf16[2,224,1280]{2,1,0:T(8,128)(2,1)}, u32[]{:S(2)}, u32[]{:S(2)}) collective-permute-start(bf16[2,224,1280]{2,1,0:T(8,128)(2,1)S(1)} %pad_maximum_fusion.2.refs_0_), channel_id=1, source_target_pairs={{0,2},{1,9},{2,4},{3,11},{4,6},{5,13},{6,0},{7,15},{8,10},{9,17},{... | collective-permute-start | bytes 3440648 | tf_op jit(solution)/shard_map/ppermute | solution.py:57
  57.0 20.2 %collective-permute-start.16 = (bf16[2,224,1280]{2,1,0:T(8,128)(2,1)}, bf16[2,224,1280]{2,1,0:T(8,128)(2,1)}, u32[]{:S(2)}, u32[]{:S(2)}) collective-permute-start(bf16[2,224,1280]{2,1,0:T(8,128)(2,1)} %pad_maximum_fusion.3.refs_1_), channel_id=1, source_target_pairs={{0,6},{1,25},{2,0},{3,27},{4,2},{5,29},{6,4},{7,31},{8,14},{9,1},{... | collective-permute-start | bytes 3440648 | tf_op jit(solution)/shard_map/ppermute | solution.py:57
  68.1 17.4 %collective-permute-start.14 = (bf16[2,224,1280]{2,1,0:T(8,128)(2,1)}, bf16[2,224,1280]{2,1,0:T(8,128)(2,1)}, u32[]{:S(2)}, u32[]{:S(2)}) collective-permute-start(bf16[2,224,1280]{2,1,0:T(8,128)(2,1)} %pad_maximum_fusion.3.refs_1_), channel_id=1, source_target_pairs={{0,2},{1,9},{2,4},{3,11},{4,6},{5,13},{6,0},{7,15},{8,10},{9,17},{... | collective-permute-start | bytes 3440648 | tf_op jit(solution)/shard_map/ppermute | solution.py:57
  68.1 19.3 %collective-permute-start.15 = (bf16[2,224,1280]{2,1,0:T(8,128)(2,1)S(1)}, bf16[2,224,1280]{2,1,0:T(8,128)(2,1)}, u32[]{:S(2)}, u32[]{:S(2)}) collective-permute-start(bf16[2,224,1280]{2,1,0:T(8,128)(2,1)S(1)} %pad_maximum_fusion.2.refs_0_), channel_id=1, source_target_pairs={{0,6},{1,25},{2,0},{3,27},{4,2},{5,29},{6,4},{7,31},{8,14},{9,1},{... | collective-permute-start | bytes 3440648 | tf_op jit(solution)/shard_map/ppermute | solution.py:57
  77.2 20.6 %collective-permute-start.17 = (bf16[2,224,1280]{2,1,0:T(8,128)(2,1)}, bf16[2,224,1280]{2,1,0:T(8,128)(2,1)}, u32[]{:S(2)}, u32[]{:S(2)}) collective-permute-start(bf16[2,224,1280]{2,1,0:T(8,128)(2,1)} %collective-permute-done.10.refs_2_), channel_id=1, source_target_pairs={{0,2},{1,9},{2,4},{3,11},{4,6},{5,13},{6,0},{7,15},{8,10},{9,17},{... | collective-permute-start | bytes 3440648 | tf_op jit(solution)/shard_map/ppermute | solution.py:57
  77.2 22.6 %collective-permute-start.18 = (bf16[2,224,1280]{2,1,0:T(8,128)(2,1)}, bf16[2,224,1280]{2,1,0:T(8,128)(2,1)}, u32[]{:S(2)}, u32[]{:S(2)}) collective-permute-start(bf16[2,224,1280]{2,1,0:T(8,128)(2,1)} %collective-permute-done.16.refs_5_.refs_7_), channel_id=1, source_target_pairs={{0,6},{1,25},{2,0},{3,27},{4,2},{5,29},{6,4},{7,31},{8,14},{9,1},{... | collective-permute-start | bytes 3440648 | tf_op jit(solution)/shard_map/ppermute | solution.py:57
  151.3 5.5 %collective-permute-start.22 = (bf16[256,128]{1,0:T(8,128)(2,1)S(1)}, bf16[256,128]{1,0:T(8,128)(2,1)S(1)}, u32[]{:S(2)}, u32[]{:S(2)}) collective-permute-start(bf16[256,128]{1,0:T(8,128)(2,1)S(1)} %shard_map.137), channel_id=1, source_target_pairs={{0,8},{1,3},{2,10},{3,5},{4,12},{5,7},{6,14},{7,1},{8,16},{9,11},{... | collective-permute-start | bytes 196616 | tf_op jit(solution)/shard_map/ppermute | solution.py:51
  152.0 5.8 %collective-permute-start.23 = (bf16[256,128]{1,0:T(8,128)(2,1)S(1)}, bf16[256,128]{1,0:T(8,128)(2,1)S(1)}, u32[]{:S(2)}, u32[]{:S(2)}) collective-permute-start(bf16[256,128]{1,0:T(8,128)(2,1)S(1)} %shard_map.137), channel_id=1, source_target_pairs={{0,16},{1,5},{2,18},{3,7},{4,20},{5,1},{6,22},{7,3},{8,24},{9,13},... | collective-permute-start | bytes 196616 | tf_op jit(solution)/shard_map/ppermute | solution.py:51
  153.8 4.6 %collective-permute-start.24 = (bf16[256,128]{1,0:T(8,128)(2,1)S(1)}, bf16[256,128]{1,0:T(8,128)(2,1)S(1)}, u32[]{:S(2)}, u32[]{:S(2)}) collective-permute-start(bf16[256,128]{1,0:T(8,128)(2,1)S(1)} %shard_map.137), channel_id=1, source_target_pairs={{0,24},{1,7},{2,26},{3,1},{4,28},{5,3},{6,30},{7,5},{8,0},{9,15},{... | collective-permute-start | bytes 196616 | tf_op jit(solution)/shard_map/ppermute | solution.py:51
  158.4 10.5 %collective-permute-start.25 = (bf16[4,256,128]{2,1,0:T(8,128)(2,1)S(1)}, bf16[4,256,128]{2,1,0:T(8,128)(2,1)S(1)}, u32[]{:S(2)}, u32[]{:S(2)}) collective-permute-start(bf16[4,256,128]{2,1,0:T(8,128)(2,1)S(1)} %pad_maximum_fusion.5.t), channel_id=1, source_target_pairs={{0,2},{1,9},{2,4},{3,11},{4,6},{5,13},{6,0},{7,15},{8,10},{9,17},{... | collective-permute-start | bytes 786440 | tf_op jit(solution)/shard_map/ppermute | solution.py:57
  158.7 10.2 %collective-permute-start.26 = (bf16[4,256,128]{2,1,0:T(8,128)(2,1)S(1)}, bf16[4,256,128]{2,1,0:T(8,128)(2,1)S(1)}, u32[]{:S(2)}, u32[]{:S(2)}) collective-permute-start(bf16[4,256,128]{2,1,0:T(8,128)(2,1)S(1)} %pad_maximum_fusion.5.t), channel_id=1, source_target_pairs={{0,4},{1,17},{2,6},{3,19},{4,0},{5,21},{6,2},{7,23},{8,12},{9,25},... | collective-permute-start | bytes 786440 | tf_op jit(solution)/shard_map/ppermute | solution.py:57
  160.4 9.4 %collective-permute-start.27 = (bf16[4,256,128]{2,1,0:T(8,128)(2,1)S(1)}, bf16[4,256,128]{2,1,0:T(8,128)(2,1)S(1)}, u32[]{:S(2)}, u32[]{:S(2)}) collective-permute-start(bf16[4,256,128]{2,1,0:T(8,128)(2,1)S(1)} %pad_maximum_fusion.5.t), channel_id=1, source_target_pairs={{0,6},{1,25},{2,0},{3,27},{4,2},{5,29},{6,4},{7,31},{8,14},{9,1},{... | collective-permute-start | bytes 786440 | tf_op jit(solution)/shard_map/ppermute | solution.py:57
  162.1 7.7 %collective-permute-start.28 = (bf16[4,256,128]{2,1,0:T(8,128)(2,1)S(1)}, bf16[4,256,128]{2,1,0:T(8,128)(2,1)S(1)}, u32[]{:S(2)}, u32[]{:S(2)}) collective-permute-start(bf16[4,256,128]{2,1,0:T(8,128)(2,1)S(1)} %pad_maximum_fusion.5.t), channel_id=1, source_target_pairs={{0,1},{1,0},{2,3},{3,2},{4,5},{5,4},{6,7},{7,6},{8,9},{9,8},{10,11... | collective-permute-start | bytes 786440 | tf_op jit(solution)/shard_map/ppermute | solution.py:47
  179.8 6.7 %collective-permute-start.20 = (bf16[256,1792]{1,0:T(8,128)(2,1)S(1)}, bf16[256,1792]{1,0:T(8,128)(2,1)S(1)}, u32[]{:S(2)}, u32[]{:S(2)}) collective-permute-start(bf16[256,1792]{1,0:T(8,128)(2,1)S(1)} %get-tuple-element.53), channel_id=1, source_target_pairs={{0,1},{1,0},{2,3},{3,2},{4,5},{5,4},{6,7},{7,6},{8,9},{9,8},{10,11... | collective-permute-start | bytes 2752520 | tf_op jit(solution)/shard_map/ppermute | solution.py:47
  182.3 7.3 %collective-permute-start.33 = (bf16[4,8,3584]{2,1,0:T(8,128)(2,1)S(1)}, bf16[4,8,3584]{2,1,0:T(8,128)(2,1)S(1)}, u32[]{:S(2)}, u32[]{:S(2)}) collective-permute-start(bf16[4,8,3584]{2,1,0:T(8,128)(2,1)S(1)} %get-tuple-element.66), channel_id=1, source_target_pairs={{0,8},{1,3},{2,10},{3,5},{4,12},{5,7},{6,14},{7,1},{8,16},{9,11},{... | collective-permute-start | bytes 688136 | tf_op jit(solution)/shard_map/ppermute | solution.py:51
  183.7 9.1 %collective-permute-start.34 = (bf16[4,8,3584]{2,1,0:T(8,128)(2,1)S(1)}, bf16[4,8,3584]{2,1,0:T(8,128)(2,1)S(1)}, u32[]{:S(2)}, u32[]{:S(2)}) collective-permute-start(bf16[4,8,3584]{2,1,0:T(8,128)(2,1)S(1)} %get-tuple-element.68), channel_id=1, source_target_pairs={{0,16},{1,5},{2,18},{3,7},{4,20},{5,1},{6,22},{7,3},{8,24},{9,13},... | collective-permute-start | bytes 688136 | tf_op jit(solution)/shard_map/ppermute | solution.py:51
  186.3 6.6 %collective-permute-start.35 = (bf16[4,8,3584]{2,1,0:T(8,128)(2,1)S(1)}, bf16[4,8,3584]{2,1,0:T(8,128)(2,1)S(1)}, u32[]{:S(2)}, u32[]{:S(2)}) collective-permute-start(bf16[4,8,3584]{2,1,0:T(8,128)(2,1)S(1)} %get-tuple-element.67), channel_id=1, source_target_pairs={{0,24},{1,7},{2,26},{3,1},{4,28},{5,3},{6,30},{7,5},{8,0},{9,15},{... | collective-permute-start | bytes 688136 | tf_op jit(solution)/shard_map/ppermute | solution.py:51
  193.1 5.5 %collective-permute-start.36 = (bf16[8,3584]{1,0:T(8,128)(2,1)S(1)}, bf16[8,3584]{1,0:T(8,128)(2,1)S(1)}, u32[]{:S(2)}, u32[]{:S(2)}) collective-permute-start(bf16[8,3584]{1,0:T(8,128)(2,1)S(1)} %get-tuple-element.77), channel_id=1, source_target_pairs={{0,2},{1,9},{2,4},{3,11},{4,6},{5,13},{6,0},{7,15},{8,10},{9,17},{... | collective-permute-start | bytes 172040 | tf_op jit(solution)/shard_map/ppermute | solution.py:57
  193.5 6.6 %collective-permute-start.37 = (bf16[8,3584]{1,0:T(8,128)(2,1)S(1)}, bf16[8,3584]{1,0:T(8,128)(2,1)S(1)}, u32[]{:S(2)}, u32[]{:S(2)}) collective-permute-start(bf16[8,3584]{1,0:T(8,128)(2,1)S(1)} %get-tuple-element.79), channel_id=1, source_target_pairs={{0,4},{1,17},{2,6},{3,19},{4,0},{5,21},{6,2},{7,23},{8,12},{9,25},... | collective-permute-start | bytes 172040 | tf_op jit(solution)/shard_map/ppermute | solution.py:57
  (24 other events, 186.9 us)
Sparse Core Ops, SparseCore 0:
  38.4 61.4 all-gather.1

commit v3 on v2

--- a/solution.py
+++ b/solution.py
@@ -68,6 +68,12 @@
     ends = jnp.cumsum(lengths, dtype=jnp.int32)
     position = jnp.arange(count, dtype=jnp.int32)
     return jnp.sum((position[:, None] >= ends[None, :]).astype(jnp.int32), axis=1)
+
+
+def chip_at(pos, core, j, k, sign):
+    shift_x = jnp.where(core == 0, sign * j, sign * k)
+    shift_z = jnp.where(core == 0, sign * k, sign * j)
+    return lax.rem(pos[2] + SIDE + shift_x, SIDE) * SIDE + lax.rem(pos[3] + SIDE + shift_z, SIDE)
 
 
 def run_copies(copies, sems):
@@ -113,7 +119,7 @@
     )(tok, gain)
 
 
-def qkv_load(order, steps, pieces, xo, xt, w, x, sems):
+def qkv_load(pos, steps, pieces, xo, xt, w, x, sems):
     cols = w.shape[1]
     depth = pieces[0].shape[1]
     tokens = xo.shape[1]
@@ -123,7 +129,7 @@
         copies.append((piece, w.at[pl.ds(n * BLOCK, depth), :]))
     started = run_copies(copies, sems)
     for n in range(2 * len(pieces)):
-        q = order[steps[n // SIDE] * SIDE + n % SIDE]
+        q = chip_at(pos, pos[0], n % SIDE, steps[n // SIDE], -1)
         x[0:tokens, n * BLOCK : (n + 1) * BLOCK] = xo[q]
         x[tokens : 2 * tokens, n * BLOCK : (n + 1) * BLOCK] = xt[q]
         w[n * BLOCK + depth : (n + 1) * BLOCK, :] = jnp.zeros((BLOCK - depth, cols), BF)
@@ -134,9 +140,9 @@
 QKV_TILE = 384
 
 
-def qkv_first_kernel(order, xo, xt, *refs):
+def qkv_first_kernel(pos, xo, xt, *refs):
     *pieces, part, w, x, sems = refs
-    qkv_load(order, (0, 1, 3), pieces, xo, xt, w, x, sems)
+    qkv_load(pos, (0, 1, 3), pieces, xo, xt, w, x, sems)
 
     @pl.loop(0, part.shape[1] // QKV_TILE)
     def _(n):
@@ -144,9 +150,9 @@
         part[:, there] = jnp.dot(x[...], w[:, there], preferred_element_type=F32)
 
 
-def qkv_last_kernel(order, xo, xt, seg_col, seg_row, part, *refs):
+def qkv_last_kernel(pos, xo, xt, seg_col, seg_row, part, *refs):
     *pieces, out, w, x, qkv, sems = refs
-    qkv_load(order, (2,), pieces, xo, xt, w, x, sems)
+    qkv_load(pos, (2,), pieces, xo, xt, w, x, sems)
 
     @pl.loop(0, part.shape[1] // QKV_TILE)
     def _(n):
@@ -162,7 +168,9 @@
         rows = pl.ds(pl.multiple_of(b * tokens, tokens), tokens)
         same = seg_col[rows, :] == seg_row[b]
         keys = qkv[rows, heads * HD : (heads + 1) * HD]
-        values = qkv[rows, (heads + 1) * HD : (heads + 2) * HD]
+        values = jnp.concatenate(
+            [qkv[rows, (heads + 1) * HD : (heads + 2) * HD], jnp.ones((tokens, HD), BF)], axis=1
+        )
         for h in range(heads):
             query = qkv[rows, h * HD : (h + 1) * HD]
             scores = lax.dot_general(
@@ -170,14 +178,12 @@
             ) * (math.log2(math.e) / math.sqrt(HD))
             scores = jnp.where(same, scores, -1e30)
             top = jnp.max(scores, axis=1, keepdims=True)
-            e = jnp.exp2(scores - top)
-            weights = (e * (1.0 / jnp.sum(e, axis=1, keepdims=True))).astype(BF)
-            out[rows, h * HD : (h + 1) * HD] = jnp.dot(
-                weights, values, preferred_element_type=F32
-            ).astype(BF)
-
-
-def qkv_first(order, x_own, x_other, pieces, cols):
+            weights = jnp.exp2(scores - top).astype(BF)
+            mixed = jnp.dot(weights, values, preferred_element_type=F32)
+            out[rows, h * HD : (h + 1) * HD] = (mixed[:, 0:HD] / mixed[:, HD : 2 * HD]).astype(BF)
+
+
+def qkv_first(pos, x_own, x_other, pieces, cols):
     tokens = x_own.shape[1]
     return pl.pallas_call(
         qkv_first_kernel,
@@ -193,10 +199,10 @@
         cost_estimate=pl.CostEstimate(
             flops=4 * tokens * 12 * BLOCK * cols, bytes_accessed=24 * BLOCK * cols, transcendentals=0
         ),
-    )(order, x_own, x_other, *pieces)
-
-
-def qkv_last(order, x_own, x_other, seg_col, seg_row, part, pieces):
+    )(pos, x_own, x_other, *pieces)
+
+
+def qkv_last(pos, x_own, x_other, seg_col, seg_row, part, pieces):
     tokens = x_own.shape[1]
     cols = part.shape[1]
     return pl.pallas_call(
@@ -214,23 +220,46 @@
         cost_estimate=pl.CostEstimate(
             flops=4 * tokens * 8 * BLOCK * cols, bytes_accessed=24 * BLOCK * cols, transcendentals=0
         ),
-    )(order, x_own, x_other, seg_col, seg_row, part, *pieces)
+    )(pos, x_own, x_other, seg_col, seg_row, part, *pieces)
+
+
+def arrange_kernel(pos, t, b1, b2, b3, out):
+    for k, piece in enumerate((t, b1, b2, b3)):
+        for j in range(SIDE):
+            out[chip_at(pos, pos[0], j, k, -1)] = piece[j]
+
+
+def arrange(pos, pieces):
+    n, rows, cols = pieces[0].shape
+    return pl.pallas_call(
+        arrange_kernel,
+        out_shape=jax.ShapeDtypeStruct((SIDE * n, rows, cols), BF),
+        in_specs=[smem()] + [vmem()] * 4,
+        out_specs=vmem(),
+        compiler_params=params(16),
+        cost_estimate=pl.CostEstimate(
+            flops=0, bytes_accessed=4 * SIDE * n * rows * cols, transcendentals=0
+        ),
+    )(pos, *pieces)
 
 
 def out_kernel(
-    order, pos, tok_own, tok_other, att, att_in, member, member_t, inv, inv_t, w_all, *refs
+    pos, tok_own, tok_other, att, att_in, member, member_t, inv, inv_t, w_all, *refs
 ):
     pieces, refs = refs[: 2 * SIDE], refs[2 * SIDE :]
     st_own, st_other, pool_own, pool_other, w, rest, full, sems = refs
     core = pos[0]
-    depth, wy = w_all.shape[2:]
+    wy = w_all.shape[2]
+    depth = pieces[0].shape[1] // 2
     tile = rest.shape[1] // 2
     chips = SIDE * SIDE
     copies = []
-    rows = [pl.ds(pl.multiple_of(order[n] * depth, 16), depth) for n in range(chips)]
+    rows = [
+        pl.ds(pl.multiple_of(chip_at(pos, core, n % SIDE, n // SIDE, -1) * depth, 16), depth)
+        for n in range(chips)
+    ]
     for i in range(SIDE):
-        for n in range(chips):
-            copies.append((w_all.at[i, n], w.at[i, rows[n], :]))
+        copies.append((w_all.at[i], w.at[i]))
     for n in range(chips):
         for t in range(2):
             copies.append(
@@ -264,38 +293,36 @@
             ).astype(BF)
 
     for i in range(SIDE):
-        for copy in started[i * chips : (i + 1) * chips]:
-            copy.wait()
+        started[i].wait()
         columns(i * wy, wy, w[i])
-    for copy in started[SIDE * chips :]:
+    for copy in started[SIDE:]:
         copy.wait()
     columns(SIDE * wy, 2 * tile, rest[...])
 
 
-def page_out(order, pos, tok_own, tok_other, att, att_in, members, lens, w_all, pieces):
+def page_out(pos, tok_own, tok_other, att, att_in, members, lens, w_all, pieces):
     tokens, width = tok_own.shape
     width = width // 2
-    depth, wy = w_all.shape[2:]
-    rows = SIDE * SIDE * depth
+    rows, wy = w_all.shape[1:]
     pages = members[0].shape[0]
     st = jax.ShapeDtypeStruct((tokens, width), BF)
     pool = jax.ShapeDtypeStruct((pages, width), BF)
     return pl.pallas_call(
         out_kernel,
         out_shape=(st, st, pool, pool),
-        in_specs=[smem()] * 2 + [vmem()] * 8 + [anym()] * 9,
+        in_specs=[smem()] + [vmem()] * 8 + [anym()] * 9,
         out_specs=(vmem(),) * 4,
         scratch_shapes=[
             pltpu.VMEM((SIDE, rows, wy), BF),
             pltpu.VMEM((rows, width - SIDE * wy), BF),
             pltpu.VMEM((2 * tokens, rows), BF),
-            pltpu.SemaphoreType.DMA((6 * SIDE * SIDE,)),
+            pltpu.SemaphoreType.DMA((SIDE + 2 * SIDE * SIDE,)),
         ],
         compiler_params=params(40),
         cost_estimate=pl.CostEstimate(
             flops=2 * 2 * tokens * width * rows, bytes_accessed=2 * width * rows, transcendentals=0
         ),
-    )(order, pos, tok_own, tok_other, att, att_in, *members, *lens, w_all, *pieces)
+    )(pos, tok_own, tok_other, att, att_in, *members, *lens, w_all, *pieces)
 
 
 def block_kernel(vec, label, out):
@@ -362,7 +389,7 @@
 
 
 def ffn_kernel(
-    order, order_t, pos, t, b1, b2, b3, tt, c1, c2, c3, gain, gate_up, down, pick,
+    pos, t, b1, b2, b3, tt, c1, c2, c3, gain, gate_up, down, pick,
     own, other, states, x, mixed, hidden, wgu, wd, acc, sems,
 ):
     core = pos[0]
@@ -370,28 +397,20 @@
     units = hidden.shape[1]
     half = units // 2
     weights = []
-    n_sem = 32
     for n in range(2):
         for g in range(2):
-            weights.append(
-                pltpu.make_async_copy(
-                    gate_up.at[g, :, n * half : (n + 1) * half],
-                    wgu.at[g, :, n * half : (n + 1) * half],
-                    sems.at[n_sem + 2 * n + g],
-                )
-            )
-    down_copy = pltpu.make_async_copy(down, wd, sems.at[n_sem + 4])
+            part = (g, slice(None), slice(n * half, (n + 1) * half))
+            weights.append((gate_up.at[part], wgu.at[part]))
+    weights.append((down, wd))
     copies = []
-    for table, side, pieces in ((order, core, (t, b1, b2, b3)), (order_t, 1 - core, (tt, c1, c2, c3))):
+    for side, pieces in ((core, (t, b1, b2, b3)), (1 - core, (tt, c1, c2, c3))):
         for k, piece in enumerate(pieces):
             for j in range(SIDE):
-                head = table[k * SIDE + j] * 2 + side
+                head = chip_at(pos, side, j, k, -1) * 2 + side
                 copies.append((piece.at[j], x.at[:, pl.ds(pl.multiple_of(head * HD, HD), HD)]))
-    started = run_copies(copies, sems)
-    for copy in weights:
-        copy.start()
-    down_copy.start()
-    for copy in started:
+    started = run_copies(copies + weights, sems)
+    weights = started[len(copies) :]
+    for copy in started[: len(copies)]:
         copy.wait()
     chunk = 32
 
@@ -409,9 +428,8 @@
         gate = jnp.dot(mixed[...], wgu[0, :, cols], preferred_element_type=F32)
         up = jnp.dot(mixed[...], wgu[1, :, cols], preferred_element_type=F32)
         hidden[:, cols] = (gate * jax.nn.sigmoid(gate) * up).astype(BF)
-    down_copy.wait()
+    weights[4].wait()
     tile = 512
-    pages = acc.shape[1]
 
     @pl.loop(0, width // tile)
     def _(n):
@@ -420,12 +438,12 @@
         acc[...] = part.reshape(acc.shape)
         for k in range(SIDE):
             for j in range(SIDE):
-                own[j, k, :, cols] = acc[order[16 + k * SIDE + j] * 2 + core].astype(BF)
-                other[j, k, :, cols] = acc[order_t[16 + k * SIDE + j] * 2 + 1 - core].astype(BF)
+                own[j, k, :, cols] = acc[chip_at(pos, core, j, k, 1) * 2 + core].astype(BF)
+                other[j, k, :, cols] = acc[chip_at(pos, 1 - core, j, k, 1) * 2 + 1 - core].astype(BF)
         states[:, cols] = jnp.dot(pick[...], x[:, cols], preferred_element_type=F32)
 
 
-def feed_forward(order, order_t, pos, pieces, pieces_t, gain, gate_up, down, pick):
+def feed_forward(pos, pieces, pieces_t, gain, gate_up, down, pick):
     width = gain.shape[1]
     units = down.shape[0]
     pages, count = pick.shape
@@ -433,7 +451,7 @@
     return pl.pallas_call(
         ffn_kernel,
         out_shape=(part, part, jax.ShapeDtypeStruct((pages, width), F32)),
-        in_specs=[smem()] * 3 + [anym()] * 8 + [vmem()] + [anym()] * 2 + [vmem()],
+        in_specs=[smem()] + [anym()] * 8 + [vmem()] + [anym()] * 2 + [vmem()],
         out_specs=(vmem(),) * 3,
         scratch_shapes=[
             pltpu.VMEM((count, 2 * SIDE * SIDE * HD), BF),
@@ -448,7 +466,7 @@
         cost_estimate=pl.CostEstimate(
             flops=6 * count * width * units, bytes_accessed=6 * width * units, transcendentals=0
         ),
-    )(order, order_t, pos, *pieces, *pieces_t, gain, gate_up, down, pick)
+    )(pos, *pieces, *pieces_t, gain, gate_up, down, pick)
 
 
 def on_device(
@@ -472,16 +490,7 @@
     core = page % 2
     z = (page // 2) % SIDE
     x = page // (2 * SIDE)
-    pos = jnp.stack([core, grp]).astype(jnp.int32)
-    step = jnp.arange(SIDE, dtype=jnp.int32)
-    zero_order = (((x - step) % SIDE)[None, :] * SIDE + ((z - step) % SIDE)[:, None]).reshape(-1)
-    one_order = (((x - step) % SIDE)[:, None] * SIDE + ((z - step) % SIDE)[None, :]).reshape(-1)
-    order = jnp.where(core == 0, zero_order, one_order)
-    order_t = jnp.where(core == 0, one_order, zero_order)
-    zero_dest = (((x + step) % SIDE)[None, :] * SIDE + ((z + step) % SIDE)[:, None]).reshape(-1)
-    one_dest = (((x + step) % SIDE)[:, None] * SIDE + ((z + step) % SIDE)[None, :]).reshape(-1)
-    dest = jnp.where(core == 0, zero_dest, one_dest)
-    dest_t = jnp.where(core == 0, one_dest, zero_dest)
+    pos = jnp.stack([core, grp, x, z]).astype(jnp.int32)
 
     out_half = w_out.shape[1] // 2
     q_half = w_query.shape[1] // 2
@@ -504,7 +513,9 @@
         high = jnp.where(core == 0, got, mine)
         return jnp.concatenate([low, high], axis=0)
 
-    wo = pair_up(out_cols(core), swap(out_cols(1 - core)))
+    wo_got = swap(out_cols(1 - core))
+    w_query, w_keyval, wo_got = lax.optimization_barrier((w_query, w_keyval, wo_got))
+    wo = pair_up(out_cols(core), wo_got)
     wq = pair_up(qkv_cols(core), swap(qkv_cols(1 - core)))
     wo_y = lax.dynamic_slice_in_dim(wo, grp * WY, WY, 1)
     tile = (out_half - SIDE * WY) // 2
@@ -531,37 +542,30 @@
     pick = (
         jnp.arange(plane, dtype=jnp.int32)[None, :] == page * pages + jnp.arange(pages)[:, None]
     ).astype(BF)
-    tables = jnp.concatenate([order, dest])
-    tables_t = jnp.concatenate([order_t, dest_t])
-    early = (
-        x_own, x_other, seg_col, seg_row, members, lens, labels, head_gain, pick,
-        tables, tables_t, pos, ffn_gain[None, :],
-    )
+    early = (seg_col, seg_row, members, lens, labels, head_gain, pick, pos, ffn_gain[None, :])
 
     line_y = jnp.stack([wo_y, move_a(wo_y, 1), move_a(wo_y, 2), move_a(wo_y, -1)])
     line_y, wq = lax.optimization_barrier((line_y, wq))
     square = (line_y, move_b(line_y, 1), move_b(line_y, 2), move_b(line_y, -1))
     q1, q3 = move_a(wq, 1), move_a(wq, -1)
     square, q1, q3 = lax.optimization_barrier((square, q1, q3))
-    wo_all = lax.all_gather(jnp.concatenate(square), "grp", axis=0, tiled=True)
-    wo_all = wo_all.reshape((SIDE, SIDE * SIDE) + wo_y.shape)
+    q1, q2, q3 = lax.optimization_barrier((q1, move_a(wq, 2), q3))
+    wo_all = lax.all_gather(arrange(pos, square), "grp", axis=0, tiled=True)
+    wo_all = wo_all.reshape(SIDE, -1, WY)
     low = jnp.stack([wq, q1])
-    high = jnp.stack([move_a(wq, 2), q3])
+    high = jnp.stack([q2, q3])
     up = [move_b(low, 1), move_b(high, 1)]
     down = [move_b(low, -1), move_b(high, -1)]
-    up[0], early = lax.optimization_barrier((up[0], early))
+    up[0], x_own, x_other, early = lax.optimization_barrier((up[0], x_own, x_other, early))
     far = [move_b(up[0], 1), move_b(down[1], -1)]
     pieces = [low, high] + up + far + down
-    (
-        x_own, x_other, seg_col, seg_row, members, lens, labels, head_gain, pick,
-        tables, tables_t, pos, ffn_row,
-    ) = early
-
-    part = qkv_first(tables, x_own, x_other, pieces[:4] + pieces[6:], QKV_COLS)
-    att = qkv_last(tables, x_own, x_other, seg_col, seg_row, part, far)
+    seg_col, seg_row, members, lens, labels, head_gain, pick, pos, ffn_row = early
+
+    part = qkv_first(pos, x_own, x_other, pieces[:4] + pieces[6:], QKV_COLS)
+    att = qkv_last(pos, x_own, x_other, seg_col, seg_row, part, far)
     att_in = swap(att)
     st_own, st_other, pool_own, pool_other = page_out(
-        tables, pos, tokens, tok_other, att, att_in, members, lens, wo_all, pieces
+        pos, tokens, tok_other, att, att_in, members, lens, wo_all, pieces
     )
 
     def side_by_side(mine, got):
@@ -581,7 +585,7 @@
     pieces = (line, move_b(line, 1), move_b(line, 2), move_b(line, -1))
     pieces_t = tuple(swap(v) for v in pieces)
     own, other, states = feed_forward(
-        tables, tables_t, pos, pieces, pieces_t, ffn_row, gate_up_weight, w_down, pick
+        pos, pieces, pieces_t, ffn_row, gate_up_weight, w_down, pick
     )
     got = swap(other)
 

time: 209 us -> 204 us (0.976)
  waiting for transfers between devices: 55.4 us -> 64.7 us
  starting transfers between devices: 49.4 us -> 40.6 us
  other arithmetic: 9.26 us -> 5.35 us
    ppermute x12, waiting for transfers between devices: 23 us -> 28.5 us  [move_a(): lax.ppermute(v, 'page', chip_perm(lambda x, z, c: (x + k, z, c) if c == 0...]
    ppermute x12, starting transfers between devices: 18.8 us -> 14.8 us  [move_a(): lax.ppermute(v, 'page', chip_perm(lambda x, z, c: (x + k, z, c) if c == 0...]
    ppermute x15, starting transfers between devices: 27.1 us -> 23.2 us  [move_b(): lax.ppermute(v, 'page', chip_perm(lambda x, z, c: (x, z + k, c) if c == 0...]
    ppermute x15, waiting for transfers between devices: 26.4 us -> 28.7 us  [move_b(): lax.ppermute(v, 'page', chip_perm(lambda x, z, c: (x, z + k, c) if c == 0...]
    unnamed x32 -> x36, local copies, waits for them, and re-layouts: 6.41 us -> 5.12 us
  transfers between devices with their start and end apart: 40 -> 40, of which waited for: 26 -> 28; matrix products, arithmetic and copies ran while one was open for 5% -> 3% of each run, Pallas kernels for 11% -> 11%
where the time goes in v3:
time: 204 us; the launch traced here: 203 us
  waiting for transfers between devices  64.7 us (32%)
  Pallas kernels  44.6 us (22%)
  starting transfers between devices  40.6 us (20%)
  blocking collectives  24.8 us (12%)
  between operations  14.5 us (7%)
  local copies, waits for them, and re-layouts  9.03 us (4%)
  other arithmetic  5.35 us (3%)
    ppermute x15, waiting for transfers between devices, move_b(): lax.ppermute(v, 'page', chip_perm(lambda x, z, c: (x, z + k, c) if c == 0...  28.7 us
    ppermute x12, waiting for transfers between devices, move_a(): lax.ppermute(v, 'page', chip_perm(lambda x, z, c: (x + k, z, c) if c == 0...  28.5 us
    all_to_all x1, blocking collectives, on_device(): lax.all_to_all(blocks, ('grp', 'page'), split_axis=0, concat_axis=0, tile...  24.8 us
    ppermute x15, starting transfers between devices, move_b(): lax.ppermute(v, 'page', chip_perm(lambda x, z, c: (x, z + k, c) if c == 0...  23.2 us
    ppermute x12, starting transfers between devices, move_a(): lax.ppermute(v, 'page', chip_perm(lambda x, z, c: (x + k, z, c) if c == 0...  14.8 us
    pallas_call x1, Pallas kernels, page_out(): pl.pallas_call(out_kernel, out_shape=(st, st, pool, pool), in_specs=[smem...  10.6 us
    pallas_call x1, Pallas kernels, qkv_first(): pl.pallas_call(qkv_first_kernel, out_shape=jax.ShapeDtypeStruct((2 * toke...  8.56 us
    pallas_call x1, Pallas kernels, feed_forward(): pl.pallas_call(ffn_kernel, out_shape=(part, part, jax.ShapeDtypeStruct((p...  8.36 us
  transfers between devices with their start and end apart: 40, of which 28 were waited for; matrix products, arithmetic and copies ran while one was open for 3% of the time, Pallas kernels for 11%

profile of v3, /device:TPU:0, one launch (start us, length us, event | category | flops | bytes accessed | tf_op | source)
XLA Modules:
  0.0 203.5 jit_solution(17652892179541489137)
XLA Ops:
  11.2 2.9 %collective-permute-start.3 = (bf16[112,384]{1,0:T(8,128)(2,1)S(1)}, bf16[112,384]{1,0:T(8,128)(2,1)S(1)}, u32[]{:S(2)}, u32[]{:S(2)}) collective-permute-start(bf16[112,384]{1,0:T(8,128)(2,1)S(1)} %fusion.19), channel_id=1, source_target_pairs={{0,24},{1,7},{2,26},{3,1},{4,28},{5,3},{6,30},{7,5},{8,0},{9,15},{... | collective-permute-start | bytes 258056 | tf_op jit(solution)/shard_map/ppermute | solution.py:51
  16.3 3.9 %collective-permute-done.2 = bf16[112,384]{1,0:T(8,128)(2,1)S(1)} collective-permute-done((bf16[112,384]{1,0:T(8,128)(2,1)S(1)}, bf16[112,384]{1,0:T(8,128)(2,1)S(1)}, u32[]{:S(2)}, u32[]{:S(2)}) %collective-permute-start.2) | collective-permute-done | bytes 86048 | tf_op jit(solution)/shard_map/ppermute | solution.py:51
  21.4 3.2 %collective-permute-start.9 = (bf16[224,1280]{1,0:T(8,128)(2,1)S(1)}, bf16[224,1280]{1,0:T(8,128)(2,1)S(1)}, u32[]{:S(2)}, u32[]{:S(2)}) collective-permute-start(bf16[224,1280]{1,0:T(8,128)(2,1)S(1)} %fusion.7), channel_id=1, source_target_pairs={{0,24},{1,7},{2,26},{3,1},{4,28},{5,3},{6,30},{7,5},{8,0},{9,15},{... | collective-permute-start | bytes 1720328 | tf_op jit(solution)/shard_map/ppermute | solution.py:51
  24.6 1.9 collective-permute-start.5
  26.5 3.6 %collective-permute-start.6 = (bf16[4,112,384]{2,1,0:T(8,128)(2,1)S(1)}, bf16[4,112,384]{2,1,0:T(8,128)(2,1)S(1)}, u32[]{:S(2)}, u32[]{:S(2)}) collective-permute-start(bf16[4,112,384]{2,1,0:T(8,128)(2,1)S(1)} %pad_maximum_fusion.3.t), channel_id=1, source_target_pairs={{0,4},{1,17},{2,6},{3,19},{4,0},{5,21},{6,2},{7,23},{8,12},{9,25},... | collective-permute-start | bytes 1032200 | tf_op jit(solution)/shard_map/ppermute | solution.py:57
  31.2 3.9 %collective-permute-done.5.b1 = bf16[4,112,384]{2,1,0:T(8,128)(2,1)S(1)} collective-permute-done((bf16[4,112,384]{2,1,0:T(8,128)(2,1)S(1)}, bf16[4,112,384]{2,1,0:T(8,128)(2,1)S(1)}, u32[]{:S(2)}, u32[]{:S(2)}) %collective-permute-start.5) | collective-permute-done | bytes 344096 | tf_op jit(solution)/shard_map/ppermute | solution.py:57
  35.1 3.9 %collective-permute-done.6.b2 = bf16[4,112,384]{2,1,0:T(8,128)(2,1)S(1)} collective-permute-done((bf16[4,112,384]{2,1,0:T(8,128)(2,1)S(1)}, bf16[4,112,384]{2,1,0:T(8,128)(2,1)S(1)}, u32[]{:S(2)}, u32[]{:S(2)}) %collective-permute-start.6) | collective-permute-done | bytes 344096 | tf_op jit(solution)/shard_map/ppermute | solution.py:57
  39.7 1.8 shard_map.135
  41.5 1.7 collective-permute-start.10
  43.8 9.0 %collective-permute-done.10 = bf16[224,1280]{1,0:T(8,128)(2,1)S(1)} collective-permute-done((bf16[224,1280]{1,0:T(8,128)(2,1)S(1)}, bf16[224,1280]{1,0:T(8,128)(2,1)S(1)}, u32[]{:S(2)}, u32[]{:S(2)}) %collective-permute-start.10) | collective-permute-done | bytes 573472 | tf_op jit(solution)/shard_map/ppermute | solution.py:51
  55.1 2.3 %collective-permute-start.16 = (bf16[2,224,1280]{2,1,0:T(8,128)(2,1)}, bf16[2,224,1280]{2,1,0:T(8,128)(2,1)}, u32[]{:S(2)}, u32[]{:S(2)}) collective-permute-start(bf16[2,224,1280]{2,1,0:T(8,128)(2,1)} %pad_maximum_fusion.2.refs_1_), channel_id=1, source_target_pairs={{0,6},{1,25},{2,0},{3,27},{4,2},{5,29},{6,4},{7,31},{8,14},{9,1},{... | collective-permute-start | bytes 3440648 | tf_op jit(solution)/shard_map/ppermute | solution.py:57
  57.7 3.8 %shard_map.131.xo = bf16[16,256,256]{2,1,0:T(8,128)(2,1)S(1)} custom-call(bf16[256,3584]{1,0:T(8,128)(2,1)} %tok_own.1, f32[1,3584]{1,0:T(1,128)S(1)} %broadcast_in_dim.14.gain), custom_call_target="tpu_custom_call" | custom-call | bytes 3670016 | tf_op jit(solution)/shard_map/pallas_call | solution.py:111
  62.8 3.2 %collective-permute-start.15 = (bf16[2,224,1280]{2,1,0:T(8,128)(2,1)S(1)}, bf16[2,224,1280]{2,1,0:T(8,128)(2,1)}, u32[]{:S(2)}, u32[]{:S(2)}) collective-permute-start(bf16[2,224,1280]{2,1,0:T(8,128)(2,1)S(1)} %pad_maximum_fusion.1.refs_0_), channel_id=1, source_target_pairs={{0,6},{1,25},{2,0},{3,27},{4,2},{5,29},{6,4},{7,31},{8,14},{9,1},{... | collective-permute-start | bytes 3440648 | tf_op jit(solution)/shard_map/ppermute | solution.py:57
  66.7 3.8 %shard_map.132.xt = bf16[16,256,256]{2,1,0:T(8,128)(2,1)S(1)} custom-call(bf16[256,3584]{1,0:T(8,128)(2,1)} %collective-permute-done.12.tok.tok_other, f32[1,3584]{1,0:T(1,128)S(1)} %broadcast_in_dim.14.gain), custom_call_target="tpu_custom_call" | custom-call | bytes 3670016 | tf_op jit(solution)/shard_map/pallas_call | solution.py:111
  71.9 3.2 %collective-permute-start.18 = (bf16[2,224,1280]{2,1,0:T(8,128)(2,1)}, bf16[2,224,1280]{2,1,0:T(8,128)(2,1)}, u32[]{:S(2)}, u32[]{:S(2)}) collective-permute-start(bf16[2,224,1280]{2,1,0:T(8,128)(2,1)} %collective-permute-done.16.refs_5_.refs_7_), channel_id=1, source_target_pairs={{0,6},{1,25},{2,0},{3,27},{4,2},{5,29},{6,4},{7,31},{8,14},{9,1},{... | collective-permute-start | bytes 3440648 | tf_op jit(solution)/shard_map/ppermute | solution.py:57
  75.9 6.5 %collective-permute-done.14.refs_3_ = bf16[2,224,1280]{2,1,0:T(8,128)(2,1)} collective-permute-done((bf16[2,224,1280]{2,1,0:T(8,128)(2,1)}, bf16[2,224,1280]{2,1,0:T(8,128)(2,1)}, u32[]{:S(2)}, u32[]{:S(2)}) %collective-permute-start.14) | collective-permute-done | bytes 1146912 | tf_op jit(solution)/shard_map/ppermute | solution.py:57
  85.1 8.6 %shard_map.133.part = f32[512,1152]{1,0:T(8,128)S(1)} custom-call(s32[4]{0:T(128)S(1)} %pad_add_fusion.2.pos, bf16[16,256,256]{2,1,0:T(8,128)(2,1)S(1)} %shard_map.131.xo, bf16[16,256,256]{2,1,0:T(8,128)(2,1)S(1)} %copy-done.1, bf16[2,224,1280]{2,1,0:T(8,128)(2,1)S(1)} %pad_maximum_fusion.1.refs_0_, bf16[2,224,1280]{2,1,0:T(8,128)(2,1)} %pad_maximum_fusion.2.refs_1_, ...), custom_call_target="tpu_custom_call" | custom-call | flops 3623878656 | bytes 7077888 | tf_op jit(solution)/shard_map/pallas_call | solution.py:188
  95.8 6.1 %shard_map.134.att = bf16[512,896]{1,0:T(8,128)(2,1)S(1)} custom-call(s32[4]{0:T(128)S(1)} %pad_add_fusion.2.pos, bf16[16,256,256]{2,1,0:T(8,128)(2,1)S(1)} %shard_map.131.xo, bf16[16,256,256]{2,1,0:T(8,128)(2,1)S(1)} %copy-done.1, s32[512,1]{1,0:T(8,128)S(1)} %copy.36.seg_col, s32[2,1,256]{2,1,0:T(1,128)S(1)} %broadcast_in_dim.16.seg_row, ...), custom_call_target="tpu_custom_call" | custom-call | flops 2415919104 | bytes 7077888 | tf_op jit(solution)/shard_map/pallas_call | solution.py:208
  105.8 10.6 %shard_map.136 = (bf16[256,1792]{1,0:T(8,128)(2,1)S(1)}, bf16[256,1792]{1,0:T(8,128)(2,1)S(1)}, bf16[8,1792]{1,0:T(8,128)(2,1)S(1)}, bf16[8,1792]{1,0:T(8,128)(2,1)S(1)}) custom-call(s32[4]{0:T(128)S(1)} %pad_add_fusion.2.pos, bf16[256,3584]{1,0:T(8,128)(2,1)} %tok_own.1, bf16[256,3584]{1,0:T(8,128)(2,1)} %collective-permute-done.12.tok.tok_other, ...), custom_call_target="tpu_custom_call" | custom-call | flops 3288334336 | bytes 6422528 | tf_op jit(solution)/shard_map/pallas_call | solution.py:310
  117.9 24.8 %all_to_all.5 = bf16[128,8,256]{2,1,0:T(8,128)(2,1)S(1)} all-to-all(bf16[128,8,256]{2,1,0:T(8,128)(2,1)S(1)} %bitcast.63), channel_id=1, replica_groups=mesh['grp'=4,'page'=32] {'grp','page'}, dimensions={0} | all-to-all | bytes 1048576 | tf_op jit(solution)/shard_map/all_to_all | solution.py:581
  145.3 1.7 collective-permute-start.23
  148.6 2.5 %collective-permute-done.23 = bf16[256,128]{1,0:T(8,128)(2,1)S(1)} collective-permute-done((bf16[256,128]{1,0:T(8,128)(2,1)S(1)}, bf16[256,128]{1,0:T(8,128)(2,1)S(1)}, u32[]{:S(2)}, u32[]{:S(2)}) %collective-permute-start.23) | collective-permute-done | bytes 65568 | tf_op jit(solution)/shard_map/ppermute | solution.py:51
  152.6 1.7 collective-permute-start.26
  154.2 1.7 collective-permute-start.27
  155.9 7.0 %collective-permute-done.25.b1 = bf16[4,256,128]{2,1,0:T(8,128)(2,1)S(1)} collective-permute-done((bf16[4,256,128]{2,1,0:T(8,128)(2,1)S(1)}, bf16[4,256,128]{2,1,0:T(8,128)(2,1)S(1)}, u32[]{:S(2)}, u32[]{:S(2)}) %collective-permute-start.25) | collective-permute-done | bytes 262176 | tf_op jit(solution)/shard_map/ppermute | solution.py:57
  165.4 8.4 %shard_map.139 = (bf16[4,4,8,3584]{3,2,1,0:T(8,128)(2,1)S(1)}, bf16[4,4,8,3584]{3,2,1,0:T(8,128)(2,1)S(1)}, f32[8,3584]{1,0:T(8,128)S(1)}) custom-call(s32[4]{0:T(128)S(1)} %pad_add_fusion.2.pos, bf16[4,256,128]{2,1,0:T(8,128)(2,1)S(1)} %pad_maximum_fusion.4.t, bf16[4,256,128]{2,1,0:T(8,128)(2,1)S(1)} %collective-permute-done.25.b1, ...), custom_call_target="tpu_custom_call" | custom-call | flops 2818572288 | bytes 11010048 | tf_op jit(solution)/shard_map/pallas_call | solution.py:451
  174.4 2.0 collective-permute-done.32
  179.1 3.5 %collective-permute-done.35 = bf16[4,8,3584]{2,1,0:T(8,128)(2,1)S(1)} collective-permute-done((bf16[4,8,3584]{2,1,0:T(8,128)(2,1)S(1)}, bf16[4,8,3584]{2,1,0:T(8,128)(2,1)S(1)}, u32[]{:S(2)}, u32[]{:S(2)}) %collective-permute-start.35) | collective-permute-done | bytes 229408 | tf_op jit(solution)/shard_map/ppermute | solution.py:51
  182.6 2.4 %collective-permute-done.34 = bf16[4,8,3584]{2,1,0:T(8,128)(2,1)S(1)} collective-permute-done((bf16[4,8,3584]{2,1,0:T(8,128)(2,1)S(1)}, bf16[4,8,3584]{2,1,0:T(8,128)(2,1)S(1)}, u32[]{:S(2)}, u32[]{:S(2)}) %collective-permute-start.34) | collective-permute-done | bytes 229408 | tf_op jit(solution)/shard_map/ppermute | solution.py:51
  185.0 2.4 %collective-permute-done.33 = bf16[4,8,3584]{2,1,0:T(8,128)(2,1)S(1)} collective-permute-done((bf16[4,8,3584]{2,1,0:T(8,128)(2,1)S(1)}, bf16[4,8,3584]{2,1,0:T(8,128)(2,1)S(1)}, u32[]{:S(2)}, u32[]{:S(2)}) %collective-permute-start.33) | collective-permute-done | bytes 229408 | tf_op jit(solution)/shard_map/ppermute | solution.py:51
  187.5 2.4 %collective-permute-start.38 = (bf16[8,3584]{1,0:T(8,128)(2,1)S(1)}, bf16[8,3584]{1,0:T(8,128)(2,1)S(1)}, u32[]{:S(2)}, u32[]{:S(2)}) collective-permute-start(bf16[8,3584]{1,0:T(8,128)(2,1)S(1)} %get-tuple-element.86), channel_id=1, source_target_pairs={{0,6},{1,25},{2,0},{3,27},{4,2},{5,29},{6,4},{7,31},{8,14},{9,1},{... | collective-permute-start | bytes 172040 | tf_op jit(solution)/shard_map/ppermute | solution.py:57
  192.3 3.5 %collective-permute-done.37 = bf16[8,3584]{1,0:T(8,128)(2,1)S(1)} collective-permute-done((bf16[8,3584]{1,0:T(8,128)(2,1)S(1)}, bf16[8,3584]{1,0:T(8,128)(2,1)S(1)}, u32[]{:S(2)}, u32[]{:S(2)}) %collective-permute-start.37) | collective-permute-done | bytes 57376 | tf_op jit(solution)/shard_map/ppermute | solution.py:57
  (140 shorter events, 41.3 us)
Async XLA Ops:
  7.2 97.4 %all-gather.2.cloned.1.call-start = ((), (), s32[]{:S(2)}) async-start(), calls=%async_computation.1 | async-start | bytes 6881280 | tf_op jit(solution)/shard_map/all_gather | solution.py:553
  10.9 10.2 %collective-permute-start.4 = (bf16[112,1152]{1,0:T(8,128)(2,1)S(1)}, bf16[112,1152]{1,0:T(8,128)(2,1)S(1)}, u32[]{:S(2)}, u32[]{:S(2)}) collective-permute-start(bf16[112,1152]{1,0:T(8,128)(2,1)S(1)} %pad_maximum_fusion.6), channel_id=1, source_target_pairs={{0,1},{1,0},{2,3},{3,2},{4,5},{5,4},{6,7},{7,6},{8,9},{9,8},{10,11... | collective-permute-start | bytes 774152 | tf_op jit(solution)/shard_map/ppermute | solution.py:47
  11.2 5.0 %collective-permute-start.3 = (bf16[112,384]{1,0:T(8,128)(2,1)S(1)}, bf16[112,384]{1,0:T(8,128)(2,1)S(1)}, u32[]{:S(2)}, u32[]{:S(2)}) collective-permute-start(bf16[112,384]{1,0:T(8,128)(2,1)S(1)} %fusion.19), channel_id=1, source_target_pairs={{0,24},{1,7},{2,26},{3,1},{4,28},{5,3},{6,30},{7,5},{8,0},{9,15},{... | collective-permute-start | bytes 258056 | tf_op jit(solution)/shard_map/ppermute | solution.py:51
  14.2 6.0 %collective-permute-start.2 = (bf16[112,384]{1,0:T(8,128)(2,1)S(1)}, bf16[112,384]{1,0:T(8,128)(2,1)S(1)}, u32[]{:S(2)}, u32[]{:S(2)}) collective-permute-start(bf16[112,384]{1,0:T(8,128)(2,1)S(1)} %fusion.19), channel_id=1, source_target_pairs={{0,16},{1,5},{2,18},{3,7},{4,20},{5,1},{6,22},{7,3},{8,24},{9,13},... | collective-permute-start | bytes 258056 | tf_op jit(solution)/shard_map/ppermute | solution.py:51
  15.0 6.1 %collective-permute-start.1 = (bf16[112,384]{1,0:T(8,128)(2,1)S(1)}, bf16[112,384]{1,0:T(8,128)(2,1)S(1)}, u32[]{:S(2)}, u32[]{:S(2)}) collective-permute-start(bf16[112,384]{1,0:T(8,128)(2,1)S(1)} %fusion.19), channel_id=1, source_target_pairs={{0,8},{1,3},{2,10},{3,5},{4,12},{5,7},{6,14},{7,1},{8,16},{9,11},{... | collective-permute-start | bytes 258056 | tf_op jit(solution)/shard_map/ppermute | solution.py:51
  21.3 18.4 %collective-permute-start.8 = (bf16[224,1280]{1,0:T(8,128)(2,1)S(1)}, bf16[224,1280]{1,0:T(8,128)(2,1)S(1)}, u32[]{:S(2)}, u32[]{:S(2)}) collective-permute-start(bf16[224,1280]{1,0:T(8,128)(2,1)S(1)} %fusion.7), channel_id=1, source_target_pairs={{0,8},{1,3},{2,10},{3,5},{4,12},{5,7},{6,14},{7,1},{8,16},{9,11},{... | collective-permute-start | bytes 1720328 | tf_op jit(solution)/shard_map/ppermute | solution.py:51
  21.4 18.3 %collective-permute-start.9 = (bf16[224,1280]{1,0:T(8,128)(2,1)S(1)}, bf16[224,1280]{1,0:T(8,128)(2,1)S(1)}, u32[]{:S(2)}, u32[]{:S(2)}) collective-permute-start(bf16[224,1280]{1,0:T(8,128)(2,1)S(1)} %fusion.7), channel_id=1, source_target_pairs={{0,24},{1,7},{2,26},{3,1},{4,28},{5,3},{6,30},{7,5},{8,0},{9,15},{... | collective-permute-start | bytes 1720328 | tf_op jit(solution)/shard_map/ppermute | solution.py:51
  24.6 10.5 %collective-permute-start.5 = (bf16[4,112,384]{2,1,0:T(8,128)(2,1)S(1)}, bf16[4,112,384]{2,1,0:T(8,128)(2,1)S(1)}, u32[]{:S(2)}, u32[]{:S(2)}) collective-permute-start(bf16[4,112,384]{2,1,0:T(8,128)(2,1)S(1)} %pad_maximum_fusion.3.t), channel_id=1, source_target_pairs={{0,2},{1,9},{2,4},{3,11},{4,6},{5,13},{6,0},{7,15},{8,10},{9,17},{... | collective-permute-start | bytes 1032200 | tf_op jit(solution)/shard_map/ppermute | solution.py:57
  26.5 12.5 %collective-permute-start.6 = (bf16[4,112,384]{2,1,0:T(8,128)(2,1)S(1)}, bf16[4,112,384]{2,1,0:T(8,128)(2,1)S(1)}, u32[]{:S(2)}, u32[]{:S(2)}) collective-permute-start(bf16[4,112,384]{2,1,0:T(8,128)(2,1)S(1)} %pad_maximum_fusion.3.t), channel_id=1, source_target_pairs={{0,4},{1,17},{2,6},{3,19},{4,0},{5,21},{6,2},{7,23},{8,12},{9,25},... | collective-permute-start | bytes 1032200 | tf_op jit(solution)/shard_map/ppermute | solution.py:57
  30.1 8.9 %collective-permute-start.7 = (bf16[4,112,384]{2,1,0:T(8,128)(2,1)S(1)}, bf16[4,112,384]{2,1,0:T(8,128)(2,1)S(1)}, u32[]{:S(2)}, u32[]{:S(2)}) collective-permute-start(bf16[4,112,384]{2,1,0:T(8,128)(2,1)S(1)} %pad_maximum_fusion.3.t), channel_id=1, source_target_pairs={{0,6},{1,25},{2,0},{3,27},{4,2},{5,29},{6,4},{7,31},{8,14},{9,1},{... | collective-permute-start | bytes 1032200 | tf_op jit(solution)/shard_map/ppermute | solution.py:57
  41.5 11.3 %collective-permute-start.10 = (bf16[224,1280]{1,0:T(8,128)(2,1)S(1)}, bf16[224,1280]{1,0:T(8,128)(2,1)S(1)}, u32[]{:S(2)}, u32[]{:S(2)}) collective-permute-start(bf16[224,1280]{1,0:T(8,128)(2,1)S(1)} %fusion.7), channel_id=1, source_target_pairs={{0,16},{1,5},{2,18},{3,7},{4,20},{5,1},{6,22},{7,3},{8,24},{9,13},... | collective-permute-start | bytes 1720328 | tf_op jit(solution)/shard_map/ppermute | solution.py:51
  43.1 23.6 %collective-permute-start.12 = (bf16[256,3584]{1,0:T(8,128)(2,1)}, bf16[256,3584]{1,0:T(8,128)(2,1)}, u32[]{:S(2)}, u32[]{:S(2)}) collective-permute-start(bf16[256,3584]{1,0:T(8,128)(2,1)} %tok_own.1), channel_id=1, source_target_pairs={{0,1},{1,0},{2,3},{3,2},{4,5},{5,4},{6,7},{7,6},{8,9},{9,8},{10,11... | collective-permute-start | bytes 5505032 | tf_op jit(solution)/shard_map/ppermute | solution.py:47
  43.8 18.7 %collective-permute-start.13 = (s32[1,8]{1,0:T(1,128)S(1)}, s32[1,8]{1,0:T(1,128)S(1)}, u32[]{:S(2)}, u32[]{:S(2)}) collective-permute-start(s32[1,8]{1,0:T(1,128)S(1)} %copy-done.16), channel_id=1, source_target_pairs={{0,1},{1,0},{2,3},{3,2},{4,5},{5,4},{6,7},{7,6},{8,9},{9,8},{10,11... | collective-permute-start | bytes 104 | tf_op jit(solution)/shard_map/ppermute | solution.py:47
  52.9 19.0 %collective-permute-start.11 = (bf16[2,224,1280]{2,1,0:T(8,128)(2,1)S(1)}, bf16[2,224,1280]{2,1,0:T(8,128)(2,1)}, u32[]{:S(2)}, u32[]{:S(2)}) collective-permute-start(bf16[2,224,1280]{2,1,0:T(8,128)(2,1)S(1)} %pad_maximum_fusion.1.refs_0_), channel_id=1, source_target_pairs={{0,2},{1,9},{2,4},{3,11},{4,6},{5,13},{6,0},{7,15},{8,10},{9,17},{... | collective-permute-start | bytes 3440648 | tf_op jit(solution)/shard_map/ppermute | solution.py:57
  55.1 16.8 %collective-permute-start.16 = (bf16[2,224,1280]{2,1,0:T(8,128)(2,1)}, bf16[2,224,1280]{2,1,0:T(8,128)(2,1)}, u32[]{:S(2)}, u32[]{:S(2)}) collective-permute-start(bf16[2,224,1280]{2,1,0:T(8,128)(2,1)} %pad_maximum_fusion.2.refs_1_), channel_id=1, source_target_pairs={{0,6},{1,25},{2,0},{3,27},{4,2},{5,29},{6,4},{7,31},{8,14},{9,1},{... | collective-permute-start | bytes 3440648 | tf_op jit(solution)/shard_map/ppermute | solution.py:57
  62.8 19.6 %collective-permute-start.14 = (bf16[2,224,1280]{2,1,0:T(8,128)(2,1)}, bf16[2,224,1280]{2,1,0:T(8,128)(2,1)}, u32[]{:S(2)}, u32[]{:S(2)}) collective-permute-start(bf16[2,224,1280]{2,1,0:T(8,128)(2,1)} %pad_maximum_fusion.2.refs_1_), channel_id=1, source_target_pairs={{0,2},{1,9},{2,4},{3,11},{4,6},{5,13},{6,0},{7,15},{8,10},{9,17},{... | collective-permute-start | bytes 3440648 | tf_op jit(solution)/shard_map/ppermute | solution.py:57
  62.8 20.7 %collective-permute-start.15 = (bf16[2,224,1280]{2,1,0:T(8,128)(2,1)S(1)}, bf16[2,224,1280]{2,1,0:T(8,128)(2,1)}, u32[]{:S(2)}, u32[]{:S(2)}) collective-permute-start(bf16[2,224,1280]{2,1,0:T(8,128)(2,1)S(1)} %pad_maximum_fusion.1.refs_0_), channel_id=1, source_target_pairs={{0,6},{1,25},{2,0},{3,27},{4,2},{5,29},{6,4},{7,31},{8,14},{9,1},{... | collective-permute-start | bytes 3440648 | tf_op jit(solution)/shard_map/ppermute | solution.py:57
  71.8 22.8 %collective-permute-start.17 = (bf16[2,224,1280]{2,1,0:T(8,128)(2,1)}, bf16[2,224,1280]{2,1,0:T(8,128)(2,1)}, u32[]{:S(2)}, u32[]{:S(2)}) collective-permute-start(bf16[2,224,1280]{2,1,0:T(8,128)(2,1)} %collective-permute-done.11.refs_2_), channel_id=1, source_target_pairs={{0,2},{1,9},{2,4},{3,11},{4,6},{5,13},{6,0},{7,15},{8,10},{9,17},{... | collective-permute-start | bytes 3440648 | tf_op jit(solution)/shard_map/ppermute | solution.py:57
  71.9 23.9 %collective-permute-start.18 = (bf16[2,224,1280]{2,1,0:T(8,128)(2,1)}, bf16[2,224,1280]{2,1,0:T(8,128)(2,1)}, u32[]{:S(2)}, u32[]{:S(2)}) collective-permute-start(bf16[2,224,1280]{2,1,0:T(8,128)(2,1)} %collective-permute-done.16.refs_5_.refs_7_), channel_id=1, source_target_pairs={{0,6},{1,25},{2,0},{3,27},{4,2},{5,29},{6,4},{7,31},{8,14},{9,1},{... | collective-permute-start | bytes 3440648 | tf_op jit(solution)/shard_map/ppermute | solution.py:57
  145.3 5.8 %collective-permute-start.23 = (bf16[256,128]{1,0:T(8,128)(2,1)S(1)}, bf16[256,128]{1,0:T(8,128)(2,1)S(1)}, u32[]{:S(2)}, u32[]{:S(2)}) collective-permute-start(bf16[256,128]{1,0:T(8,128)(2,1)S(1)} %shard_map.138), channel_id=1, source_target_pairs={{0,16},{1,5},{2,18},{3,7},{4,20},{5,1},{6,22},{7,3},{8,24},{9,13},... | collective-permute-start | bytes 196616 | tf_op jit(solution)/shard_map/ppermute | solution.py:51
  147.0 5.5 %collective-permute-start.22 = (bf16[256,128]{1,0:T(8,128)(2,1)S(1)}, bf16[256,128]{1,0:T(8,128)(2,1)S(1)}, u32[]{:S(2)}, u32[]{:S(2)}) collective-permute-start(bf16[256,128]{1,0:T(8,128)(2,1)S(1)} %shard_map.138), channel_id=1, source_target_pairs={{0,8},{1,3},{2,10},{3,5},{4,12},{5,7},{6,14},{7,1},{8,16},{9,11},{... | collective-permute-start | bytes 196616 | tf_op jit(solution)/shard_map/ppermute | solution.py:51
  152.5 10.5 %collective-permute-start.25 = (bf16[4,256,128]{2,1,0:T(8,128)(2,1)S(1)}, bf16[4,256,128]{2,1,0:T(8,128)(2,1)S(1)}, u32[]{:S(2)}, u32[]{:S(2)}) collective-permute-start(bf16[4,256,128]{2,1,0:T(8,128)(2,1)S(1)} %pad_maximum_fusion.4.t), channel_id=1, source_target_pairs={{0,2},{1,9},{2,4},{3,11},{4,6},{5,13},{6,0},{7,15},{8,10},{9,17},{... | collective-permute-start | bytes 786440 | tf_op jit(solution)/shard_map/ppermute | solution.py:57
  152.6 10.4 %collective-permute-start.26 = (bf16[4,256,128]{2,1,0:T(8,128)(2,1)S(1)}, bf16[4,256,128]{2,1,0:T(8,128)(2,1)S(1)}, u32[]{:S(2)}, u32[]{:S(2)}) collective-permute-start(bf16[4,256,128]{2,1,0:T(8,128)(2,1)S(1)} %pad_maximum_fusion.4.t), channel_id=1, source_target_pairs={{0,4},{1,17},{2,6},{3,19},{4,0},{5,21},{6,2},{7,23},{8,12},{9,25},... | collective-permute-start | bytes 786440 | tf_op jit(solution)/shard_map/ppermute | solution.py:57
  154.2 9.6 %collective-permute-start.27 = (bf16[4,256,128]{2,1,0:T(8,128)(2,1)S(1)}, bf16[4,256,128]{2,1,0:T(8,128)(2,1)S(1)}, u32[]{:S(2)}, u32[]{:S(2)}) collective-permute-start(bf16[4,256,128]{2,1,0:T(8,128)(2,1)S(1)} %pad_maximum_fusion.4.t), channel_id=1, source_target_pairs={{0,6},{1,25},{2,0},{3,27},{4,2},{5,29},{6,4},{7,31},{8,14},{9,1},{... | collective-permute-start | bytes 786440 | tf_op jit(solution)/shard_map/ppermute | solution.py:57
  155.9 7.9 %collective-permute-start.28 = (bf16[4,256,128]{2,1,0:T(8,128)(2,1)S(1)}, bf16[4,256,128]{2,1,0:T(8,128)(2,1)S(1)}, u32[]{:S(2)}, u32[]{:S(2)}) collective-permute-start(bf16[4,256,128]{2,1,0:T(8,128)(2,1)S(1)} %pad_maximum_fusion.4.t), channel_id=1, source_target_pairs={{0,1},{1,0},{2,3},{3,2},{4,5},{5,4},{6,7},{7,6},{8,9},{9,8},{10,11... | collective-permute-start | bytes 786440 | tf_op jit(solution)/shard_map/ppermute | solution.py:47
  174.0 5.0 %collective-permute-start.20 = (bf16[256,1792]{1,0:T(8,128)(2,1)S(1)}, bf16[256,1792]{1,0:T(8,128)(2,1)S(1)}, u32[]{:S(2)}, u32[]{:S(2)}) collective-permute-start(bf16[256,1792]{1,0:T(8,128)(2,1)S(1)} %get-tuple-element.62), channel_id=1, source_target_pairs={{0,1},{1,0},{2,3},{3,2},{4,5},{5,4},{6,7},{7,6},{8,9},{9,8},{10,11... | collective-permute-start | bytes 2752520 | tf_op jit(solution)/shard_map/ppermute | solution.py:47
  176.5 6.1 %collective-permute-start.35 = (bf16[4,8,3584]{2,1,0:T(8,128)(2,1)S(1)}, bf16[4,8,3584]{2,1,0:T(8,128)(2,1)S(1)}, u32[]{:S(2)}, u32[]{:S(2)}) collective-permute-start(bf16[4,8,3584]{2,1,0:T(8,128)(2,1)S(1)} %get-tuple-element.75), channel_id=1, source_target_pairs={{0,24},{1,7},{2,26},{3,1},{4,28},{5,3},{6,30},{7,5},{8,0},{9,15},{... | collective-permute-start | bytes 688136 | tf_op jit(solution)/shard_map/ppermute | solution.py:51
  177.4 7.6 %collective-permute-start.34 = (bf16[4,8,3584]{2,1,0:T(8,128)(2,1)S(1)}, bf16[4,8,3584]{2,1,0:T(8,128)(2,1)S(1)}, u32[]{:S(2)}, u32[]{:S(2)}) collective-permute-start(bf16[4,8,3584]{2,1,0:T(8,128)(2,1)S(1)} %get-tuple-element.76), channel_id=1, source_target_pairs={{0,16},{1,5},{2,18},{3,7},{4,20},{5,1},{6,22},{7,3},{8,24},{9,13},... | collective-permute-start | bytes 688136 | tf_op jit(solution)/shard_map/ppermute | solution.py:51
  178.3 9.1 %collective-permute-start.33 = (bf16[4,8,3584]{2,1,0:T(8,128)(2,1)S(1)}, bf16[4,8,3584]{2,1,0:T(8,128)(2,1)S(1)}, u32[]{:S(2)}, u32[]{:S(2)}) collective-permute-start(bf16[4,8,3584]{2,1,0:T(8,128)(2,1)S(1)} %get-tuple-element.74), channel_id=1, source_target_pairs={{0,8},{1,3},{2,10},{3,5},{4,12},{5,7},{6,14},{7,1},{8,16},{9,11},{... | collective-permute-start | bytes 688136 | tf_op jit(solution)/shard_map/ppermute | solution.py:51
  187.5 4.7 %collective-permute-start.38 = (bf16[8,3584]{1,0:T(8,128)(2,1)S(1)}, bf16[8,3584]{1,0:T(8,128)(2,1)S(1)}, u32[]{:S(2)}, u32[]{:S(2)}) collective-permute-start(bf16[8,3584]{1,0:T(8,128)(2,1)S(1)} %get-tuple-element.86), channel_id=1, source_target_pairs={{0,6},{1,25},{2,0},{3,27},{4,2},{5,29},{6,4},{7,31},{8,14},{9,1},{... | collective-permute-start | bytes 172040 | tf_op jit(solution)/shard_map/ppermute | solution.py:57
  189.9 5.8 %collective-permute-start.37 = (bf16[8,3584]{1,0:T(8,128)(2,1)S(1)}, bf16[8,3584]{1,0:T(8,128)(2,1)S(1)}, u32[]{:S(2)}, u32[]{:S(2)}) collective-permute-start(bf16[8,3584]{1,0:T(8,128)(2,1)S(1)} %get-tuple-element.87), channel_id=1, source_target_pairs={{0,4},{1,17},{2,6},{3,19},{4,0},{5,21},{6,2},{7,23},{8,12},{9,25},... | collective-permute-start | bytes 172040 | tf_op jit(solution)/shard_map/ppermute | solution.py:57
  190.0 6.0 %collective-permute-start.36 = (bf16[8,3584]{1,0:T(8,128)(2,1)S(1)}, bf16[8,3584]{1,0:T(8,128)(2,1)S(1)}, u32[]{:S(2)}, u32[]{:S(2)}) collective-permute-start(bf16[8,3584]{1,0:T(8,128)(2,1)S(1)} %get-tuple-element.85), channel_id=1, source_target_pairs={{0,2},{1,9},{2,4},{3,11},{4,6},{5,13},{6,0},{7,15},{8,10},{9,17},{... | collective-permute-start | bytes 172040 | tf_op jit(solution)/shard_map/ppermute | solution.py:57
  (26 other events, 153.5 us)
Sparse Core Ops, SparseCore 0:
  41.6 60.5 all-gather.1

commit v4 on v3

--- a/solution.py
+++ b/solution.py
@@ -154,9 +154,8 @@
     *pieces, out, w, x, qkv, sems = refs
     qkv_load(pos, (2,), pieces, xo, xt, w, x, sems)
 
-    @pl.loop(0, part.shape[1] // QKV_TILE)
-    def _(n):
-        there = pl.ds(pl.multiple_of(n * QKV_TILE, 128), QKV_TILE)
+    for lo in range(0, part.shape[1], BLOCK):
+        there = slice(lo, min(lo + BLOCK, part.shape[1]))
         last = jnp.dot(x[...], w[:, there], preferred_element_type=F32)
         qkv[:, there] = (part[:, there] + last).astype(BF)
 
@@ -389,28 +388,20 @@
 
 
 def ffn_kernel(
-    pos, t, b1, b2, b3, tt, c1, c2, c3, gain, gate_up, down, pick,
-    own, other, states, x, mixed, hidden, wgu, wd, acc, sems,
+    pos, t, b1, b2, b3, tt, c1, c2, c3, gain, wgu, wd, pick,
+    own, other, states, x, mixed, hidden, acc, sems,
 ):
     core = pos[0]
     width = gain.shape[1]
     units = hidden.shape[1]
     half = units // 2
-    weights = []
-    for n in range(2):
-        for g in range(2):
-            part = (g, slice(None), slice(n * half, (n + 1) * half))
-            weights.append((gate_up.at[part], wgu.at[part]))
-    weights.append((down, wd))
     copies = []
     for side, pieces in ((core, (t, b1, b2, b3)), (1 - core, (tt, c1, c2, c3))):
         for k, piece in enumerate(pieces):
             for j in range(SIDE):
                 head = chip_at(pos, side, j, k, -1) * 2 + side
                 copies.append((piece.at[j], x.at[:, pl.ds(pl.multiple_of(head * HD, HD), HD)]))
-    started = run_copies(copies + weights, sems)
-    weights = started[len(copies) :]
-    for copy in started[: len(copies)]:
+    for copy in run_copies(copies, sems):
         copy.wait()
     chunk = 32
 
@@ -422,13 +413,10 @@
         mixed[rows, :] = (wide * scale * gain[...]).astype(BF)
 
     for n in range(2):
-        weights[2 * n].wait()
-        weights[2 * n + 1].wait()
         cols = slice(n * half, (n + 1) * half)
         gate = jnp.dot(mixed[...], wgu[0, :, cols], preferred_element_type=F32)
         up = jnp.dot(mixed[...], wgu[1, :, cols], preferred_element_type=F32)
         hidden[:, cols] = (gate * jax.nn.sigmoid(gate) * up).astype(BF)
-    weights[4].wait()
     tile = 512
 
     @pl.loop(0, width // tile)
@@ -443,6 +431,24 @@
         states[:, cols] = jnp.dot(pick[...], x[:, cols], preferred_element_type=F32)
 
 
+def load_kernel(src, out, sem):
+    copy = pltpu.make_async_copy(src, out, sem)
+    copy.start()
+    copy.wait()
+
+
+def load_weights(weights):
+    return pl.pallas_call(
+        load_kernel,
+        out_shape=jax.ShapeDtypeStruct(weights.shape, weights.dtype),
+        in_specs=[anym()],
+        out_specs=vmem(),
+        scratch_shapes=[pltpu.SemaphoreType.DMA],
+        compiler_params=params(12),
+        cost_estimate=pl.CostEstimate(flops=0, bytes_accessed=2 * weights.size, transcendentals=0),
+    )(weights)
+
+
 def feed_forward(pos, pieces, pieces_t, gain, gate_up, down, pick):
     width = gain.shape[1]
     units = down.shape[0]
@@ -451,18 +457,16 @@
     return pl.pallas_call(
         ffn_kernel,
         out_shape=(part, part, jax.ShapeDtypeStruct((pages, width), F32)),
-        in_specs=[smem()] + [anym()] * 8 + [vmem()] + [anym()] * 2 + [vmem()],
+        in_specs=[smem()] + [anym()] * 8 + [vmem()] * 4,
         out_specs=(vmem(),) * 3,
         scratch_shapes=[
             pltpu.VMEM((count, 2 * SIDE * SIDE * HD), BF),
             pltpu.VMEM((count, width), BF),
             pltpu.VMEM((count, units), BF),
-            pltpu.VMEM((2, width, units), BF),
-            pltpu.VMEM((units, width), BF),
             pltpu.VMEM((count // pages, pages, 512), F32),
             pltpu.SemaphoreType.DMA((40,)),
         ],
-        compiler_params=params(40),
+        compiler_params=params(12),
         cost_estimate=pl.CostEstimate(
             flops=6 * count * width * units, bytes_accessed=6 * width * units, transcendentals=0
         ),
@@ -579,9 +583,12 @@
     blocks = page_blocks(vectors, labels, slots)
     blocks = jnp.broadcast_to(blocks[None], (SIDE,) + blocks.shape).reshape(-1, pages, 2 * HD)
     gathered = lax.all_to_all(blocks, ("grp", "page"), split_axis=0, concat_axis=0, tiled=True)
+    gathered, gate_up_weight = lax.optimization_barrier((gathered, gate_up_weight))
+    gate_up_weight = load_weights(gate_up_weight)
     mixed = doc_attention(pos, gathered.reshape(-1, 2 * HD), head_gain, plane)
 
     line = jnp.stack([mixed, move_a(mixed, 1), move_a(mixed, 2), move_a(mixed, -1)])
+    line, gate_up_weight = lax.optimization_barrier((line, gate_up_weight))
     pieces = (line, move_b(line, 1), move_b(line, 2), move_b(line, -1))
     pieces_t = tuple(swap(v) for v in pieces)
     own, other, states = feed_forward(

time: 204 us -> 203 us (level)
  waiting for transfers between devices: 64.7 us -> 61 us
  local copies, waits for them, and re-layouts: 9.03 us -> 12.2 us
    ppermute x12, waiting for transfers between devices: 28.5 us -> 24.9 us  [move_a(): lax.ppermute(v, 'page', chip_perm(lambda x, z, c: (x + k, z, c) if c == 0...]
    unnamed x36 -> x38, local copies, waits for them, and re-layouts: 5.12 us -> 8.21 us
  transfers between devices with their start and end apart: 40 -> 40, of which waited for: 28 -> 27; matrix products, arithmetic and copies ran while one was open for 3% -> 3% of each run, Pallas kernels for 11% -> 11%
where the time goes in v4:
time: 203 us
  waiting for transfers between devices  61 us (30%)
  Pallas kernels  43.4 us (21%)
  starting transfers between devices  41.3 us (20%)
  blocking collectives  24.8 us (12%)
  between operations  14.5 us (7%)
  local copies, waits for them, and re-layouts  12.2 us (6%)
  other arithmetic  5.38 us (3%)
    ppermute x15, waiting for transfers between devices, move_b(): lax.ppermute(v, 'page', chip_perm(lambda x, z, c: (x, z + k, c) if c == 0...  28.6 us
    ppermute x12, waiting for transfers between devices, move_a(): lax.ppermute(v, 'page', chip_perm(lambda x, z, c: (x + k, z, c) if c == 0...  24.9 us
    all_to_all x1, blocking collectives, on_device(): lax.all_to_all(blocks, ('grp', 'page'), split_axis=0, concat_axis=0, tile...  24.8 us
    ppermute x15, starting transfers between devices, move_b(): lax.ppermute(v, 'page', chip_perm(lambda x, z, c: (x, z + k, c) if c == 0...  23.3 us
    ppermute x12, starting transfers between devices, move_a(): lax.ppermute(v, 'page', chip_perm(lambda x, z, c: (x + k, z, c) if c == 0...  15.4 us
    pallas_call x1, Pallas kernels, page_out(): pl.pallas_call(out_kernel, out_shape=(st, st, pool, pool), in_specs=[smem...  10.4 us
    pallas_call x1, Pallas kernels, qkv_first(): pl.pallas_call(qkv_first_kernel, out_shape=jax.ShapeDtypeStruct((2 * toke...  8.55 us
    unnamed x38, local copies, waits for them, and re-layouts  8.21 us
  transfers between devices with their start and end apart: 40, of which 27 were waited for; matrix products, arithmetic and copies ran while one was open for 3% of the time, Pallas kernels for 11%

profile of v4, /device:TPU:0, one launch (start us, length us, event | category | flops | bytes accessed | tf_op | source)
XLA Modules:
  0.0 202.6 jit_solution(1549401548824525034)
XLA Ops:
  11.2 2.9 %collective-permute-start.3 = (bf16[112,384]{1,0:T(8,128)(2,1)S(1)}, bf16[112,384]{1,0:T(8,128)(2,1)S(1)}, u32[]{:S(2)}, u32[]{:S(2)}) collective-permute-start(bf16[112,384]{1,0:T(8,128)(2,1)S(1)} %fusion.19), channel_id=1, source_target_pairs={{0,24},{1,7},{2,26},{3,1},{4,28},{5,3},{6,30},{7,5},{8,0},{9,15},{... | collective-permute-start | bytes 258056 | tf_op jit(solution)/shard_map/ppermute | solution.py:51
  16.3 3.9 %collective-permute-done.2 = bf16[112,384]{1,0:T(8,128)(2,1)S(1)} collective-permute-done((bf16[112,384]{1,0:T(8,128)(2,1)S(1)}, bf16[112,384]{1,0:T(8,128)(2,1)S(1)}, u32[]{:S(2)}, u32[]{:S(2)}) %collective-permute-start.2) | collective-permute-done | bytes 86048 | tf_op jit(solution)/shard_map/ppermute | solution.py:51
  21.4 3.2 %collective-permute-start.9 = (bf16[224,1280]{1,0:T(8,128)(2,1)S(1)}, bf16[224,1280]{1,0:T(8,128)(2,1)S(1)}, u32[]{:S(2)}, u32[]{:S(2)}) collective-permute-start(bf16[224,1280]{1,0:T(8,128)(2,1)S(1)} %fusion.7), channel_id=1, source_target_pairs={{0,24},{1,7},{2,26},{3,1},{4,28},{5,3},{6,30},{7,5},{8,0},{9,15},{... | collective-permute-start | bytes 1720328 | tf_op jit(solution)/shard_map/ppermute | solution.py:51
  24.6 1.9 collective-permute-start.5
  26.5 3.6 %collective-permute-start.6 = (bf16[4,112,384]{2,1,0:T(8,128)(2,1)S(1)}, bf16[4,112,384]{2,1,0:T(8,128)(2,1)S(1)}, u32[]{:S(2)}, u32[]{:S(2)}) collective-permute-start(bf16[4,112,384]{2,1,0:T(8,128)(2,1)S(1)} %pad_maximum_fusion.3.t), channel_id=1, source_target_pairs={{0,4},{1,17},{2,6},{3,19},{4,0},{5,21},{6,2},{7,23},{8,12},{9,25},... | collective-permute-start | bytes 1032200 | tf_op jit(solution)/shard_map/ppermute | solution.py:57
  31.2 3.9 %collective-permute-done.5.b1 = bf16[4,112,384]{2,1,0:T(8,128)(2,1)S(1)} collective-permute-done((bf16[4,112,384]{2,1,0:T(8,128)(2,1)S(1)}, bf16[4,112,384]{2,1,0:T(8,128)(2,1)S(1)}, u32[]{:S(2)}, u32[]{:S(2)}) %collective-permute-start.5) | collective-permute-done | bytes 344096 | tf_op jit(solution)/shard_map/ppermute | solution.py:57
  35.1 3.9 %collective-permute-done.6.b2 = bf16[4,112,384]{2,1,0:T(8,128)(2,1)S(1)} collective-permute-done((bf16[4,112,384]{2,1,0:T(8,128)(2,1)S(1)}, bf16[4,112,384]{2,1,0:T(8,128)(2,1)S(1)}, u32[]{:S(2)}, u32[]{:S(2)}) %collective-permute-start.6) | collective-permute-done | bytes 344096 | tf_op jit(solution)/shard_map/ppermute | solution.py:57
  39.7 1.8 shard_map.135
  41.5 1.7 collective-permute-start.10
  43.8 9.0 %collective-permute-done.10 = bf16[224,1280]{1,0:T(8,128)(2,1)S(1)} collective-permute-done((bf16[224,1280]{1,0:T(8,128)(2,1)S(1)}, bf16[224,1280]{1,0:T(8,128)(2,1)S(1)}, u32[]{:S(2)}, u32[]{:S(2)}) %collective-permute-start.10) | collective-permute-done | bytes 573472 | tf_op jit(solution)/shard_map/ppermute | solution.py:51
  55.1 2.3 %collective-permute-start.16 = (bf16[2,224,1280]{2,1,0:T(8,128)(2,1)}, bf16[2,224,1280]{2,1,0:T(8,128)(2,1)}, u32[]{:S(2)}, u32[]{:S(2)}) collective-permute-start(bf16[2,224,1280]{2,1,0:T(8,128)(2,1)} %pad_maximum_fusion.2.refs_1_), channel_id=1, source_target_pairs={{0,6},{1,25},{2,0},{3,27},{4,2},{5,29},{6,4},{7,31},{8,14},{9,1},{... | collective-permute-start | bytes 3440648 | tf_op jit(solution)/shard_map/ppermute | solution.py:57
  57.7 3.8 %shard_map.131.xo = bf16[16,256,256]{2,1,0:T(8,128)(2,1)S(1)} custom-call(bf16[256,3584]{1,0:T(8,128)(2,1)} %tok_own.1, f32[1,3584]{1,0:T(1,128)S(1)} %broadcast_in_dim.14.gain), custom_call_target="tpu_custom_call" | custom-call | bytes 3670016 | tf_op jit(solution)/shard_map/pallas_call | solution.py:111
  62.8 3.2 %collective-permute-start.15 = (bf16[2,224,1280]{2,1,0:T(8,128)(2,1)S(1)}, bf16[2,224,1280]{2,1,0:T(8,128)(2,1)}, u32[]{:S(2)}, u32[]{:S(2)}) collective-permute-start(bf16[2,224,1280]{2,1,0:T(8,128)(2,1)S(1)} %pad_maximum_fusion.1.refs_0_), channel_id=1, source_target_pairs={{0,6},{1,25},{2,0},{3,27},{4,2},{5,29},{6,4},{7,31},{8,14},{9,1},{... | collective-permute-start | bytes 3440648 | tf_op jit(solution)/shard_map/ppermute | solution.py:57
  66.8 3.8 %shard_map.132.xt = bf16[16,256,256]{2,1,0:T(8,128)(2,1)S(1)} custom-call(bf16[256,3584]{1,0:T(8,128)(2,1)} %collective-permute-done.12.tok.tok_other, f32[1,3584]{1,0:T(1,128)S(1)} %broadcast_in_dim.14.gain), custom_call_target="tpu_custom_call" | custom-call | bytes 3670016 | tf_op jit(solution)/shard_map/pallas_call | solution.py:111
  71.9 3.2 %collective-permute-start.18 = (bf16[2,224,1280]{2,1,0:T(8,128)(2,1)}, bf16[2,224,1280]{2,1,0:T(8,128)(2,1)}, u32[]{:S(2)}, u32[]{:S(2)}) collective-permute-start(bf16[2,224,1280]{2,1,0:T(8,128)(2,1)} %collective-permute-done.16.refs_5_.refs_7_), channel_id=1, source_target_pairs={{0,6},{1,25},{2,0},{3,27},{4,2},{5,29},{6,4},{7,31},{8,14},{9,1},{... | collective-permute-start | bytes 3440648 | tf_op jit(solution)/shard_map/ppermute | solution.py:57
  76.0 6.4 %collective-permute-done.14.refs_3_ = bf16[2,224,1280]{2,1,0:T(8,128)(2,1)} collective-permute-done((bf16[2,224,1280]{2,1,0:T(8,128)(2,1)}, bf16[2,224,1280]{2,1,0:T(8,128)(2,1)}, u32[]{:S(2)}, u32[]{:S(2)}) %collective-permute-start.14) | collective-permute-done | bytes 1146912 | tf_op jit(solution)/shard_map/ppermute | solution.py:57
  85.1 8.6 %shard_map.133.part = f32[512,1152]{1,0:T(8,128)S(1)} custom-call(s32[4]{0:T(128)S(1)} %pad_add_fusion.2.pos, bf16[16,256,256]{2,1,0:T(8,128)(2,1)S(1)} %shard_map.131.xo, bf16[16,256,256]{2,1,0:T(8,128)(2,1)S(1)} %copy-done.1, bf16[2,224,1280]{2,1,0:T(8,128)(2,1)S(1)} %pad_maximum_fusion.1.refs_0_, bf16[2,224,1280]{2,1,0:T(8,128)(2,1)} %pad_maximum_fusion.2.refs_1_, ...), custom_call_target="tpu_custom_call" | custom-call | flops 3623878656 | bytes 7077888 | tf_op jit(solution)/shard_map/pallas_call | solution.py:187
  95.8 5.5 %shard_map.134.att = bf16[512,896]{1,0:T(8,128)(2,1)S(1)} custom-call(s32[4]{0:T(128)S(1)} %pad_add_fusion.2.pos, bf16[16,256,256]{2,1,0:T(8,128)(2,1)S(1)} %shard_map.131.xo, bf16[16,256,256]{2,1,0:T(8,128)(2,1)S(1)} %copy-done.1, s32[512,1]{1,0:T(8,128)S(1)} %copy.36.seg_col, s32[2,1,256]{2,1,0:T(1,128)S(1)} %broadcast_in_dim.16.seg_row, ...), custom_call_target="tpu_custom_call" | custom-call | flops 2415919104 | bytes 7077888 | tf_op jit(solution)/shard_map/pallas_call | solution.py:207
  105.2 10.4 %shard_map.136 = (bf16[256,1792]{1,0:T(8,128)(2,1)S(1)}, bf16[256,1792]{1,0:T(8,128)(2,1)S(1)}, bf16[8,1792]{1,0:T(8,128)(2,1)S(1)}, bf16[8,1792]{1,0:T(8,128)(2,1)S(1)}) custom-call(s32[4]{0:T(128)S(1)} %pad_add_fusion.2.pos, bf16[256,3584]{1,0:T(8,128)(2,1)} %tok_own.1, bf16[256,3584]{1,0:T(8,128)(2,1)} %collective-permute-done.12.tok.tok_other, ...), custom_call_target="tpu_custom_call" | custom-call | flops 3288334336 | bytes 6422528 | tf_op jit(solution)/shard_map/pallas_call | solution.py:309
  117.1 24.8 %all_to_all.5 = bf16[128,8,256]{2,1,0:T(8,128)(2,1)S(1)} all-to-all(bf16[128,8,256]{2,1,0:T(8,128)(2,1)S(1)} %bitcast.63), channel_id=1, replica_groups=mesh['grp'=4,'page'=32] {'grp','page'}, dimensions={0} | all-to-all | bytes 1048576 | tf_op jit(solution)/shard_map/all_to_all | solution.py:585
  144.6 1.7 collective-permute-start.23
  146.2 3.1 %copy-done.2 = bf16[2,3584,512]{2,1,0:T(8,128)(2,1)S(1)} copy-done((bf16[2,3584,512]{2,1,0:T(8,128)(2,1)S(1)}, bf16[2,3584,512]{2,1,0:T(8,128)(2,1)}, u32[]{:S(2)}) %copy-start.2) | copy-done | bytes 7340056
  151.8 1.7 collective-permute-start.26
  153.5 1.7 collective-permute-start.27
  155.2 7.0 %collective-permute-done.25.b1 = bf16[4,256,128]{2,1,0:T(8,128)(2,1)S(1)} collective-permute-done((bf16[4,256,128]{2,1,0:T(8,128)(2,1)S(1)}, bf16[4,256,128]{2,1,0:T(8,128)(2,1)S(1)}, u32[]{:S(2)}, u32[]{:S(2)}) %collective-permute-start.25) | collective-permute-done | bytes 262176 | tf_op jit(solution)/shard_map/ppermute | solution.py:57
  164.7 7.5 %shard_map.140 = (bf16[4,4,8,3584]{3,2,1,0:T(8,128)(2,1)S(1)}, bf16[4,4,8,3584]{3,2,1,0:T(8,128)(2,1)S(1)}, f32[8,3584]{1,0:T(8,128)S(1)}) custom-call(s32[4]{0:T(128)S(1)} %pad_add_fusion.2.pos, bf16[4,256,128]{2,1,0:T(8,128)(2,1)S(1)} %pad_maximum_fusion.4.t, bf16[4,256,128]{2,1,0:T(8,128)(2,1)S(1)} %collective-permute-done.25.b1, ...), custom_call_target="tpu_custom_call" | custom-call | flops 2818572288 | bytes 11010048 | tf_op jit(solution)/shard_map/pallas_call | solution.py:457
  172.7 2.0 collective-permute-done.32
  178.1 2.8 %collective-permute-done.35 = bf16[4,8,3584]{2,1,0:T(8,128)(2,1)S(1)} collective-permute-done((bf16[4,8,3584]{2,1,0:T(8,128)(2,1)S(1)}, bf16[4,8,3584]{2,1,0:T(8,128)(2,1)S(1)}, u32[]{:S(2)}, u32[]{:S(2)}) %collective-permute-start.35) | collective-permute-done | bytes 229408 | tf_op jit(solution)/shard_map/ppermute | solution.py:51
  180.9 3.0 %collective-permute-done.34 = bf16[4,8,3584]{2,1,0:T(8,128)(2,1)S(1)} collective-permute-done((bf16[4,8,3584]{2,1,0:T(8,128)(2,1)S(1)}, bf16[4,8,3584]{2,1,0:T(8,128)(2,1)S(1)}, u32[]{:S(2)}, u32[]{:S(2)}) %collective-permute-start.34) | collective-permute-done | bytes 229408 | tf_op jit(solution)/shard_map/ppermute | solution.py:51
  183.9 2.4 %collective-permute-done.33 = bf16[4,8,3584]{2,1,0:T(8,128)(2,1)S(1)} collective-permute-done((bf16[4,8,3584]{2,1,0:T(8,128)(2,1)S(1)}, bf16[4,8,3584]{2,1,0:T(8,128)(2,1)S(1)}, u32[]{:S(2)}, u32[]{:S(2)}) %collective-permute-start.33) | collective-permute-done | bytes 229408 | tf_op jit(solution)/shard_map/ppermute | solution.py:51
  186.5 2.6 %collective-permute-start.38 = (bf16[8,3584]{1,0:T(8,128)(2,1)S(1)}, bf16[8,3584]{1,0:T(8,128)(2,1)S(1)}, u32[]{:S(2)}, u32[]{:S(2)}) collective-permute-start(bf16[8,3584]{1,0:T(8,128)(2,1)S(1)} %get-tuple-element.94), channel_id=1, source_target_pairs={{0,6},{1,25},{2,0},{3,27},{4,2},{5,29},{6,4},{7,31},{8,14},{9,1},{... | collective-permute-start | bytes 172040 | tf_op jit(solution)/shard_map/ppermute | solution.py:57
  191.3 3.5 %collective-permute-done.37 = bf16[8,3584]{1,0:T(8,128)(2,1)S(1)} collective-permute-done((bf16[8,3584]{1,0:T(8,128)(2,1)S(1)}, bf16[8,3584]{1,0:T(8,128)(2,1)S(1)}, u32[]{:S(2)}, u32[]{:S(2)}) %collective-permute-start.37) | collective-permute-done | bytes 57376 | tf_op jit(solution)/shard_map/ppermute | solution.py:57
  (143 shorter events, 41.5 us)
Async XLA Ops:
  7.2 96.8 %all-gather.2.cloned.1.call-start = ((), (), s32[]{:S(2)}) async-start(), calls=%async_computation.1 | async-start | bytes 6881280 | tf_op jit(solution)/shard_map/all_gather | solution.py:557
  10.9 10.2 %collective-permute-start.4 = (bf16[112,1152]{1,0:T(8,128)(2,1)S(1)}, bf16[112,1152]{1,0:T(8,128)(2,1)S(1)}, u32[]{:S(2)}, u32[]{:S(2)}) collective-permute-start(bf16[112,1152]{1,0:T(8,128)(2,1)S(1)} %pad_maximum_fusion.6), channel_id=1, source_target_pairs={{0,1},{1,0},{2,3},{3,2},{4,5},{5,4},{6,7},{7,6},{8,9},{9,8},{10,11... | collective-permute-start | bytes 774152 | tf_op jit(solution)/shard_map/ppermute | solution.py:47
  11.2 5.0 %collective-permute-start.3 = (bf16[112,384]{1,0:T(8,128)(2,1)S(1)}, bf16[112,384]{1,0:T(8,128)(2,1)S(1)}, u32[]{:S(2)}, u32[]{:S(2)}) collective-permute-start(bf16[112,384]{1,0:T(8,128)(2,1)S(1)} %fusion.19), channel_id=1, source_target_pairs={{0,24},{1,7},{2,26},{3,1},{4,28},{5,3},{6,30},{7,5},{8,0},{9,15},{... | collective-permute-start | bytes 258056 | tf_op jit(solution)/shard_map/ppermute | solution.py:51
  14.2 6.0 %collective-permute-start.2 = (bf16[112,384]{1,0:T(8,128)(2,1)S(1)}, bf16[112,384]{1,0:T(8,128)(2,1)S(1)}, u32[]{:S(2)}, u32[]{:S(2)}) collective-permute-start(bf16[112,384]{1,0:T(8,128)(2,1)S(1)} %fusion.19), channel_id=1, source_target_pairs={{0,16},{1,5},{2,18},{3,7},{4,20},{5,1},{6,22},{7,3},{8,24},{9,13},... | collective-permute-start | bytes 258056 | tf_op jit(solution)/shard_map/ppermute | solution.py:51
  15.0 6.1 %collective-permute-start.1 = (bf16[112,384]{1,0:T(8,128)(2,1)S(1)}, bf16[112,384]{1,0:T(8,128)(2,1)S(1)}, u32[]{:S(2)}, u32[]{:S(2)}) collective-permute-start(bf16[112,384]{1,0:T(8,128)(2,1)S(1)} %fusion.19), channel_id=1, source_target_pairs={{0,8},{1,3},{2,10},{3,5},{4,12},{5,7},{6,14},{7,1},{8,16},{9,11},{... | collective-permute-start | bytes 258056 | tf_op jit(solution)/shard_map/ppermute | solution.py:51
  21.3 18.4 %collective-permute-start.8 = (bf16[224,1280]{1,0:T(8,128)(2,1)S(1)}, bf16[224,1280]{1,0:T(8,128)(2,1)S(1)}, u32[]{:S(2)}, u32[]{:S(2)}) collective-permute-start(bf16[224,1280]{1,0:T(8,128)(2,1)S(1)} %fusion.7), channel_id=1, source_target_pairs={{0,8},{1,3},{2,10},{3,5},{4,12},{5,7},{6,14},{7,1},{8,16},{9,11},{... | collective-permute-start | bytes 1720328 | tf_op jit(solution)/shard_map/ppermute | solution.py:51
  21.4 18.3 %collective-permute-start.9 = (bf16[224,1280]{1,0:T(8,128)(2,1)S(1)}, bf16[224,1280]{1,0:T(8,128)(2,1)S(1)}, u32[]{:S(2)}, u32[]{:S(2)}) collective-permute-start(bf16[224,1280]{1,0:T(8,128)(2,1)S(1)} %fusion.7), channel_id=1, source_target_pairs={{0,24},{1,7},{2,26},{3,1},{4,28},{5,3},{6,30},{7,5},{8,0},{9,15},{... | collective-permute-start | bytes 1720328 | tf_op jit(solution)/shard_map/ppermute | solution.py:51
  24.6 10.5 %collective-permute-start.5 = (bf16[4,112,384]{2,1,0:T(8,128)(2,1)S(1)}, bf16[4,112,384]{2,1,0:T(8,128)(2,1)S(1)}, u32[]{:S(2)}, u32[]{:S(2)}) collective-permute-start(bf16[4,112,384]{2,1,0:T(8,128)(2,1)S(1)} %pad_maximum_fusion.3.t), channel_id=1, source_target_pairs={{0,2},{1,9},{2,4},{3,11},{4,6},{5,13},{6,0},{7,15},{8,10},{9,17},{... | collective-permute-start | bytes 1032200 | tf_op jit(solution)/shard_map/ppermute | solution.py:57
  26.5 12.5 %collective-permute-start.6 = (bf16[4,112,384]{2,1,0:T(8,128)(2,1)S(1)}, bf16[4,112,384]{2,1,0:T(8,128)(2,1)S(1)}, u32[]{:S(2)}, u32[]{:S(2)}) collective-permute-start(bf16[4,112,384]{2,1,0:T(8,128)(2,1)S(1)} %pad_maximum_fusion.3.t), channel_id=1, source_target_pairs={{0,4},{1,17},{2,6},{3,19},{4,0},{5,21},{6,2},{7,23},{8,12},{9,25},... | collective-permute-start | bytes 1032200 | tf_op jit(solution)/shard_map/ppermute | solution.py:57
  30.1 8.9 %collective-permute-start.7 = (bf16[4,112,384]{2,1,0:T(8,128)(2,1)S(1)}, bf16[4,112,384]{2,1,0:T(8,128)(2,1)S(1)}, u32[]{:S(2)}, u32[]{:S(2)}) collective-permute-start(bf16[4,112,384]{2,1,0:T(8,128)(2,1)S(1)} %pad_maximum_fusion.3.t), channel_id=1, source_target_pairs={{0,6},{1,25},{2,0},{3,27},{4,2},{5,29},{6,4},{7,31},{8,14},{9,1},{... | collective-permute-start | bytes 1032200 | tf_op jit(solution)/shard_map/ppermute | solution.py:57
  41.5 11.3 %collective-permute-start.10 = (bf16[224,1280]{1,0:T(8,128)(2,1)S(1)}, bf16[224,1280]{1,0:T(8,128)(2,1)S(1)}, u32[]{:S(2)}, u32[]{:S(2)}) collective-permute-start(bf16[224,1280]{1,0:T(8,128)(2,1)S(1)} %fusion.7), channel_id=1, source_target_pairs={{0,16},{1,5},{2,18},{3,7},{4,20},{5,1},{6,22},{7,3},{8,24},{9,13},... | collective-permute-start | bytes 1720328 | tf_op jit(solution)/shard_map/ppermute | solution.py:51
  43.1 23.6 %collective-permute-start.12 = (bf16[256,3584]{1,0:T(8,128)(2,1)}, bf16[256,3584]{1,0:T(8,128)(2,1)}, u32[]{:S(2)}, u32[]{:S(2)}) collective-permute-start(bf16[256,3584]{1,0:T(8,128)(2,1)} %tok_own.1), channel_id=1, source_target_pairs={{0,1},{1,0},{2,3},{3,2},{4,5},{5,4},{6,7},{7,6},{8,9},{9,8},{10,11... | collective-permute-start | bytes 5505032 | tf_op jit(solution)/shard_map/ppermute | solution.py:47
  43.8 18.8 %collective-permute-start.13 = (s32[1,8]{1,0:T(1,128)S(1)}, s32[1,8]{1,0:T(1,128)S(1)}, u32[]{:S(2)}, u32[]{:S(2)}) collective-permute-start(s32[1,8]{1,0:T(1,128)S(1)} %copy-done.17), channel_id=1, source_target_pairs={{0,1},{1,0},{2,3},{3,2},{4,5},{5,4},{6,7},{7,6},{8,9},{9,8},{10,11... | collective-permute-start | bytes 104 | tf_op jit(solution)/shard_map/ppermute | solution.py:47
  52.9 19.0 %collective-permute-start.11 = (bf16[2,224,1280]{2,1,0:T(8,128)(2,1)S(1)}, bf16[2,224,1280]{2,1,0:T(8,128)(2,1)}, u32[]{:S(2)}, u32[]{:S(2)}) collective-permute-start(bf16[2,224,1280]{2,1,0:T(8,128)(2,1)S(1)} %pad_maximum_fusion.1.refs_0_), channel_id=1, source_target_pairs={{0,2},{1,9},{2,4},{3,11},{4,6},{5,13},{6,0},{7,15},{8,10},{9,17},{... | collective-permute-start | bytes 3440648 | tf_op jit(solution)/shard_map/ppermute | solution.py:57
  55.1 16.8 %collective-permute-start.16 = (bf16[2,224,1280]{2,1,0:T(8,128)(2,1)}, bf16[2,224,1280]{2,1,0:T(8,128)(2,1)}, u32[]{:S(2)}, u32[]{:S(2)}) collective-permute-start(bf16[2,224,1280]{2,1,0:T(8,128)(2,1)} %pad_maximum_fusion.2.refs_1_), channel_id=1, source_target_pairs={{0,6},{1,25},{2,0},{3,27},{4,2},{5,29},{6,4},{7,31},{8,14},{9,1},{... | collective-permute-start | bytes 3440648 | tf_op jit(solution)/shard_map/ppermute | solution.py:57
  62.8 19.6 %collective-permute-start.14 = (bf16[2,224,1280]{2,1,0:T(8,128)(2,1)}, bf16[2,224,1280]{2,1,0:T(8,128)(2,1)}, u32[]{:S(2)}, u32[]{:S(2)}) collective-permute-start(bf16[2,224,1280]{2,1,0:T(8,128)(2,1)} %pad_maximum_fusion.2.refs_1_), channel_id=1, source_target_pairs={{0,2},{1,9},{2,4},{3,11},{4,6},{5,13},{6,0},{7,15},{8,10},{9,17},{... | collective-permute-start | bytes 3440648 | tf_op jit(solution)/shard_map/ppermute | solution.py:57
  62.8 20.7 %collective-permute-start.15 = (bf16[2,224,1280]{2,1,0:T(8,128)(2,1)S(1)}, bf16[2,224,1280]{2,1,0:T(8,128)(2,1)}, u32[]{:S(2)}, u32[]{:S(2)}) collective-permute-start(bf16[2,224,1280]{2,1,0:T(8,128)(2,1)S(1)} %pad_maximum_fusion.1.refs_0_), channel_id=1, source_target_pairs={{0,6},{1,25},{2,0},{3,27},{4,2},{5,29},{6,4},{7,31},{8,14},{9,1},{... | collective-permute-start | bytes 3440648 | tf_op jit(solution)/shard_map/ppermute | solution.py:57
  71.9 22.8 %collective-permute-start.17 = (bf16[2,224,1280]{2,1,0:T(8,128)(2,1)}, bf16[2,224,1280]{2,1,0:T(8,128)(2,1)}, u32[]{:S(2)}, u32[]{:S(2)}) collective-permute-start(bf16[2,224,1280]{2,1,0:T(8,128)(2,1)} %collective-permute-done.11.refs_2_), channel_id=1, source_target_pairs={{0,2},{1,9},{2,4},{3,11},{4,6},{5,13},{6,0},{7,15},{8,10},{9,17},{... | collective-permute-start | bytes 3440648 | tf_op jit(solution)/shard_map/ppermute | solution.py:57
  71.9 23.9 %collective-permute-start.18 = (bf16[2,224,1280]{2,1,0:T(8,128)(2,1)}, bf16[2,224,1280]{2,1,0:T(8,128)(2,1)}, u32[]{:S(2)}, u32[]{:S(2)}) collective-permute-start(bf16[2,224,1280]{2,1,0:T(8,128)(2,1)} %collective-permute-done.16.refs_5_.refs_7_), channel_id=1, source_target_pairs={{0,6},{1,25},{2,0},{3,27},{4,2},{5,29},{6,4},{7,31},{8,14},{9,1},{... | collective-permute-start | bytes 3440648 | tf_op jit(solution)/shard_map/ppermute | solution.py:57
  143.5 6.4 %collective-permute-start.24 = (bf16[256,128]{1,0:T(8,128)(2,1)S(1)}, bf16[256,128]{1,0:T(8,128)(2,1)S(1)}, u32[]{:S(2)}, u32[]{:S(2)}) collective-permute-start(bf16[256,128]{1,0:T(8,128)(2,1)S(1)} %shard_map.138), channel_id=1, source_target_pairs={{0,24},{1,7},{2,26},{3,1},{4,28},{5,3},{6,30},{7,5},{8,0},{9,15},{... | collective-permute-start | bytes 196616 | tf_op jit(solution)/shard_map/ppermute | solution.py:51
  144.6 5.8 %collective-permute-start.23 = (bf16[256,128]{1,0:T(8,128)(2,1)S(1)}, bf16[256,128]{1,0:T(8,128)(2,1)S(1)}, u32[]{:S(2)}, u32[]{:S(2)}) collective-permute-start(bf16[256,128]{1,0:T(8,128)(2,1)S(1)} %shard_map.138), channel_id=1, source_target_pairs={{0,16},{1,5},{2,18},{3,7},{4,20},{5,1},{6,22},{7,3},{8,24},{9,13},... | collective-permute-start | bytes 196616 | tf_op jit(solution)/shard_map/ppermute | solution.py:51
  146.2 5.5 %collective-permute-start.22 = (bf16[256,128]{1,0:T(8,128)(2,1)S(1)}, bf16[256,128]{1,0:T(8,128)(2,1)S(1)}, u32[]{:S(2)}, u32[]{:S(2)}) collective-permute-start(bf16[256,128]{1,0:T(8,128)(2,1)S(1)} %shard_map.138), channel_id=1, source_target_pairs={{0,8},{1,3},{2,10},{3,5},{4,12},{5,7},{6,14},{7,1},{8,16},{9,11},{... | collective-permute-start | bytes 196616 | tf_op jit(solution)/shard_map/ppermute | solution.py:51
  151.8 10.5 %collective-permute-start.25 = (bf16[4,256,128]{2,1,0:T(8,128)(2,1)S(1)}, bf16[4,256,128]{2,1,0:T(8,128)(2,1)S(1)}, u32[]{:S(2)}, u32[]{:S(2)}) collective-permute-start(bf16[4,256,128]{2,1,0:T(8,128)(2,1)S(1)} %pad_maximum_fusion.4.t), channel_id=1, source_target_pairs={{0,2},{1,9},{2,4},{3,11},{4,6},{5,13},{6,0},{7,15},{8,10},{9,17},{... | collective-permute-start | bytes 786440 | tf_op jit(solution)/shard_map/ppermute | solution.py:57
  151.8 10.4 %collective-permute-start.26 = (bf16[4,256,128]{2,1,0:T(8,128)(2,1)S(1)}, bf16[4,256,128]{2,1,0:T(8,128)(2,1)S(1)}, u32[]{:S(2)}, u32[]{:S(2)}) collective-permute-start(bf16[4,256,128]{2,1,0:T(8,128)(2,1)S(1)} %pad_maximum_fusion.4.t), channel_id=1, source_target_pairs={{0,4},{1,17},{2,6},{3,19},{4,0},{5,21},{6,2},{7,23},{8,12},{9,25},... | collective-permute-start | bytes 786440 | tf_op jit(solution)/shard_map/ppermute | solution.py:57
  153.5 9.6 %collective-permute-start.27 = (bf16[4,256,128]{2,1,0:T(8,128)(2,1)S(1)}, bf16[4,256,128]{2,1,0:T(8,128)(2,1)S(1)}, u32[]{:S(2)}, u32[]{:S(2)}) collective-permute-start(bf16[4,256,128]{2,1,0:T(8,128)(2,1)S(1)} %pad_maximum_fusion.4.t), channel_id=1, source_target_pairs={{0,6},{1,25},{2,0},{3,27},{4,2},{5,29},{6,4},{7,31},{8,14},{9,1},{... | collective-permute-start | bytes 786440 | tf_op jit(solution)/shard_map/ppermute | solution.py:57
  155.2 7.9 %collective-permute-start.28 = (bf16[4,256,128]{2,1,0:T(8,128)(2,1)S(1)}, bf16[4,256,128]{2,1,0:T(8,128)(2,1)S(1)}, u32[]{:S(2)}, u32[]{:S(2)}) collective-permute-start(bf16[4,256,128]{2,1,0:T(8,128)(2,1)S(1)} %pad_maximum_fusion.4.t), channel_id=1, source_target_pairs={{0,1},{1,0},{2,3},{3,2},{4,5},{5,4},{6,7},{7,6},{8,9},{9,8},{10,11... | collective-permute-start | bytes 786440 | tf_op jit(solution)/shard_map/ppermute | solution.py:47
  172.4 5.6 %collective-permute-start.20 = (bf16[256,1792]{1,0:T(8,128)(2,1)S(1)}, bf16[256,1792]{1,0:T(8,128)(2,1)S(1)}, u32[]{:S(2)}, u32[]{:S(2)}) collective-permute-start(bf16[256,1792]{1,0:T(8,128)(2,1)S(1)} %get-tuple-element.66), channel_id=1, source_target_pairs={{0,1},{1,0},{2,3},{3,2},{4,5},{5,4},{6,7},{7,6},{8,9},{9,8},{10,11... | collective-permute-start | bytes 2752520 | tf_op jit(solution)/shard_map/ppermute | solution.py:47
  174.9 6.1 %collective-permute-start.35 = (bf16[4,8,3584]{2,1,0:T(8,128)(2,1)S(1)}, bf16[4,8,3584]{2,1,0:T(8,128)(2,1)S(1)}, u32[]{:S(2)}, u32[]{:S(2)}) collective-permute-start(bf16[4,8,3584]{2,1,0:T(8,128)(2,1)S(1)} %get-tuple-element.83), channel_id=1, source_target_pairs={{0,24},{1,7},{2,26},{3,1},{4,28},{5,3},{6,30},{7,5},{8,0},{9,15},{... | collective-permute-start | bytes 688136 | tf_op jit(solution)/shard_map/ppermute | solution.py:51
  176.3 7.6 %collective-permute-start.34 = (bf16[4,8,3584]{2,1,0:T(8,128)(2,1)S(1)}, bf16[4,8,3584]{2,1,0:T(8,128)(2,1)S(1)}, u32[]{:S(2)}, u32[]{:S(2)}) collective-permute-start(bf16[4,8,3584]{2,1,0:T(8,128)(2,1)S(1)} %get-tuple-element.84), channel_id=1, source_target_pairs={{0,16},{1,5},{2,18},{3,7},{4,20},{5,1},{6,22},{7,3},{8,24},{9,13},... | collective-permute-start | bytes 688136 | tf_op jit(solution)/shard_map/ppermute | solution.py:51
  176.9 9.3 %collective-permute-start.33 = (bf16[4,8,3584]{2,1,0:T(8,128)(2,1)S(1)}, bf16[4,8,3584]{2,1,0:T(8,128)(2,1)S(1)}, u32[]{:S(2)}, u32[]{:S(2)}) collective-permute-start(bf16[4,8,3584]{2,1,0:T(8,128)(2,1)S(1)} %get-tuple-element.82), channel_id=1, source_target_pairs={{0,8},{1,3},{2,10},{3,5},{4,12},{5,7},{6,14},{7,1},{8,16},{9,11},{... | collective-permute-start | bytes 688136 | tf_op jit(solution)/shard_map/ppermute | solution.py:51
  189.0 5.8 %collective-permute-start.37 = (bf16[8,3584]{1,0:T(8,128)(2,1)S(1)}, bf16[8,3584]{1,0:T(8,128)(2,1)S(1)}, u32[]{:S(2)}, u32[]{:S(2)}) collective-permute-start(bf16[8,3584]{1,0:T(8,128)(2,1)S(1)} %get-tuple-element.95), channel_id=1, source_target_pairs={{0,4},{1,17},{2,6},{3,19},{4,0},{5,21},{6,2},{7,23},{8,12},{9,25},... | collective-permute-start | bytes 172040 | tf_op jit(solution)/shard_map/ppermute | solution.py:57
  189.0 6.0 %collective-permute-start.36 = (bf16[8,3584]{1,0:T(8,128)(2,1)S(1)}, bf16[8,3584]{1,0:T(8,128)(2,1)S(1)}, u32[]{:S(2)}, u32[]{:S(2)}) collective-permute-start(bf16[8,3584]{1,0:T(8,128)(2,1)S(1)} %get-tuple-element.93), channel_id=1, source_target_pairs={{0,2},{1,9},{2,4},{3,11},{4,6},{5,13},{6,0},{7,15},{8,10},{9,17},{... | collective-permute-start | bytes 172040 | tf_op jit(solution)/shard_map/ppermute | solution.py:57
  (27 other events, 112.9 us)
Sparse Core Ops, SparseCore 0:
  41.6 60.5 all-gather.1

commit v5 on v4

--- a/solution.py
+++ b/solution.py
@@ -583,12 +583,11 @@
     blocks = page_blocks(vectors, labels, slots)
     blocks = jnp.broadcast_to(blocks[None], (SIDE,) + blocks.shape).reshape(-1, pages, 2 * HD)
     gathered = lax.all_to_all(blocks, ("grp", "page"), split_axis=0, concat_axis=0, tiled=True)
-    gathered, gate_up_weight = lax.optimization_barrier((gathered, gate_up_weight))
-    gate_up_weight = load_weights(gate_up_weight)
     mixed = doc_attention(pos, gathered.reshape(-1, 2 * HD), head_gain, plane)
 
     line = jnp.stack([mixed, move_a(mixed, 1), move_a(mixed, 2), move_a(mixed, -1)])
     line, gate_up_weight = lax.optimization_barrier((line, gate_up_weight))
+    gate_up_weight = load_weights(gate_up_weight)
     pieces = (line, move_b(line, 1), move_b(line, 2), move_b(line, -1))
     pieces_t = tuple(swap(v) for v in pieces)
     own, other, states = feed_forward(

time: 203 us -> 203 us (level)
  waiting for transfers between devices: 61 us -> 64.1 us
  local copies, waits for them, and re-layouts: 12.2 us -> 9.79 us
    ppermute x12, waiting for transfers between devices: 24.9 us -> 28.5 us  [move_a(): lax.ppermute(v, 'page', chip_perm(lambda x, z, c: (x + k, z, c) if c == 0...]
    unnamed x38 -> x40, local copies, waits for them, and re-layouts: 8.21 us -> 5.82 us
  transfers between devices with their start and end apart: 40 -> 40, of which waited for: 27 -> 28; matrix products, arithmetic and copies ran while one was open for 3% -> 3% of each run, Pallas kernels for 11% -> 11%
where the time goes in v5:
time: 203 us
  waiting for transfers between devices  64.1 us (32%)
  Pallas kernels  43.6 us (21%)
  starting transfers between devices  40.7 us (20%)
  blocking collectives  24.8 us (12%)
  between operations  14.5 us (7%)
  local copies, waits for them, and re-layouts  9.79 us (5%)
  other arithmetic  5.36 us (3%)
    ppermute x15, waiting for transfers between devices, move_b(): lax.ppermute(v, 'page', chip_perm(lambda x, z, c: (x, z + k, c) if c == 0...  28.6 us
    ppermute x12, waiting for transfers between devices, move_a(): lax.ppermute(v, 'page', chip_perm(lambda x, z, c: (x + k, z, c) if c == 0...  28.5 us
    all_to_all x1, blocking collectives, on_device(): lax.all_to_all(blocks, ('grp', 'page'), split_axis=0, concat_axis=0, tile...  24.8 us
    ppermute x15, starting transfers between devices, move_b(): lax.ppermute(v, 'page', chip_perm(lambda x, z, c: (x, z + k, c) if c == 0...  23.2 us
    ppermute x12, starting transfers between devices, move_a(): lax.ppermute(v, 'page', chip_perm(lambda x, z, c: (x + k, z, c) if c == 0...  14.8 us
    pallas_call x1, Pallas kernels, page_out(): pl.pallas_call(out_kernel, out_shape=(st, st, pool, pool), in_specs=[smem...  10.6 us
    pallas_call x1, Pallas kernels, qkv_first(): pl.pallas_call(qkv_first_kernel, out_shape=jax.ShapeDtypeStruct((2 * toke...  8.55 us
    pallas_call x2, Pallas kernels, norm_blocks(): pl.pallas_call(norm_kernel, out_shape=jax.ShapeDtypeStruct((chips, count,...  7.57 us
  transfers between devices with their start and end apart: 40, of which 28 were waited for; matrix products, arithmetic and copies ran while one was open for 3% of the time, Pallas kernels for 11%

profile of v5, /device:TPU:0, one launch (start us, length us, event | category | flops | bytes accessed | tf_op | source)
XLA Modules:
  0.0 202.8 jit_solution(8714328885624004372)
XLA Ops:
  11.2 2.9 %collective-permute-start.3 = (bf16[112,384]{1,0:T(8,128)(2,1)S(1)}, bf16[112,384]{1,0:T(8,128)(2,1)S(1)}, u32[]{:S(2)}, u32[]{:S(2)}) collective-permute-start(bf16[112,384]{1,0:T(8,128)(2,1)S(1)} %fusion.19), channel_id=1, source_target_pairs={{0,24},{1,7},{2,26},{3,1},{4,28},{5,3},{6,30},{7,5},{8,0},{9,15},{... | collective-permute-start | bytes 258056 | tf_op jit(solution)/shard_map/ppermute | solution.py:51
  16.3 3.9 %collective-permute-done.2 = bf16[112,384]{1,0:T(8,128)(2,1)S(1)} collective-permute-done((bf16[112,384]{1,0:T(8,128)(2,1)S(1)}, bf16[112,384]{1,0:T(8,128)(2,1)S(1)}, u32[]{:S(2)}, u32[]{:S(2)}) %collective-permute-start.2) | collective-permute-done | bytes 86048 | tf_op jit(solution)/shard_map/ppermute | solution.py:51
  21.4 3.2 %collective-permute-start.9 = (bf16[224,1280]{1,0:T(8,128)(2,1)S(1)}, bf16[224,1280]{1,0:T(8,128)(2,1)S(1)}, u32[]{:S(2)}, u32[]{:S(2)}) collective-permute-start(bf16[224,1280]{1,0:T(8,128)(2,1)S(1)} %fusion.7), channel_id=1, source_target_pairs={{0,24},{1,7},{2,26},{3,1},{4,28},{5,3},{6,30},{7,5},{8,0},{9,15},{... | collective-permute-start | bytes 1720328 | tf_op jit(solution)/shard_map/ppermute | solution.py:51
  24.6 1.9 collective-permute-start.5
  26.5 3.6 %collective-permute-start.6 = (bf16[4,112,384]{2,1,0:T(8,128)(2,1)S(1)}, bf16[4,112,384]{2,1,0:T(8,128)(2,1)S(1)}, u32[]{:S(2)}, u32[]{:S(2)}) collective-permute-start(bf16[4,112,384]{2,1,0:T(8,128)(2,1)S(1)} %pad_maximum_fusion.3.t), channel_id=1, source_target_pairs={{0,4},{1,17},{2,6},{3,19},{4,0},{5,21},{6,2},{7,23},{8,12},{9,25},... | collective-permute-start | bytes 1032200 | tf_op jit(solution)/shard_map/ppermute | solution.py:57
  31.2 3.9 %collective-permute-done.5.b1 = bf16[4,112,384]{2,1,0:T(8,128)(2,1)S(1)} collective-permute-done((bf16[4,112,384]{2,1,0:T(8,128)(2,1)S(1)}, bf16[4,112,384]{2,1,0:T(8,128)(2,1)S(1)}, u32[]{:S(2)}, u32[]{:S(2)}) %collective-permute-start.5) | collective-permute-done | bytes 344096 | tf_op jit(solution)/shard_map/ppermute | solution.py:57
  35.1 3.9 %collective-permute-done.6.b2 = bf16[4,112,384]{2,1,0:T(8,128)(2,1)S(1)} collective-permute-done((bf16[4,112,384]{2,1,0:T(8,128)(2,1)S(1)}, bf16[4,112,384]{2,1,0:T(8,128)(2,1)S(1)}, u32[]{:S(2)}, u32[]{:S(2)}) %collective-permute-start.6) | collective-permute-done | bytes 344096 | tf_op jit(solution)/shard_map/ppermute | solution.py:57
  39.7 1.8 shard_map.135
  41.5 1.7 collective-permute-start.10
  43.8 9.0 %collective-permute-done.10 = bf16[224,1280]{1,0:T(8,128)(2,1)S(1)} collective-permute-done((bf16[224,1280]{1,0:T(8,128)(2,1)S(1)}, bf16[224,1280]{1,0:T(8,128)(2,1)S(1)}, u32[]{:S(2)}, u32[]{:S(2)}) %collective-permute-start.10) | collective-permute-done | bytes 573472 | tf_op jit(solution)/shard_map/ppermute | solution.py:51
  55.0 2.3 %collective-permute-start.16 = (bf16[2,224,1280]{2,1,0:T(8,128)(2,1)}, bf16[2,224,1280]{2,1,0:T(8,128)(2,1)}, u32[]{:S(2)}, u32[]{:S(2)}) collective-permute-start(bf16[2,224,1280]{2,1,0:T(8,128)(2,1)} %pad_maximum_fusion.2.refs_1_), channel_id=1, source_target_pairs={{0,6},{1,25},{2,0},{3,27},{4,2},{5,29},{6,4},{7,31},{8,14},{9,1},{... | collective-permute-start | bytes 3440648 | tf_op jit(solution)/shard_map/ppermute | solution.py:57
  57.7 3.8 %shard_map.131.xo = bf16[16,256,256]{2,1,0:T(8,128)(2,1)S(1)} custom-call(bf16[256,3584]{1,0:T(8,128)(2,1)} %tok_own.1, f32[1,3584]{1,0:T(1,128)S(1)} %broadcast_in_dim.14.gain), custom_call_target="tpu_custom_call" | custom-call | bytes 3670016 | tf_op jit(solution)/shard_map/pallas_call | solution.py:111
  62.8 3.2 %collective-permute-start.15 = (bf16[2,224,1280]{2,1,0:T(8,128)(2,1)S(1)}, bf16[2,224,1280]{2,1,0:T(8,128)(2,1)}, u32[]{:S(2)}, u32[]{:S(2)}) collective-permute-start(bf16[2,224,1280]{2,1,0:T(8,128)(2,1)S(1)} %pad_maximum_fusion.1.refs_0_), channel_id=1, source_target_pairs={{0,6},{1,25},{2,0},{3,27},{4,2},{5,29},{6,4},{7,31},{8,14},{9,1},{... | collective-permute-start | bytes 3440648 | tf_op jit(solution)/shard_map/ppermute | solution.py:57
  66.8 3.8 %shard_map.132.xt = bf16[16,256,256]{2,1,0:T(8,128)(2,1)S(1)} custom-call(bf16[256,3584]{1,0:T(8,128)(2,1)} %collective-permute-done.12.tok.tok_other, f32[1,3584]{1,0:T(1,128)S(1)} %broadcast_in_dim.14.gain), custom_call_target="tpu_custom_call" | custom-call | bytes 3670016 | tf_op jit(solution)/shard_map/pallas_call | solution.py:111
  71.9 3.2 %collective-permute-start.18 = (bf16[2,224,1280]{2,1,0:T(8,128)(2,1)}, bf16[2,224,1280]{2,1,0:T(8,128)(2,1)}, u32[]{:S(2)}, u32[]{:S(2)}) collective-permute-start(bf16[2,224,1280]{2,1,0:T(8,128)(2,1)} %collective-permute-done.16.refs_5_.refs_7_), channel_id=1, source_target_pairs={{0,6},{1,25},{2,0},{3,27},{4,2},{5,29},{6,4},{7,31},{8,14},{9,1},{... | collective-permute-start | bytes 3440648 | tf_op jit(solution)/shard_map/ppermute | solution.py:57
  76.0 6.4 %collective-permute-done.14.refs_3_ = bf16[2,224,1280]{2,1,0:T(8,128)(2,1)} collective-permute-done((bf16[2,224,1280]{2,1,0:T(8,128)(2,1)}, bf16[2,224,1280]{2,1,0:T(8,128)(2,1)}, u32[]{:S(2)}, u32[]{:S(2)}) %collective-permute-start.14) | collective-permute-done | bytes 1146912 | tf_op jit(solution)/shard_map/ppermute | solution.py:57
  85.1 8.6 %shard_map.133.part = f32[512,1152]{1,0:T(8,128)S(1)} custom-call(s32[4]{0:T(128)S(1)} %pad_add_fusion.2.pos, bf16[16,256,256]{2,1,0:T(8,128)(2,1)S(1)} %shard_map.131.xo, bf16[16,256,256]{2,1,0:T(8,128)(2,1)S(1)} %copy-done.1, bf16[2,224,1280]{2,1,0:T(8,128)(2,1)S(1)} %pad_maximum_fusion.1.refs_0_, bf16[2,224,1280]{2,1,0:T(8,128)(2,1)} %pad_maximum_fusion.2.refs_1_, ...), custom_call_target="tpu_custom_call" | custom-call | flops 3623878656 | bytes 7077888 | tf_op jit(solution)/shard_map/pallas_call | solution.py:187
  95.8 5.5 %shard_map.134.att = bf16[512,896]{1,0:T(8,128)(2,1)S(1)} custom-call(s32[4]{0:T(128)S(1)} %pad_add_fusion.2.pos, bf16[16,256,256]{2,1,0:T(8,128)(2,1)S(1)} %shard_map.131.xo, bf16[16,256,256]{2,1,0:T(8,128)(2,1)S(1)} %copy-done.1, s32[512,1]{1,0:T(8,128)S(1)} %copy.36.seg_col, s32[2,1,256]{2,1,0:T(1,128)S(1)} %broadcast_in_dim.16.seg_row, ...), custom_call_target="tpu_custom_call" | custom-call | flops 2415919104 | bytes 7077888 | tf_op jit(solution)/shard_map/pallas_call | solution.py:207
  105.3 10.6 %shard_map.136 = (bf16[256,1792]{1,0:T(8,128)(2,1)S(1)}, bf16[256,1792]{1,0:T(8,128)(2,1)S(1)}, bf16[8,1792]{1,0:T(8,128)(2,1)S(1)}, bf16[8,1792]{1,0:T(8,128)(2,1)S(1)}) custom-call(s32[4]{0:T(128)S(1)} %pad_add_fusion.2.pos, bf16[256,3584]{1,0:T(8,128)(2,1)} %tok_own.1, bf16[256,3584]{1,0:T(8,128)(2,1)} %collective-permute-done.12.tok.tok_other, ...), custom_call_target="tpu_custom_call" | custom-call | flops 3288334336 | bytes 6422528 | tf_op jit(solution)/shard_map/pallas_call | solution.py:309
  117.5 24.8 %all_to_all.5 = bf16[128,8,256]{2,1,0:T(8,128)(2,1)S(1)} all-to-all(bf16[128,8,256]{2,1,0:T(8,128)(2,1)S(1)} %bitcast.65), channel_id=1, replica_groups=mesh['grp'=4,'page'=32] {'grp','page'}, dimensions={0} | all-to-all | bytes 1048576 | tf_op jit(solution)/shard_map/all_to_all | solution.py:585
  144.9 1.7 collective-permute-start.23
  148.2 2.5 %collective-permute-done.23 = bf16[256,128]{1,0:T(8,128)(2,1)S(1)} collective-permute-done((bf16[256,128]{1,0:T(8,128)(2,1)S(1)}, bf16[256,128]{1,0:T(8,128)(2,1)S(1)}, u32[]{:S(2)}, u32[]{:S(2)}) %collective-permute-start.23) | collective-permute-done | bytes 65568 | tf_op jit(solution)/shard_map/ppermute | solution.py:51
  152.2 1.7 collective-permute-start.26
  153.8 1.7 collective-permute-start.27
  155.6 7.0 %collective-permute-done.25.b1 = bf16[4,256,128]{2,1,0:T(8,128)(2,1)S(1)} collective-permute-done((bf16[4,256,128]{2,1,0:T(8,128)(2,1)S(1)}, bf16[4,256,128]{2,1,0:T(8,128)(2,1)S(1)}, u32[]{:S(2)}, u32[]{:S(2)}) %collective-permute-start.25) | collective-permute-done | bytes 262176 | tf_op jit(solution)/shard_map/ppermute | solution.py:57
  165.5 7.5 %shard_map.140 = (bf16[4,4,8,3584]{3,2,1,0:T(8,128)(2,1)S(1)}, bf16[4,4,8,3584]{3,2,1,0:T(8,128)(2,1)S(1)}, f32[8,3584]{1,0:T(8,128)S(1)}) custom-call(s32[4]{0:T(128)S(1)} %pad_add_fusion.2.pos, bf16[4,256,128]{2,1,0:T(8,128)(2,1)S(1)} %pad_maximum_fusion.4.t, bf16[4,256,128]{2,1,0:T(8,128)(2,1)S(1)} %collective-permute-done.25.b1, ...), custom_call_target="tpu_custom_call" | custom-call | flops 2818572288 | bytes 11010048 | tf_op jit(solution)/shard_map/pallas_call | solution.py:457
  173.7 2.0 collective-permute-done.32
  178.5 3.5 %collective-permute-done.35 = bf16[4,8,3584]{2,1,0:T(8,128)(2,1)S(1)} collective-permute-done((bf16[4,8,3584]{2,1,0:T(8,128)(2,1)S(1)}, bf16[4,8,3584]{2,1,0:T(8,128)(2,1)S(1)}, u32[]{:S(2)}, u32[]{:S(2)}) %collective-permute-start.35) | collective-permute-done | bytes 229408 | tf_op jit(solution)/shard_map/ppermute | solution.py:51
  181.9 2.4 %collective-permute-done.34 = bf16[4,8,3584]{2,1,0:T(8,128)(2,1)S(1)} collective-permute-done((bf16[4,8,3584]{2,1,0:T(8,128)(2,1)S(1)}, bf16[4,8,3584]{2,1,0:T(8,128)(2,1)S(1)}, u32[]{:S(2)}, u32[]{:S(2)}) %collective-permute-start.34) | collective-permute-done | bytes 229408 | tf_op jit(solution)/shard_map/ppermute | solution.py:51
  184.3 2.4 %collective-permute-done.33 = bf16[4,8,3584]{2,1,0:T(8,128)(2,1)S(1)} collective-permute-done((bf16[4,8,3584]{2,1,0:T(8,128)(2,1)S(1)}, bf16[4,8,3584]{2,1,0:T(8,128)(2,1)S(1)}, u32[]{:S(2)}, u32[]{:S(2)}) %collective-permute-start.33) | collective-permute-done | bytes 229408 | tf_op jit(solution)/shard_map/ppermute | solution.py:51
  186.9 2.4 %collective-permute-start.38 = (bf16[8,3584]{1,0:T(8,128)(2,1)S(1)}, bf16[8,3584]{1,0:T(8,128)(2,1)S(1)}, u32[]{:S(2)}, u32[]{:S(2)}) collective-permute-start(bf16[8,3584]{1,0:T(8,128)(2,1)S(1)} %get-tuple-element.90), channel_id=1, source_target_pairs={{0,6},{1,25},{2,0},{3,27},{4,2},{5,29},{6,4},{7,31},{8,14},{9,1},{... | collective-permute-start | bytes 172040 | tf_op jit(solution)/shard_map/ppermute | solution.py:57
  191.6 3.5 %collective-permute-done.37 = bf16[8,3584]{1,0:T(8,128)(2,1)S(1)} collective-permute-done((bf16[8,3584]{1,0:T(8,128)(2,1)S(1)}, bf16[8,3584]{1,0:T(8,128)(2,1)S(1)}, u32[]{:S(2)}, u32[]{:S(2)}) %collective-permute-start.37) | collective-permute-done | bytes 57376 | tf_op jit(solution)/shard_map/ppermute | solution.py:57
  (146 shorter events, 42.1 us)
Async XLA Ops:
  7.2 96.8 %all-gather.2.cloned.1.call-start = ((), (), s32[]{:S(2)}) async-start(), calls=%async_computation.1 | async-start | bytes 6881280 | tf_op jit(solution)/shard_map/all_gather | solution.py:557
  10.9 10.2 %collective-permute-start.4 = (bf16[112,1152]{1,0:T(8,128)(2,1)S(1)}, bf16[112,1152]{1,0:T(8,128)(2,1)S(1)}, u32[]{:S(2)}, u32[]{:S(2)}) collective-permute-start(bf16[112,1152]{1,0:T(8,128)(2,1)S(1)} %pad_maximum_fusion.6), channel_id=1, source_target_pairs={{0,1},{1,0},{2,3},{3,2},{4,5},{5,4},{6,7},{7,6},{8,9},{9,8},{10,11... | collective-permute-start | bytes 774152 | tf_op jit(solution)/shard_map/ppermute | solution.py:47
  11.2 5.0 %collective-permute-start.3 = (bf16[112,384]{1,0:T(8,128)(2,1)S(1)}, bf16[112,384]{1,0:T(8,128)(2,1)S(1)}, u32[]{:S(2)}, u32[]{:S(2)}) collective-permute-start(bf16[112,384]{1,0:T(8,128)(2,1)S(1)} %fusion.19), channel_id=1, source_target_pairs={{0,24},{1,7},{2,26},{3,1},{4,28},{5,3},{6,30},{7,5},{8,0},{9,15},{... | collective-permute-start | bytes 258056 | tf_op jit(solution)/shard_map/ppermute | solution.py:51
  14.2 6.0 %collective-permute-start.2 = (bf16[112,384]{1,0:T(8,128)(2,1)S(1)}, bf16[112,384]{1,0:T(8,128)(2,1)S(1)}, u32[]{:S(2)}, u32[]{:S(2)}) collective-permute-start(bf16[112,384]{1,0:T(8,128)(2,1)S(1)} %fusion.19), channel_id=1, source_target_pairs={{0,16},{1,5},{2,18},{3,7},{4,20},{5,1},{6,22},{7,3},{8,24},{9,13},... | collective-permute-start | bytes 258056 | tf_op jit(solution)/shard_map/ppermute | solution.py:51
  15.0 6.1 %collective-permute-start.1 = (bf16[112,384]{1,0:T(8,128)(2,1)S(1)}, bf16[112,384]{1,0:T(8,128)(2,1)S(1)}, u32[]{:S(2)}, u32[]{:S(2)}) collective-permute-start(bf16[112,384]{1,0:T(8,128)(2,1)S(1)} %fusion.19), channel_id=1, source_target_pairs={{0,8},{1,3},{2,10},{3,5},{4,12},{5,7},{6,14},{7,1},{8,16},{9,11},{... | collective-permute-start | bytes 258056 | tf_op jit(solution)/shard_map/ppermute | solution.py:51
  21.3 18.4 %collective-permute-start.8 = (bf16[224,1280]{1,0:T(8,128)(2,1)S(1)}, bf16[224,1280]{1,0:T(8,128)(2,1)S(1)}, u32[]{:S(2)}, u32[]{:S(2)}) collective-permute-start(bf16[224,1280]{1,0:T(8,128)(2,1)S(1)} %fusion.7), channel_id=1, source_target_pairs={{0,8},{1,3},{2,10},{3,5},{4,12},{5,7},{6,14},{7,1},{8,16},{9,11},{... | collective-permute-start | bytes 1720328 | tf_op jit(solution)/shard_map/ppermute | solution.py:51
  21.4 18.3 %collective-permute-start.9 = (bf16[224,1280]{1,0:T(8,128)(2,1)S(1)}, bf16[224,1280]{1,0:T(8,128)(2,1)S(1)}, u32[]{:S(2)}, u32[]{:S(2)}) collective-permute-start(bf16[224,1280]{1,0:T(8,128)(2,1)S(1)} %fusion.7), channel_id=1, source_target_pairs={{0,24},{1,7},{2,26},{3,1},{4,28},{5,3},{6,30},{7,5},{8,0},{9,15},{... | collective-permute-start | bytes 1720328 | tf_op jit(solution)/shard_map/ppermute | solution.py:51
  24.6 10.5 %collective-permute-start.5 = (bf16[4,112,384]{2,1,0:T(8,128)(2,1)S(1)}, bf16[4,112,384]{2,1,0:T(8,128)(2,1)S(1)}, u32[]{:S(2)}, u32[]{:S(2)}) collective-permute-start(bf16[4,112,384]{2,1,0:T(8,128)(2,1)S(1)} %pad_maximum_fusion.3.t), channel_id=1, source_target_pairs={{0,2},{1,9},{2,4},{3,11},{4,6},{5,13},{6,0},{7,15},{8,10},{9,17},{... | collective-permute-start | bytes 1032200 | tf_op jit(solution)/shard_map/ppermute | solution.py:57
  26.5 12.5 %collective-permute-start.6 = (bf16[4,112,384]{2,1,0:T(8,128)(2,1)S(1)}, bf16[4,112,384]{2,1,0:T(8,128)(2,1)S(1)}, u32[]{:S(2)}, u32[]{:S(2)}) collective-permute-start(bf16[4,112,384]{2,1,0:T(8,128)(2,1)S(1)} %pad_maximum_fusion.3.t), channel_id=1, source_target_pairs={{0,4},{1,17},{2,6},{3,19},{4,0},{5,21},{6,2},{7,23},{8,12},{9,25},... | collective-permute-start | bytes 1032200 | tf_op jit(solution)/shard_map/ppermute | solution.py:57
  30.1 8.9 %collective-permute-start.7 = (bf16[4,112,384]{2,1,0:T(8,128)(2,1)S(1)}, bf16[4,112,384]{2,1,0:T(8,128)(2,1)S(1)}, u32[]{:S(2)}, u32[]{:S(2)}) collective-permute-start(bf16[4,112,384]{2,1,0:T(8,128)(2,1)S(1)} %pad_maximum_fusion.3.t), channel_id=1, source_target_pairs={{0,6},{1,25},{2,0},{3,27},{4,2},{5,29},{6,4},{7,31},{8,14},{9,1},{... | collective-permute-start | bytes 1032200 | tf_op jit(solution)/shard_map/ppermute | solution.py:57
  41.5 11.3 %collective-permute-start.10 = (bf16[224,1280]{1,0:T(8,128)(2,1)S(1)}, bf16[224,1280]{1,0:T(8,128)(2,1)S(1)}, u32[]{:S(2)}, u32[]{:S(2)}) collective-permute-start(bf16[224,1280]{1,0:T(8,128)(2,1)S(1)} %fusion.7), channel_id=1, source_target_pairs={{0,16},{1,5},{2,18},{3,7},{4,20},{5,1},{6,22},{7,3},{8,24},{9,13},... | collective-permute-start | bytes 1720328 | tf_op jit(solution)/shard_map/ppermute | solution.py:51
  43.1 23.6 %collective-permute-start.12 = (bf16[256,3584]{1,0:T(8,128)(2,1)}, bf16[256,3584]{1,0:T(8,128)(2,1)}, u32[]{:S(2)}, u32[]{:S(2)}) collective-permute-start(bf16[256,3584]{1,0:T(8,128)(2,1)} %tok_own.1), channel_id=1, source_target_pairs={{0,1},{1,0},{2,3},{3,2},{4,5},{5,4},{6,7},{7,6},{8,9},{9,8},{10,11... | collective-permute-start | bytes 5505032 | tf_op jit(solution)/shard_map/ppermute | solution.py:47
  43.8 18.8 %collective-permute-start.13 = (s32[1,8]{1,0:T(1,128)S(1)}, s32[1,8]{1,0:T(1,128)S(1)}, u32[]{:S(2)}, u32[]{:S(2)}) collective-permute-start(s32[1,8]{1,0:T(1,128)S(1)} %copy-done.16), channel_id=1, source_target_pairs={{0,1},{1,0},{2,3},{3,2},{4,5},{5,4},{6,7},{7,6},{8,9},{9,8},{10,11... | collective-permute-start | bytes 104 | tf_op jit(solution)/shard_map/ppermute | solution.py:47
  52.9 19.0 %collective-permute-start.11 = (bf16[2,224,1280]{2,1,0:T(8,128)(2,1)S(1)}, bf16[2,224,1280]{2,1,0:T(8,128)(2,1)}, u32[]{:S(2)}, u32[]{:S(2)}) collective-permute-start(bf16[2,224,1280]{2,1,0:T(8,128)(2,1)S(1)} %pad_maximum_fusion.1.refs_0_), channel_id=1, source_target_pairs={{0,2},{1,9},{2,4},{3,11},{4,6},{5,13},{6,0},{7,15},{8,10},{9,17},{... | collective-permute-start | bytes 3440648 | tf_op jit(solution)/shard_map/ppermute | solution.py:57
  55.0 16.9 %collective-permute-start.16 = (bf16[2,224,1280]{2,1,0:T(8,128)(2,1)}, bf16[2,224,1280]{2,1,0:T(8,128)(2,1)}, u32[]{:S(2)}, u32[]{:S(2)}) collective-permute-start(bf16[2,224,1280]{2,1,0:T(8,128)(2,1)} %pad_maximum_fusion.2.refs_1_), channel_id=1, source_target_pairs={{0,6},{1,25},{2,0},{3,27},{4,2},{5,29},{6,4},{7,31},{8,14},{9,1},{... | collective-permute-start | bytes 3440648 | tf_op jit(solution)/shard_map/ppermute | solution.py:57
  62.8 19.6 %collective-permute-start.14 = (bf16[2,224,1280]{2,1,0:T(8,128)(2,1)}, bf16[2,224,1280]{2,1,0:T(8,128)(2,1)}, u32[]{:S(2)}, u32[]{:S(2)}) collective-permute-start(bf16[2,224,1280]{2,1,0:T(8,128)(2,1)} %pad_maximum_fusion.2.refs_1_), channel_id=1, source_target_pairs={{0,2},{1,9},{2,4},{3,11},{4,6},{5,13},{6,0},{7,15},{8,10},{9,17},{... | collective-permute-start | bytes 3440648 | tf_op jit(solution)/shard_map/ppermute | solution.py:57
  62.8 20.7 %collective-permute-start.15 = (bf16[2,224,1280]{2,1,0:T(8,128)(2,1)S(1)}, bf16[2,224,1280]{2,1,0:T(8,128)(2,1)}, u32[]{:S(2)}, u32[]{:S(2)}) collective-permute-start(bf16[2,224,1280]{2,1,0:T(8,128)(2,1)S(1)} %pad_maximum_fusion.1.refs_0_), channel_id=1, source_target_pairs={{0,6},{1,25},{2,0},{3,27},{4,2},{5,29},{6,4},{7,31},{8,14},{9,1},{... | collective-permute-start | bytes 3440648 | tf_op jit(solution)/shard_map/ppermute | solution.py:57
  71.9 22.8 %collective-permute-start.17 = (bf16[2,224,1280]{2,1,0:T(8,128)(2,1)}, bf16[2,224,1280]{2,1,0:T(8,128)(2,1)}, u32[]{:S(2)}, u32[]{:S(2)}) collective-permute-start(bf16[2,224,1280]{2,1,0:T(8,128)(2,1)} %collective-permute-done.11.refs_2_), channel_id=1, source_target_pairs={{0,2},{1,9},{2,4},{3,11},{4,6},{5,13},{6,0},{7,15},{8,10},{9,17},{... | collective-permute-start | bytes 3440648 | tf_op jit(solution)/shard_map/ppermute | solution.py:57
  71.9 23.9 %collective-permute-start.18 = (bf16[2,224,1280]{2,1,0:T(8,128)(2,1)}, bf16[2,224,1280]{2,1,0:T(8,128)(2,1)}, u32[]{:S(2)}, u32[]{:S(2)}) collective-permute-start(bf16[2,224,1280]{2,1,0:T(8,128)(2,1)} %collective-permute-done.16.refs_5_.refs_7_), channel_id=1, source_target_pairs={{0,6},{1,25},{2,0},{3,27},{4,2},{5,29},{6,4},{7,31},{8,14},{9,1},{... | collective-permute-start | bytes 3440648 | tf_op jit(solution)/shard_map/ppermute | solution.py:57
  144.9 5.8 %collective-permute-start.23 = (bf16[256,128]{1,0:T(8,128)(2,1)S(1)}, bf16[256,128]{1,0:T(8,128)(2,1)S(1)}, u32[]{:S(2)}, u32[]{:S(2)}) collective-permute-start(bf16[256,128]{1,0:T(8,128)(2,1)S(1)} %shard_map.138), channel_id=1, source_target_pairs={{0,16},{1,5},{2,18},{3,7},{4,20},{5,1},{6,22},{7,3},{8,24},{9,13},... | collective-permute-start | bytes 196616 | tf_op jit(solution)/shard_map/ppermute | solution.py:51
  146.6 5.5 %collective-permute-start.22 = (bf16[256,128]{1,0:T(8,128)(2,1)S(1)}, bf16[256,128]{1,0:T(8,128)(2,1)S(1)}, u32[]{:S(2)}, u32[]{:S(2)}) collective-permute-start(bf16[256,128]{1,0:T(8,128)(2,1)S(1)} %shard_map.138), channel_id=1, source_target_pairs={{0,8},{1,3},{2,10},{3,5},{4,12},{5,7},{6,14},{7,1},{8,16},{9,11},{... | collective-permute-start | bytes 196616 | tf_op jit(solution)/shard_map/ppermute | solution.py:51
  152.1 10.5 %collective-permute-start.25 = (bf16[4,256,128]{2,1,0:T(8,128)(2,1)S(1)}, bf16[4,256,128]{2,1,0:T(8,128)(2,1)S(1)}, u32[]{:S(2)}, u32[]{:S(2)}) collective-permute-start(bf16[4,256,128]{2,1,0:T(8,128)(2,1)S(1)} %pad_maximum_fusion.4.t), channel_id=1, source_target_pairs={{0,2},{1,9},{2,4},{3,11},{4,6},{5,13},{6,0},{7,15},{8,10},{9,17},{... | collective-permute-start | bytes 786440 | tf_op jit(solution)/shard_map/ppermute | solution.py:57
  152.2 10.4 %collective-permute-start.26 = (bf16[4,256,128]{2,1,0:T(8,128)(2,1)S(1)}, bf16[4,256,128]{2,1,0:T(8,128)(2,1)S(1)}, u32[]{:S(2)}, u32[]{:S(2)}) collective-permute-start(bf16[4,256,128]{2,1,0:T(8,128)(2,1)S(1)} %pad_maximum_fusion.4.t), channel_id=1, source_target_pairs={{0,4},{1,17},{2,6},{3,19},{4,0},{5,21},{6,2},{7,23},{8,12},{9,25},... | collective-permute-start | bytes 786440 | tf_op jit(solution)/shard_map/ppermute | solution.py:57
  153.8 9.6 %collective-permute-start.27 = (bf16[4,256,128]{2,1,0:T(8,128)(2,1)S(1)}, bf16[4,256,128]{2,1,0:T(8,128)(2,1)S(1)}, u32[]{:S(2)}, u32[]{:S(2)}) collective-permute-start(bf16[4,256,128]{2,1,0:T(8,128)(2,1)S(1)} %pad_maximum_fusion.4.t), channel_id=1, source_target_pairs={{0,6},{1,25},{2,0},{3,27},{4,2},{5,29},{6,4},{7,31},{8,14},{9,1},{... | collective-permute-start | bytes 786440 | tf_op jit(solution)/shard_map/ppermute | solution.py:57
  155.5 8.5 %collective-permute-start.28 = (bf16[4,256,128]{2,1,0:T(8,128)(2,1)S(1)}, bf16[4,256,128]{2,1,0:T(8,128)(2,1)S(1)}, u32[]{:S(2)}, u32[]{:S(2)}) collective-permute-start(bf16[4,256,128]{2,1,0:T(8,128)(2,1)S(1)} %pad_maximum_fusion.4.t), channel_id=1, source_target_pairs={{0,1},{1,0},{2,3},{3,2},{4,5},{5,4},{6,7},{7,6},{8,9},{9,8},{10,11... | collective-permute-start | bytes 786440 | tf_op jit(solution)/shard_map/ppermute | solution.py:47
  173.6 4.8 %collective-permute-start.20 = (bf16[256,1792]{1,0:T(8,128)(2,1)S(1)}, bf16[256,1792]{1,0:T(8,128)(2,1)S(1)}, u32[]{:S(2)}, u32[]{:S(2)}) collective-permute-start(bf16[256,1792]{1,0:T(8,128)(2,1)S(1)} %get-tuple-element.64), channel_id=1, source_target_pairs={{0,1},{1,0},{2,3},{3,2},{4,5},{5,4},{6,7},{7,6},{8,9},{9,8},{10,11... | collective-permute-start | bytes 2752520 | tf_op jit(solution)/shard_map/ppermute | solution.py:47
  175.8 6.1 %collective-permute-start.35 = (bf16[4,8,3584]{2,1,0:T(8,128)(2,1)S(1)}, bf16[4,8,3584]{2,1,0:T(8,128)(2,1)S(1)}, u32[]{:S(2)}, u32[]{:S(2)}) collective-permute-start(bf16[4,8,3584]{2,1,0:T(8,128)(2,1)S(1)} %get-tuple-element.79), channel_id=1, source_target_pairs={{0,24},{1,7},{2,26},{3,1},{4,28},{5,3},{6,30},{7,5},{8,0},{9,15},{... | collective-permute-start | bytes 688136 | tf_op jit(solution)/shard_map/ppermute | solution.py:51
  176.7 7.6 %collective-permute-start.34 = (bf16[4,8,3584]{2,1,0:T(8,128)(2,1)S(1)}, bf16[4,8,3584]{2,1,0:T(8,128)(2,1)S(1)}, u32[]{:S(2)}, u32[]{:S(2)}) collective-permute-start(bf16[4,8,3584]{2,1,0:T(8,128)(2,1)S(1)} %get-tuple-element.80), channel_id=1, source_target_pairs={{0,16},{1,5},{2,18},{3,7},{4,20},{5,1},{6,22},{7,3},{8,24},{9,13},... | collective-permute-start | bytes 688136 | tf_op jit(solution)/shard_map/ppermute | solution.py:51
  177.6 9.1 %collective-permute-start.33 = (bf16[4,8,3584]{2,1,0:T(8,128)(2,1)S(1)}, bf16[4,8,3584]{2,1,0:T(8,128)(2,1)S(1)}, u32[]{:S(2)}, u32[]{:S(2)}) collective-permute-start(bf16[4,8,3584]{2,1,0:T(8,128)(2,1)S(1)} %get-tuple-element.78), channel_id=1, source_target_pairs={{0,8},{1,3},{2,10},{3,5},{4,12},{5,7},{6,14},{7,1},{8,16},{9,11},{... | collective-permute-start | bytes 688136 | tf_op jit(solution)/shard_map/ppermute | solution.py:51
  186.9 4.7 %collective-permute-start.38 = (bf16[8,3584]{1,0:T(8,128)(2,1)S(1)}, bf16[8,3584]{1,0:T(8,128)(2,1)S(1)}, u32[]{:S(2)}, u32[]{:S(2)}) collective-permute-start(bf16[8,3584]{1,0:T(8,128)(2,1)S(1)} %get-tuple-element.90), channel_id=1, source_target_pairs={{0,6},{1,25},{2,0},{3,27},{4,2},{5,29},{6,4},{7,31},{8,14},{9,1},{... | collective-permute-start | bytes 172040 | tf_op jit(solution)/shard_map/ppermute | solution.py:57
  189.3 5.8 %collective-permute-start.37 = (bf16[8,3584]{1,0:T(8,128)(2,1)S(1)}, bf16[8,3584]{1,0:T(8,128)(2,1)S(1)}, u32[]{:S(2)}, u32[]{:S(2)}) collective-permute-start(bf16[8,3584]{1,0:T(8,128)(2,1)S(1)} %get-tuple-element.91), channel_id=1, source_target_pairs={{0,4},{1,17},{2,6},{3,19},{4,0},{5,21},{6,2},{7,23},{8,12},{9,25},... | collective-permute-start | bytes 172040 | tf_op jit(solution)/shard_map/ppermute | solution.py:57
  189.3 6.0 %collective-permute-start.36 = (bf16[8,3584]{1,0:T(8,128)(2,1)S(1)}, bf16[8,3584]{1,0:T(8,128)(2,1)S(1)}, u32[]{:S(2)}, u32[]{:S(2)}) collective-permute-start(bf16[8,3584]{1,0:T(8,128)(2,1)S(1)} %get-tuple-element.89), channel_id=1, source_target_pairs={{0,2},{1,9},{2,4},{3,11},{4,6},{5,13},{6,0},{7,15},{8,10},{9,17},{... | collective-permute-start | bytes 172040 | tf_op jit(solution)/shard_map/ppermute | solution.py:57
  (28 other events, 213.8 us)
Sparse Core Ops, SparseCore 0:
  41.6 60.5 all-gather.1

commit v6 on v4

--- a/solution.py
+++ b/solution.py
@@ -417,7 +417,7 @@
         gate = jnp.dot(mixed[...], wgu[0, :, cols], preferred_element_type=F32)
         up = jnp.dot(mixed[...], wgu[1, :, cols], preferred_element_type=F32)
         hidden[:, cols] = (gate * jax.nn.sigmoid(gate) * up).astype(BF)
-    tile = 512
+    tile = acc.shape[2]
 
     @pl.loop(0, width // tile)
     def _(n):
@@ -463,10 +463,10 @@
             pltpu.VMEM((count, 2 * SIDE * SIDE * HD), BF),
             pltpu.VMEM((count, width), BF),
             pltpu.VMEM((count, units), BF),
-            pltpu.VMEM((count // pages, pages, 512), F32),
+            pltpu.VMEM((count // pages, pages, width // 2), F32),
             pltpu.SemaphoreType.DMA((40,)),
         ],
-        compiler_params=params(12),
+        compiler_params=params(20),
         cost_estimate=pl.CostEstimate(
             flops=6 * count * width * units, bytes_accessed=6 * width * units, transcendentals=0
         ),

time: 203 us -> 202 us (level)
  no operation moved by 1% of the time
where the time goes in v6:
time: 202 us
  waiting for transfers between devices  61 us (30%)
  Pallas kernels  42.7 us (21%)
  starting transfers between devices  41.3 us (20%)
  blocking collectives  24.8 us (12%)
  between operations  14.5 us (7%)
  local copies, waits for them, and re-layouts  12.2 us (6%)
  other arithmetic  5.37 us (3%)
    ppermute x15, waiting for transfers between devices, move_b(): lax.ppermute(v, 'page', chip_perm(lambda x, z, c: (x, z + k, c) if c == 0...  28.6 us
    ppermute x12, waiting for transfers between devices, move_a(): lax.ppermute(v, 'page', chip_perm(lambda x, z, c: (x + k, z, c) if c == 0...  24.9 us
    all_to_all x1, blocking collectives, on_device(): lax.all_to_all(blocks, ('grp', 'page'), split_axis=0, concat_axis=0, tile...  24.8 us
    ppermute x15, starting transfers between devices, move_b(): lax.ppermute(v, 'page', chip_perm(lambda x, z, c: (x, z + k, c) if c == 0...  23.3 us
    ppermute x12, starting transfers between devices, move_a(): lax.ppermute(v, 'page', chip_perm(lambda x, z, c: (x + k, z, c) if c == 0...  15.4 us
    pallas_call x1, Pallas kernels, page_out(): pl.pallas_call(out_kernel, out_shape=(st, st, pool, pool), in_specs=[smem...  10.4 us
    pallas_call x1, Pallas kernels, qkv_first(): pl.pallas_call(qkv_first_kernel, out_shape=jax.ShapeDtypeStruct((2 * toke...  8.55 us
    unnamed x38, local copies, waits for them, and re-layouts  8.21 us
  transfers between devices with their start and end apart: 40, of which 27 were waited for; matrix products, arithmetic and copies ran while one was open for 3% of the time, Pallas kernels for 11%

profile of v6, /device:TPU:0, one launch (start us, length us, event | category | flops | bytes accessed | tf_op | source)
XLA Modules:
  0.0 201.8 jit_solution(2279870724663848655)
XLA Ops:
  11.2 2.9 %collective-permute-start.3 = (bf16[112,384]{1,0:T(8,128)(2,1)S(1)}, bf16[112,384]{1,0:T(8,128)(2,1)S(1)}, u32[]{:S(2)}, u32[]{:S(2)}) collective-permute-start(bf16[112,384]{1,0:T(8,128)(2,1)S(1)} %fusion.19), channel_id=1, source_target_pairs={{0,24},{1,7},{2,26},{3,1},{4,28},{5,3},{6,30},{7,5},{8,0},{9,15},{... | collective-permute-start | bytes 258056 | tf_op jit(solution)/shard_map/ppermute | solution.py:51
  16.3 3.9 %collective-permute-done.2 = bf16[112,384]{1,0:T(8,128)(2,1)S(1)} collective-permute-done((bf16[112,384]{1,0:T(8,128)(2,1)S(1)}, bf16[112,384]{1,0:T(8,128)(2,1)S(1)}, u32[]{:S(2)}, u32[]{:S(2)}) %collective-permute-start.2) | collective-permute-done | bytes 86048 | tf_op jit(solution)/shard_map/ppermute | solution.py:51
  21.4 3.2 %collective-permute-start.9 = (bf16[224,1280]{1,0:T(8,128)(2,1)S(1)}, bf16[224,1280]{1,0:T(8,128)(2,1)S(1)}, u32[]{:S(2)}, u32[]{:S(2)}) collective-permute-start(bf16[224,1280]{1,0:T(8,128)(2,1)S(1)} %fusion.7), channel_id=1, source_target_pairs={{0,24},{1,7},{2,26},{3,1},{4,28},{5,3},{6,30},{7,5},{8,0},{9,15},{... | collective-permute-start | bytes 1720328 | tf_op jit(solution)/shard_map/ppermute | solution.py:51
  24.6 1.9 collective-permute-start.5
  26.5 3.6 %collective-permute-start.6 = (bf16[4,112,384]{2,1,0:T(8,128)(2,1)S(1)}, bf16[4,112,384]{2,1,0:T(8,128)(2,1)S(1)}, u32[]{:S(2)}, u32[]{:S(2)}) collective-permute-start(bf16[4,112,384]{2,1,0:T(8,128)(2,1)S(1)} %pad_maximum_fusion.3.t), channel_id=1, source_target_pairs={{0,4},{1,17},{2,6},{3,19},{4,0},{5,21},{6,2},{7,23},{8,12},{9,25},... | collective-permute-start | bytes 1032200 | tf_op jit(solution)/shard_map/ppermute | solution.py:57
  31.2 3.9 %collective-permute-done.5.b1 = bf16[4,112,384]{2,1,0:T(8,128)(2,1)S(1)} collective-permute-done((bf16[4,112,384]{2,1,0:T(8,128)(2,1)S(1)}, bf16[4,112,384]{2,1,0:T(8,128)(2,1)S(1)}, u32[]{:S(2)}, u32[]{:S(2)}) %collective-permute-start.5) | collective-permute-done | bytes 344096 | tf_op jit(solution)/shard_map/ppermute | solution.py:57
  35.1 3.9 %collective-permute-done.6.b2 = bf16[4,112,384]{2,1,0:T(8,128)(2,1)S(1)} collective-permute-done((bf16[4,112,384]{2,1,0:T(8,128)(2,1)S(1)}, bf16[4,112,384]{2,1,0:T(8,128)(2,1)S(1)}, u32[]{:S(2)}, u32[]{:S(2)}) %collective-permute-start.6) | collective-permute-done | bytes 344096 | tf_op jit(solution)/shard_map/ppermute | solution.py:57
  39.7 1.8 shard_map.135
  41.5 1.7 collective-permute-start.10
  43.8 9.0 %collective-permute-done.10 = bf16[224,1280]{1,0:T(8,128)(2,1)S(1)} collective-permute-done((bf16[224,1280]{1,0:T(8,128)(2,1)S(1)}, bf16[224,1280]{1,0:T(8,128)(2,1)S(1)}, u32[]{:S(2)}, u32[]{:S(2)}) %collective-permute-start.10) | collective-permute-done | bytes 573472 | tf_op jit(solution)/shard_map/ppermute | solution.py:51
  55.1 2.3 %collective-permute-start.16 = (bf16[2,224,1280]{2,1,0:T(8,128)(2,1)}, bf16[2,224,1280]{2,1,0:T(8,128)(2,1)}, u32[]{:S(2)}, u32[]{:S(2)}) collective-permute-start(bf16[2,224,1280]{2,1,0:T(8,128)(2,1)} %pad_maximum_fusion.2.refs_1_), channel_id=1, source_target_pairs={{0,6},{1,25},{2,0},{3,27},{4,2},{5,29},{6,4},{7,31},{8,14},{9,1},{... | collective-permute-start | bytes 3440648 | tf_op jit(solution)/shard_map/ppermute | solution.py:57
  57.7 3.8 %shard_map.131.xo = bf16[16,256,256]{2,1,0:T(8,128)(2,1)S(1)} custom-call(bf16[256,3584]{1,0:T(8,128)(2,1)} %tok_own.1, f32[1,3584]{1,0:T(1,128)S(1)} %broadcast_in_dim.14.gain), custom_call_target="tpu_custom_call" | custom-call | bytes 3670016 | tf_op jit(solution)/shard_map/pallas_call | solution.py:111
  62.8 3.2 %collective-permute-start.15 = (bf16[2,224,1280]{2,1,0:T(8,128)(2,1)S(1)}, bf16[2,224,1280]{2,1,0:T(8,128)(2,1)}, u32[]{:S(2)}, u32[]{:S(2)}) collective-permute-start(bf16[2,224,1280]{2,1,0:T(8,128)(2,1)S(1)} %pad_maximum_fusion.1.refs_0_), channel_id=1, source_target_pairs={{0,6},{1,25},{2,0},{3,27},{4,2},{5,29},{6,4},{7,31},{8,14},{9,1},{... | collective-permute-start | bytes 3440648 | tf_op jit(solution)/shard_map/ppermute | solution.py:57
  66.8 3.8 %shard_map.132.xt = bf16[16,256,256]{2,1,0:T(8,128)(2,1)S(1)} custom-call(bf16[256,3584]{1,0:T(8,128)(2,1)} %collective-permute-done.12.tok.tok_other, f32[1,3584]{1,0:T(1,128)S(1)} %broadcast_in_dim.14.gain), custom_call_target="tpu_custom_call" | custom-call | bytes 3670016 | tf_op jit(solution)/shard_map/pallas_call | solution.py:111
  71.9 3.2 %collective-permute-start.18 = (bf16[2,224,1280]{2,1,0:T(8,128)(2,1)}, bf16[2,224,1280]{2,1,0:T(8,128)(2,1)}, u32[]{:S(2)}, u32[]{:S(2)}) collective-permute-start(bf16[2,224,1280]{2,1,0:T(8,128)(2,1)} %collective-permute-done.16.refs_5_.refs_7_), channel_id=1, source_target_pairs={{0,6},{1,25},{2,0},{3,27},{4,2},{5,29},{6,4},{7,31},{8,14},{9,1},{... | collective-permute-start | bytes 3440648 | tf_op jit(solution)/shard_map/ppermute | solution.py:57
  76.0 6.4 %collective-permute-done.14.refs_3_ = bf16[2,224,1280]{2,1,0:T(8,128)(2,1)} collective-permute-done((bf16[2,224,1280]{2,1,0:T(8,128)(2,1)}, bf16[2,224,1280]{2,1,0:T(8,128)(2,1)}, u32[]{:S(2)}, u32[]{:S(2)}) %collective-permute-start.14) | collective-permute-done | bytes 1146912 | tf_op jit(solution)/shard_map/ppermute | solution.py:57
  85.1 8.6 %shard_map.133.part = f32[512,1152]{1,0:T(8,128)S(1)} custom-call(s32[4]{0:T(128)S(1)} %pad_add_fusion.2.pos, bf16[16,256,256]{2,1,0:T(8,128)(2,1)S(1)} %shard_map.131.xo, bf16[16,256,256]{2,1,0:T(8,128)(2,1)S(1)} %copy-done.1, bf16[2,224,1280]{2,1,0:T(8,128)(2,1)S(1)} %pad_maximum_fusion.1.refs_0_, bf16[2,224,1280]{2,1,0:T(8,128)(2,1)} %pad_maximum_fusion.2.refs_1_, ...), custom_call_target="tpu_custom_call" | custom-call | flops 3623878656 | bytes 7077888 | tf_op jit(solution)/shard_map/pallas_call | solution.py:187
  95.8 5.5 %shard_map.134.att = bf16[512,896]{1,0:T(8,128)(2,1)S(1)} custom-call(s32[4]{0:T(128)S(1)} %pad_add_fusion.2.pos, bf16[16,256,256]{2,1,0:T(8,128)(2,1)S(1)} %shard_map.131.xo, bf16[16,256,256]{2,1,0:T(8,128)(2,1)S(1)} %copy-done.1, s32[512,1]{1,0:T(8,128)S(1)} %copy.36.seg_col, s32[2,1,256]{2,1,0:T(1,128)S(1)} %broadcast_in_dim.16.seg_row, ...), custom_call_target="tpu_custom_call" | custom-call | flops 2415919104 | bytes 7077888 | tf_op jit(solution)/shard_map/pallas_call | solution.py:207
  105.2 10.4 %shard_map.136 = (bf16[256,1792]{1,0:T(8,128)(2,1)S(1)}, bf16[256,1792]{1,0:T(8,128)(2,1)S(1)}, bf16[8,1792]{1,0:T(8,128)(2,1)S(1)}, bf16[8,1792]{1,0:T(8,128)(2,1)S(1)}) custom-call(s32[4]{0:T(128)S(1)} %pad_add_fusion.2.pos, bf16[256,3584]{1,0:T(8,128)(2,1)} %tok_own.1, bf16[256,3584]{1,0:T(8,128)(2,1)} %collective-permute-done.12.tok.tok_other, ...), custom_call_target="tpu_custom_call" | custom-call | flops 3288334336 | bytes 6422528 | tf_op jit(solution)/shard_map/pallas_call | solution.py:309
  117.1 24.8 %all_to_all.5 = bf16[128,8,256]{2,1,0:T(8,128)(2,1)S(1)} all-to-all(bf16[128,8,256]{2,1,0:T(8,128)(2,1)S(1)} %bitcast.63), channel_id=1, replica_groups=mesh['grp'=4,'page'=32] {'grp','page'}, dimensions={0} | all-to-all | bytes 1048576 | tf_op jit(solution)/shard_map/all_to_all | solution.py:585
  144.6 1.7 collective-permute-start.23
  146.2 3.1 %copy-done.2 = bf16[2,3584,512]{2,1,0:T(8,128)(2,1)S(1)} copy-done((bf16[2,3584,512]{2,1,0:T(8,128)(2,1)S(1)}, bf16[2,3584,512]{2,1,0:T(8,128)(2,1)}, u32[]{:S(2)}) %copy-start.2) | copy-done | bytes 7340056
  151.8 1.7 collective-permute-start.26
  153.5 1.7 collective-permute-start.27
  155.2 7.0 %collective-permute-done.25.b1 = bf16[4,256,128]{2,1,0:T(8,128)(2,1)S(1)} collective-permute-done((bf16[4,256,128]{2,1,0:T(8,128)(2,1)S(1)}, bf16[4,256,128]{2,1,0:T(8,128)(2,1)S(1)}, u32[]{:S(2)}, u32[]{:S(2)}) %collective-permute-start.25) | collective-permute-done | bytes 262176 | tf_op jit(solution)/shard_map/ppermute | solution.py:57
  164.7 6.7 %shard_map.140 = (bf16[4,4,8,3584]{3,2,1,0:T(8,128)(2,1)S(1)}, bf16[4,4,8,3584]{3,2,1,0:T(8,128)(2,1)S(1)}, f32[8,3584]{1,0:T(8,128)S(1)}) custom-call(s32[4]{0:T(128)S(1)} %pad_add_fusion.2.pos, bf16[4,256,128]{2,1,0:T(8,128)(2,1)S(1)} %pad_maximum_fusion.4.t, bf16[4,256,128]{2,1,0:T(8,128)(2,1)S(1)} %collective-permute-done.25.b1, ...), custom_call_target="tpu_custom_call" | custom-call | flops 2818572288 | bytes 11010048 | tf_op jit(solution)/shard_map/pallas_call | solution.py:457
  172.0 2.0 collective-permute-done.32
  177.4 2.8 %collective-permute-done.35 = bf16[4,8,3584]{2,1,0:T(8,128)(2,1)S(1)} collective-permute-done((bf16[4,8,3584]{2,1,0:T(8,128)(2,1)S(1)}, bf16[4,8,3584]{2,1,0:T(8,128)(2,1)S(1)}, u32[]{:S(2)}, u32[]{:S(2)}) %collective-permute-start.35) | collective-permute-done | bytes 229408 | tf_op jit(solution)/shard_map/ppermute | solution.py:51
  180.2 3.0 %collective-permute-done.34 = bf16[4,8,3584]{2,1,0:T(8,128)(2,1)S(1)} collective-permute-done((bf16[4,8,3584]{2,1,0:T(8,128)(2,1)S(1)}, bf16[4,8,3584]{2,1,0:T(8,128)(2,1)S(1)}, u32[]{:S(2)}, u32[]{:S(2)}) %collective-permute-start.34) | collective-permute-done | bytes 229408 | tf_op jit(solution)/shard_map/ppermute | solution.py:51
  183.2 2.4 %collective-permute-done.33 = bf16[4,8,3584]{2,1,0:T(8,128)(2,1)S(1)} collective-permute-done((bf16[4,8,3584]{2,1,0:T(8,128)(2,1)S(1)}, bf16[4,8,3584]{2,1,0:T(8,128)(2,1)S(1)}, u32[]{:S(2)}, u32[]{:S(2)}) %collective-permute-start.33) | collective-permute-done | bytes 229408 | tf_op jit(solution)/shard_map/ppermute | solution.py:51
  185.7 2.5 %collective-permute-start.38 = (bf16[8,3584]{1,0:T(8,128)(2,1)S(1)}, bf16[8,3584]{1,0:T(8,128)(2,1)S(1)}, u32[]{:S(2)}, u32[]{:S(2)}) collective-permute-start(bf16[8,3584]{1,0:T(8,128)(2,1)S(1)} %get-tuple-element.94), channel_id=1, source_target_pairs={{0,6},{1,25},{2,0},{3,27},{4,2},{5,29},{6,4},{7,31},{8,14},{9,1},{... | collective-permute-start | bytes 172040 | tf_op jit(solution)/shard_map/ppermute | solution.py:57
  190.6 3.5 %collective-permute-done.37 = bf16[8,3584]{1,0:T(8,128)(2,1)S(1)} collective-permute-done((bf16[8,3584]{1,0:T(8,128)(2,1)S(1)}, bf16[8,3584]{1,0:T(8,128)(2,1)S(1)}, u32[]{:S(2)}, u32[]{:S(2)}) %collective-permute-start.37) | collective-permute-done | bytes 57376 | tf_op jit(solution)/shard_map/ppermute | solution.py:57
  (143 shorter events, 41.5 us)
Async XLA Ops:
  7.2 96.8 %all-gather.2.cloned.1.call-start = ((), (), s32[]{:S(2)}) async-start(), calls=%async_computation.1 | async-start | bytes 6881280 | tf_op jit(solution)/shard_map/all_gather | solution.py:557
  10.9 10.2 %collective-permute-start.4 = (bf16[112,1152]{1,0:T(8,128)(2,1)S(1)}, bf16[112,1152]{1,0:T(8,128)(2,1)S(1)}, u32[]{:S(2)}, u32[]{:S(2)}) collective-permute-start(bf16[112,1152]{1,0:T(8,128)(2,1)S(1)} %pad_maximum_fusion.6), channel_id=1, source_target_pairs={{0,1},{1,0},{2,3},{3,2},{4,5},{5,4},{6,7},{7,6},{8,9},{9,8},{10,11... | collective-permute-start | bytes 774152 | tf_op jit(solution)/shard_map/ppermute | solution.py:47
  11.2 5.0 %collective-permute-start.3 = (bf16[112,384]{1,0:T(8,128)(2,1)S(1)}, bf16[112,384]{1,0:T(8,128)(2,1)S(1)}, u32[]{:S(2)}, u32[]{:S(2)}) collective-permute-start(bf16[112,384]{1,0:T(8,128)(2,1)S(1)} %fusion.19), channel_id=1, source_target_pairs={{0,24},{1,7},{2,26},{3,1},{4,28},{5,3},{6,30},{7,5},{8,0},{9,15},{... | collective-permute-start | bytes 258056 | tf_op jit(solution)/shard_map/ppermute | solution.py:51
  14.2 6.0 %collective-permute-start.2 = (bf16[112,384]{1,0:T(8,128)(2,1)S(1)}, bf16[112,384]{1,0:T(8,128)(2,1)S(1)}, u32[]{:S(2)}, u32[]{:S(2)}) collective-permute-start(bf16[112,384]{1,0:T(8,128)(2,1)S(1)} %fusion.19), channel_id=1, source_target_pairs={{0,16},{1,5},{2,18},{3,7},{4,20},{5,1},{6,22},{7,3},{8,24},{9,13},... | collective-permute-start | bytes 258056 | tf_op jit(solution)/shard_map/ppermute | solution.py:51
  15.0 6.1 %collective-permute-start.1 = (bf16[112,384]{1,0:T(8,128)(2,1)S(1)}, bf16[112,384]{1,0:T(8,128)(2,1)S(1)}, u32[]{:S(2)}, u32[]{:S(2)}) collective-permute-start(bf16[112,384]{1,0:T(8,128)(2,1)S(1)} %fusion.19), channel_id=1, source_target_pairs={{0,8},{1,3},{2,10},{3,5},{4,12},{5,7},{6,14},{7,1},{8,16},{9,11},{... | collective-permute-start | bytes 258056 | tf_op jit(solution)/shard_map/ppermute | solution.py:51
  21.3 18.4 %collective-permute-start.8 = (bf16[224,1280]{1,0:T(8,128)(2,1)S(1)}, bf16[224,1280]{1,0:T(8,128)(2,1)S(1)}, u32[]{:S(2)}, u32[]{:S(2)}) collective-permute-start(bf16[224,1280]{1,0:T(8,128)(2,1)S(1)} %fusion.7), channel_id=1, source_target_pairs={{0,8},{1,3},{2,10},{3,5},{4,12},{5,7},{6,14},{7,1},{8,16},{9,11},{... | collective-permute-start | bytes 1720328 | tf_op jit(solution)/shard_map/ppermute | solution.py:51
  21.4 18.3 %collective-permute-start.9 = (bf16[224,1280]{1,0:T(8,128)(2,1)S(1)}, bf16[224,1280]{1,0:T(8,128)(2,1)S(1)}, u32[]{:S(2)}, u32[]{:S(2)}) collective-permute-start(bf16[224,1280]{1,0:T(8,128)(2,1)S(1)} %fusion.7), channel_id=1, source_target_pairs={{0,24},{1,7},{2,26},{3,1},{4,28},{5,3},{6,30},{7,5},{8,0},{9,15},{... | collective-permute-start | bytes 1720328 | tf_op jit(solution)/shard_map/ppermute | solution.py:51
  24.6 10.5 %collective-permute-start.5 = (bf16[4,112,384]{2,1,0:T(8,128)(2,1)S(1)}, bf16[4,112,384]{2,1,0:T(8,128)(2,1)S(1)}, u32[]{:S(2)}, u32[]{:S(2)}) collective-permute-start(bf16[4,112,384]{2,1,0:T(8,128)(2,1)S(1)} %pad_maximum_fusion.3.t), channel_id=1, source_target_pairs={{0,2},{1,9},{2,4},{3,11},{4,6},{5,13},{6,0},{7,15},{8,10},{9,17},{... | collective-permute-start | bytes 1032200 | tf_op jit(solution)/shard_map/ppermute | solution.py:57
  26.5 12.5 %collective-permute-start.6 = (bf16[4,112,384]{2,1,0:T(8,128)(2,1)S(1)}, bf16[4,112,384]{2,1,0:T(8,128)(2,1)S(1)}, u32[]{:S(2)}, u32[]{:S(2)}) collective-permute-start(bf16[4,112,384]{2,1,0:T(8,128)(2,1)S(1)} %pad_maximum_fusion.3.t), channel_id=1, source_target_pairs={{0,4},{1,17},{2,6},{3,19},{4,0},{5,21},{6,2},{7,23},{8,12},{9,25},... | collective-permute-start | bytes 1032200 | tf_op jit(solution)/shard_map/ppermute | solution.py:57
  30.1 8.9 %collective-permute-start.7 = (bf16[4,112,384]{2,1,0:T(8,128)(2,1)S(1)}, bf16[4,112,384]{2,1,0:T(8,128)(2,1)S(1)}, u32[]{:S(2)}, u32[]{:S(2)}) collective-permute-start(bf16[4,112,384]{2,1,0:T(8,128)(2,1)S(1)} %pad_maximum_fusion.3.t), channel_id=1, source_target_pairs={{0,6},{1,25},{2,0},{3,27},{4,2},{5,29},{6,4},{7,31},{8,14},{9,1},{... | collective-permute-start | bytes 1032200 | tf_op jit(solution)/shard_map/ppermute | solution.py:57
  41.5 11.3 %collective-permute-start.10 = (bf16[224,1280]{1,0:T(8,128)(2,1)S(1)}, bf16[224,1280]{1,0:T(8,128)(2,1)S(1)}, u32[]{:S(2)}, u32[]{:S(2)}) collective-permute-start(bf16[224,1280]{1,0:T(8,128)(2,1)S(1)} %fusion.7), channel_id=1, source_target_pairs={{0,16},{1,5},{2,18},{3,7},{4,20},{5,1},{6,22},{7,3},{8,24},{9,13},... | collective-permute-start | bytes 1720328 | tf_op jit(solution)/shard_map/ppermute | solution.py:51
  43.1 23.6 %collective-permute-start.12 = (bf16[256,3584]{1,0:T(8,128)(2,1)}, bf16[256,3584]{1,0:T(8,128)(2,1)}, u32[]{:S(2)}, u32[]{:S(2)}) collective-permute-start(bf16[256,3584]{1,0:T(8,128)(2,1)} %tok_own.1), channel_id=1, source_target_pairs={{0,1},{1,0},{2,3},{3,2},{4,5},{5,4},{6,7},{7,6},{8,9},{9,8},{10,11... | collective-permute-start | bytes 5505032 | tf_op jit(solution)/shard_map/ppermute | solution.py:47
  43.8 18.8 %collective-permute-start.13 = (s32[1,8]{1,0:T(1,128)S(1)}, s32[1,8]{1,0:T(1,128)S(1)}, u32[]{:S(2)}, u32[]{:S(2)}) collective-permute-start(s32[1,8]{1,0:T(1,128)S(1)} %copy-done.17), channel_id=1, source_target_pairs={{0,1},{1,0},{2,3},{3,2},{4,5},{5,4},{6,7},{7,6},{8,9},{9,8},{10,11... | collective-permute-start | bytes 104 | tf_op jit(solution)/shard_map/ppermute | solution.py:47
  52.9 19.0 %collective-permute-start.11 = (bf16[2,224,1280]{2,1,0:T(8,128)(2,1)S(1)}, bf16[2,224,1280]{2,1,0:T(8,128)(2,1)}, u32[]{:S(2)}, u32[]{:S(2)}) collective-permute-start(bf16[2,224,1280]{2,1,0:T(8,128)(2,1)S(1)} %pad_maximum_fusion.1.refs_0_), channel_id=1, source_target_pairs={{0,2},{1,9},{2,4},{3,11},{4,6},{5,13},{6,0},{7,15},{8,10},{9,17},{... | collective-permute-start | bytes 3440648 | tf_op jit(solution)/shard_map/ppermute | solution.py:57
  55.1 16.8 %collective-permute-start.16 = (bf16[2,224,1280]{2,1,0:T(8,128)(2,1)}, bf16[2,224,1280]{2,1,0:T(8,128)(2,1)}, u32[]{:S(2)}, u32[]{:S(2)}) collective-permute-start(bf16[2,224,1280]{2,1,0:T(8,128)(2,1)} %pad_maximum_fusion.2.refs_1_), channel_id=1, source_target_pairs={{0,6},{1,25},{2,0},{3,27},{4,2},{5,29},{6,4},{7,31},{8,14},{9,1},{... | collective-permute-start | bytes 3440648 | tf_op jit(solution)/shard_map/ppermute | solution.py:57
  62.8 19.6 %collective-permute-start.14 = (bf16[2,224,1280]{2,1,0:T(8,128)(2,1)}, bf16[2,224,1280]{2,1,0:T(8,128)(2,1)}, u32[]{:S(2)}, u32[]{:S(2)}) collective-permute-start(bf16[2,224,1280]{2,1,0:T(8,128)(2,1)} %pad_maximum_fusion.2.refs_1_), channel_id=1, source_target_pairs={{0,2},{1,9},{2,4},{3,11},{4,6},{5,13},{6,0},{7,15},{8,10},{9,17},{... | collective-permute-start | bytes 3440648 | tf_op jit(solution)/shard_map/ppermute | solution.py:57
  62.8 20.7 %collective-permute-start.15 = (bf16[2,224,1280]{2,1,0:T(8,128)(2,1)S(1)}, bf16[2,224,1280]{2,1,0:T(8,128)(2,1)}, u32[]{:S(2)}, u32[]{:S(2)}) collective-permute-start(bf16[2,224,1280]{2,1,0:T(8,128)(2,1)S(1)} %pad_maximum_fusion.1.refs_0_), channel_id=1, source_target_pairs={{0,6},{1,25},{2,0},{3,27},{4,2},{5,29},{6,4},{7,31},{8,14},{9,1},{... | collective-permute-start | bytes 3440648 | tf_op jit(solution)/shard_map/ppermute | solution.py:57
  71.9 22.8 %collective-permute-start.17 = (bf16[2,224,1280]{2,1,0:T(8,128)(2,1)}, bf16[2,224,1280]{2,1,0:T(8,128)(2,1)}, u32[]{:S(2)}, u32[]{:S(2)}) collective-permute-start(bf16[2,224,1280]{2,1,0:T(8,128)(2,1)} %collective-permute-done.11.refs_2_), channel_id=1, source_target_pairs={{0,2},{1,9},{2,4},{3,11},{4,6},{5,13},{6,0},{7,15},{8,10},{9,17},{... | collective-permute-start | bytes 3440648 | tf_op jit(solution)/shard_map/ppermute | solution.py:57
  71.9 23.9 %collective-permute-start.18 = (bf16[2,224,1280]{2,1,0:T(8,128)(2,1)}, bf16[2,224,1280]{2,1,0:T(8,128)(2,1)}, u32[]{:S(2)}, u32[]{:S(2)}) collective-permute-start(bf16[2,224,1280]{2,1,0:T(8,128)(2,1)} %collective-permute-done.16.refs_5_.refs_7_), channel_id=1, source_target_pairs={{0,6},{1,25},{2,0},{3,27},{4,2},{5,29},{6,4},{7,31},{8,14},{9,1},{... | collective-permute-start | bytes 3440648 | tf_op jit(solution)/shard_map/ppermute | solution.py:57
  143.5 6.4 %collective-permute-start.24 = (bf16[256,128]{1,0:T(8,128)(2,1)S(1)}, bf16[256,128]{1,0:T(8,128)(2,1)S(1)}, u32[]{:S(2)}, u32[]{:S(2)}) collective-permute-start(bf16[256,128]{1,0:T(8,128)(2,1)S(1)} %shard_map.138), channel_id=1, source_target_pairs={{0,24},{1,7},{2,26},{3,1},{4,28},{5,3},{6,30},{7,5},{8,0},{9,15},{... | collective-permute-start | bytes 196616 | tf_op jit(solution)/shard_map/ppermute | solution.py:51
  144.6 5.8 %collective-permute-start.23 = (bf16[256,128]{1,0:T(8,128)(2,1)S(1)}, bf16[256,128]{1,0:T(8,128)(2,1)S(1)}, u32[]{:S(2)}, u32[]{:S(2)}) collective-permute-start(bf16[256,128]{1,0:T(8,128)(2,1)S(1)} %shard_map.138), channel_id=1, source_target_pairs={{0,16},{1,5},{2,18},{3,7},{4,20},{5,1},{6,22},{7,3},{8,24},{9,13},... | collective-permute-start | bytes 196616 | tf_op jit(solution)/shard_map/ppermute | solution.py:51
  146.2 5.5 %collective-permute-start.22 = (bf16[256,128]{1,0:T(8,128)(2,1)S(1)}, bf16[256,128]{1,0:T(8,128)(2,1)S(1)}, u32[]{:S(2)}, u32[]{:S(2)}) collective-permute-start(bf16[256,128]{1,0:T(8,128)(2,1)S(1)} %shard_map.138), channel_id=1, source_target_pairs={{0,8},{1,3},{2,10},{3,5},{4,12},{5,7},{6,14},{7,1},{8,16},{9,11},{... | collective-permute-start | bytes 196616 | tf_op jit(solution)/shard_map/ppermute | solution.py:51
  151.8 10.5 %collective-permute-start.25 = (bf16[4,256,128]{2,1,0:T(8,128)(2,1)S(1)}, bf16[4,256,128]{2,1,0:T(8,128)(2,1)S(1)}, u32[]{:S(2)}, u32[]{:S(2)}) collective-permute-start(bf16[4,256,128]{2,1,0:T(8,128)(2,1)S(1)} %pad_maximum_fusion.4.t), channel_id=1, source_target_pairs={{0,2},{1,9},{2,4},{3,11},{4,6},{5,13},{6,0},{7,15},{8,10},{9,17},{... | collective-permute-start | bytes 786440 | tf_op jit(solution)/shard_map/ppermute | solution.py:57
  151.8 10.4 %collective-permute-start.26 = (bf16[4,256,128]{2,1,0:T(8,128)(2,1)S(1)}, bf16[4,256,128]{2,1,0:T(8,128)(2,1)S(1)}, u32[]{:S(2)}, u32[]{:S(2)}) collective-permute-start(bf16[4,256,128]{2,1,0:T(8,128)(2,1)S(1)} %pad_maximum_fusion.4.t), channel_id=1, source_target_pairs={{0,4},{1,17},{2,6},{3,19},{4,0},{5,21},{6,2},{7,23},{8,12},{9,25},... | collective-permute-start | bytes 786440 | tf_op jit(solution)/shard_map/ppermute | solution.py:57
  153.5 9.6 %collective-permute-start.27 = (bf16[4,256,128]{2,1,0:T(8,128)(2,1)S(1)}, bf16[4,256,128]{2,1,0:T(8,128)(2,1)S(1)}, u32[]{:S(2)}, u32[]{:S(2)}) collective-permute-start(bf16[4,256,128]{2,1,0:T(8,128)(2,1)S(1)} %pad_maximum_fusion.4.t), channel_id=1, source_target_pairs={{0,6},{1,25},{2,0},{3,27},{4,2},{5,29},{6,4},{7,31},{8,14},{9,1},{... | collective-permute-start | bytes 786440 | tf_op jit(solution)/shard_map/ppermute | solution.py:57
  155.2 7.9 %collective-permute-start.28 = (bf16[4,256,128]{2,1,0:T(8,128)(2,1)S(1)}, bf16[4,256,128]{2,1,0:T(8,128)(2,1)S(1)}, u32[]{:S(2)}, u32[]{:S(2)}) collective-permute-start(bf16[4,256,128]{2,1,0:T(8,128)(2,1)S(1)} %pad_maximum_fusion.4.t), channel_id=1, source_target_pairs={{0,1},{1,0},{2,3},{3,2},{4,5},{5,4},{6,7},{7,6},{8,9},{9,8},{10,11... | collective-permute-start | bytes 786440 | tf_op jit(solution)/shard_map/ppermute | solution.py:47
  171.6 5.6 %collective-permute-start.20 = (bf16[256,1792]{1,0:T(8,128)(2,1)S(1)}, bf16[256,1792]{1,0:T(8,128)(2,1)S(1)}, u32[]{:S(2)}, u32[]{:S(2)}) collective-permute-start(bf16[256,1792]{1,0:T(8,128)(2,1)S(1)} %get-tuple-element.66), channel_id=1, source_target_pairs={{0,1},{1,0},{2,3},{3,2},{4,5},{5,4},{6,7},{7,6},{8,9},{9,8},{10,11... | collective-permute-start | bytes 2752520 | tf_op jit(solution)/shard_map/ppermute | solution.py:47
  174.1 6.1 %collective-permute-start.35 = (bf16[4,8,3584]{2,1,0:T(8,128)(2,1)S(1)}, bf16[4,8,3584]{2,1,0:T(8,128)(2,1)S(1)}, u32[]{:S(2)}, u32[]{:S(2)}) collective-permute-start(bf16[4,8,3584]{2,1,0:T(8,128)(2,1)S(1)} %get-tuple-element.83), channel_id=1, source_target_pairs={{0,24},{1,7},{2,26},{3,1},{4,28},{5,3},{6,30},{7,5},{8,0},{9,15},{... | collective-permute-start | bytes 688136 | tf_op jit(solution)/shard_map/ppermute | solution.py:51
  175.6 7.6 %collective-permute-start.34 = (bf16[4,8,3584]{2,1,0:T(8,128)(2,1)S(1)}, bf16[4,8,3584]{2,1,0:T(8,128)(2,1)S(1)}, u32[]{:S(2)}, u32[]{:S(2)}) collective-permute-start(bf16[4,8,3584]{2,1,0:T(8,128)(2,1)S(1)} %get-tuple-element.84), channel_id=1, source_target_pairs={{0,16},{1,5},{2,18},{3,7},{4,20},{5,1},{6,22},{7,3},{8,24},{9,13},... | collective-permute-start | bytes 688136 | tf_op jit(solution)/shard_map/ppermute | solution.py:51
  176.2 9.3 %collective-permute-start.33 = (bf16[4,8,3584]{2,1,0:T(8,128)(2,1)S(1)}, bf16[4,8,3584]{2,1,0:T(8,128)(2,1)S(1)}, u32[]{:S(2)}, u32[]{:S(2)}) collective-permute-start(bf16[4,8,3584]{2,1,0:T(8,128)(2,1)S(1)} %get-tuple-element.82), channel_id=1, source_target_pairs={{0,8},{1,3},{2,10},{3,5},{4,12},{5,7},{6,14},{7,1},{8,16},{9,11},{... | collective-permute-start | bytes 688136 | tf_op jit(solution)/shard_map/ppermute | solution.py:51
  188.3 5.8 %collective-permute-start.37 = (bf16[8,3584]{1,0:T(8,128)(2,1)S(1)}, bf16[8,3584]{1,0:T(8,128)(2,1)S(1)}, u32[]{:S(2)}, u32[]{:S(2)}) collective-permute-start(bf16[8,3584]{1,0:T(8,128)(2,1)S(1)} %get-tuple-element.95), channel_id=1, source_target_pairs={{0,4},{1,17},{2,6},{3,19},{4,0},{5,21},{6,2},{7,23},{8,12},{9,25},... | collective-permute-start | bytes 172040 | tf_op jit(solution)/shard_map/ppermute | solution.py:57
  188.3 6.0 %collective-permute-start.36 = (bf16[8,3584]{1,0:T(8,128)(2,1)S(1)}, bf16[8,3584]{1,0:T(8,128)(2,1)S(1)}, u32[]{:S(2)}, u32[]{:S(2)}) collective-permute-start(bf16[8,3584]{1,0:T(8,128)(2,1)S(1)} %get-tuple-element.93), channel_id=1, source_target_pairs={{0,2},{1,9},{2,4},{3,11},{4,6},{5,13},{6,0},{7,15},{8,10},{9,17},{... | collective-permute-start | bytes 172040 | tf_op jit(solution)/shard_map/ppermute | solution.py:57
  (27 other events, 112.8 us)
Sparse Core Ops, SparseCore 0:
  41.6 60.5 all-gather.1
